TPU v7x, 32 devices: a whole 2x2x4 slice. The times are simulated.
32 devices in a mesh: req: 16 (over z, y, x), tp: 2 (over core).
Axes of the slice: x: 2, y: 2, z: 4, core: 2. Of those that a mesh axis runs over, the one named last changes fastest.
Arguments:
- tokens: bfloat16 [8192, 2048], P('req', 'tp'), may hold values from -6 to 6
- attn_gain: float32 [2048], replicated, may hold values from 0.1 to 1.9
- w_query: bfloat16 [2048, 1024], P(None, 'tp'), may hold values from -0.25 to 0.25
- key_weight: bfloat16 [2048, 256], P(None, 'tp'), may hold values from -0.125 to 0.125
- value_weight: bfloat16 [2048, 256], P(None, 'tp'), may hold values from -0.125 to 0.125
- w_attn_out: bfloat16 [1024, 2048], P('tp'), may hold values from -1 to 1
- kv_pages: bfloat16 [512, 2, 2, 128, 128], P('req', None, 'tp'), may hold values from -240 to 240
- page_table: int32 [16, 32], P('req'), may hold values from 0 to 511, as said below
- cached_len: int32 [16], P('req'), may hold values from 3072 to 4096, as said below
- w_gate_z: bfloat16 [2048, 1536], P(None, 'tp'), may hold values from -0.125 to 0.125
- w_ssm_in: bfloat16 [2048, 1536], P(None, 'tp'), may hold values from -0.125 to 0.125
- w_bc: bfloat16 [2048, 512], replicated, may hold values from -0.125 to 0.125
- w_dt: bfloat16 [2048, 24], P(None, 'tp'), may hold values from -0.125 to 0.125
- conv_w_x: float32 [4, 1536], P(None, 'tp'), may hold values from -3 to 3
- conv_w_bc: float32 [4, 512], replicated, may hold values from -3 to 3
- conv_x_state: bfloat16 [16, 3, 1536], P('req', None, 'tp'), may hold values from -6 to 6
- conv_bc_state: bfloat16 [16, 3, 512], P('req'), may hold values from -6 to 6
- dt_bias: float32 [24], P('tp'), may hold values from -3 to 0
- decay_rate: float32 [24], P('tp'), may hold values from 0.002 to 0.2
- skip_gain: float32 [24], P('tp'), may hold values from 0.5 to 1.5
- mixer_gain: float32 [1536], P('tp'), may hold values from 0.1 to 1.9
- w_mixer_out: bfloat16 [1536, 2048], P('tp'), may hold values from -0.15625 to 0.15625
- ssm_state: float32 [16, 24, 64, 256], P('req', 'tp'), may hold values from -6 to 6
Outputs:
- mixed: bfloat16 [8192, 2048], P('req', 'tp')
- final_state: float32 [16, 24, 64, 256], P('req', 'tp')
Inputs may be any that keep to these rules, and one draw needn't show every extreme that they name: `page_table`: entries are page numbers below 512. Of one request's 32 entries at most 2 lie among the pages of one index of req, and some request has exactly 2 there. Requests in aligned runs of 4 may share their leading entries. `cached_len`: some request has exactly 4096.
All inputs are finite; a program needn't handle non-finite values.
Results may differ from a plain program's by a relative error of at most 0.018.
The roundings to bfloat16 on the way count: a program that leaves them out, or rounds other values in their place, can miss the bound.
Values may be sent and summed in bfloat16 or wider, within the bound.
No kernel may reach another device: no remote copies, remote signals or barrier semaphores. Data moves between devices by JAX's collectives and lax.ppermute only.
A program may use at most 128 MiB of HBM per device.

v0:
```python
from functools import partial

import jax
import jax.numpy as jnp
from jax import lax
from jax.sharding import PartitionSpec as P

HEAD_SIZE = 128
MP = 64
MN = 256
DSSM = 1536


EPSILON = 1e-05
ROPE_BASE = 100000.0
NEG_FILL = -1e30


def rms_scale(value_vectors, gain_row):
    mean_sq = jnp.mean(value_vectors * value_vectors, axis=-1, keepdims=True)
    return value_vectors * lax.rsqrt(mean_sq + EPSILON) * gain_row


def stored(value_vectors):
    return lax.optimization_barrier(value_vectors.astype(jnp.bfloat16))


def apply_rotary(value_vectors, token_positions):
    full_width = value_vectors.shape[-1]
    half_width = full_width // 2
    inverse = ROPE_BASE ** (-2.0 * jnp.arange(half_width, dtype=jnp.float32) / full_width)
    angles = token_positions.astype(jnp.float32)[:, None] * inverse[None, :]
    cosine = jnp.concatenate([jnp.cos(angles), jnp.cos(angles)], axis=-1)[:, None, :]
    sine_row = jnp.concatenate([jnp.sin(angles), jnp.sin(angles)], axis=-1)[:, None, :]
    turned = jnp.concatenate(
        [-value_vectors[..., half_width:], value_vectors[..., :half_width]], axis=-1
    )
    return value_vectors * cosine + turned * sine_row


def short_conv(history, fresh_rows, kernel):
    joined = jnp.concatenate([history, fresh_rows], axis=0).astype(jnp.float32)
    row_count = fresh_rows.shape[0]
    summed = joined[0:row_count] * kernel[0]
    for tap_index in range(1, kernel.shape[0]):
        summed = summed + joined[tap_index : tap_index + row_count] * kernel[tap_index]
    return jax.nn.silu(summed)


def pick_pages(table_row, target, pages_dev, capacity):
    page_count = table_row.shape[0]
    owners = table_row // pages_dev
    local_slot = table_row % pages_dev
    page_index = jnp.arange(page_count, dtype=jnp.int32)
    earlier = (page_index[None, :] < page_index[:, None]) & (owners[None, :] == owners[:, None])
    ranks = jnp.sum(earlier.astype(jnp.int32), axis=1)
    places = jnp.arange(capacity, dtype=jnp.int32)
    chosen = ((owners == target)[:, None] & (ranks[:, None] == places[None, :])).astype(jnp.int32)
    return (
        jnp.sum(chosen * local_slot[:, None], axis=0),
        jnp.sum(chosen * page_index[:, None], axis=0),
        jnp.sum(chosen, axis=0),
    )


def attend(query_rows, key_rows, value_rows, visible, score_scale):
    scores = (
        jnp.einsum("rd,kd->rk", query_rows, key_rows, preferred_element_type=jnp.float32)
        * score_scale
    )
    scores = jnp.where(visible, scores, NEG_FILL)
    row_top = jnp.max(scores, axis=-1, keepdims=True)
    weights = jnp.where(visible, jnp.exp(scores - row_top), 0.0)
    weight_sum = jnp.sum(weights, axis=-1, keepdims=True)
    summed = jnp.dot(weights.astype(jnp.bfloat16), value_rows, preferred_element_type=jnp.float32)
    return (summed, row_top, weight_sum)


def shards(
    tokens,
    attn_gain,
    w_query,
    key_weight,
    value_weight,
    w_attn_out,
    kv_pages,
    page_table,
    cached_len,
    w_gate_z,
    w_ssm_in,
    w_bc,
    w_dt,
    conv_w_x,
    conv_w_bc,
    conv_x_state,
    conv_bc_state,
    dt_bias,
    decay_rate,
    skip_gain,
    mixer_gain,
    w_mixer_out,
    ssm_state,
):
    gathered = lax.all_gather(tokens, "tp", axis=1, tiled=True)
    row_count = gathered.shape[0]
    normed_input = rms_scale(gathered.astype(jnp.float32), attn_gain).astype(jnp.bfloat16)
    length = cached_len[0]
    row_order = jnp.arange(row_count, dtype=jnp.int32)
    token_positions = length + row_order
    query_vectors = apply_rotary(
        jnp.dot(normed_input, w_query, preferred_element_type=jnp.float32).reshape(
            row_count, -1, HEAD_SIZE
        ),
        token_positions,
    ).astype(jnp.bfloat16)
    incoming_keys = apply_rotary(
        jnp.dot(normed_input, key_weight, preferred_element_type=jnp.float32).reshape(
            row_count, -1, HEAD_SIZE
        ),
        token_positions,
    ).astype(jnp.bfloat16)
    incoming_values = (
        jnp.dot(normed_input, value_weight, preferred_element_type=jnp.float32)
        .astype(jnp.bfloat16)
        .reshape(row_count, -1, HEAD_SIZE)
    )
    kv_local = incoming_keys.shape[1]
    devices = lax.axis_size("req")
    pages_dev = kv_pages.shape[0]
    capacity = pages_dev // devices
    page_size = kv_pages.shape[3]
    targets = jnp.arange(devices, dtype=jnp.int32)
    want_slot, page_of, present = jax.vmap(
        partial(pick_pages, page_table[0], pages_dev=pages_dev, capacity=capacity)
    )(targets)
    requested = lax.all_to_all(want_slot, "req", split_axis=0, concat_axis=0, tiled=True)
    fetched = kv_pages[requested.reshape(-1)].reshape((devices, capacity) + kv_pages.shape[1:])
    arrived = lax.all_to_all(fetched, "req", split_axis=0, concat_axis=0, tiled=True)
    cached_key_rows = jnp.transpose(arrived[:, :, 0], (2, 0, 1, 3, 4)).reshape(
        kv_local, -1, HEAD_SIZE
    )
    cached_value_rows = jnp.transpose(arrived[:, :, 1], (2, 0, 1, 3, 4)).reshape(
        kv_local, -1, HEAD_SIZE
    )
    cache_pos = (
        page_of[:, :, None] * page_size + jnp.arange(page_size, dtype=jnp.int32)[None, None, :]
    ).reshape(-1)
    live = jnp.broadcast_to(present[:, :, None] > 0, (devices, capacity, page_size)).reshape(-1) & (
        cache_pos < length
    )
    causal = row_order[None, :] <= row_order[:, None]
    cache_visible = jnp.broadcast_to(live[None, :], (row_count, live.shape[0]))
    score_scale = HEAD_SIZE ** (-0.5)
    head_queries = jnp.transpose(query_vectors, (1, 0, 2))
    key_cache = cached_key_rows[0]
    value_cache = cached_value_rows[0]
    key_fresh = incoming_keys[:, 0]
    value_fresh = incoming_values[:, 0]
    key_all = jnp.concatenate([key_cache, key_fresh], axis=0)
    value_all = jnp.concatenate([value_cache, value_fresh], axis=0)
    visible_all = jnp.concatenate([cache_visible, causal], axis=1)

    def one_head(query_rows):
        head_sum, row_top, head_total = attend(
            query_rows, key_all, value_all, visible_all, score_scale
        )
        return head_sum / head_total

    contexts = [lax.map(one_head, head_queries)]
    context = (
        jnp.transpose(jnp.stack(contexts), (2, 0, 1, 3)).reshape(row_count, -1).astype(jnp.bfloat16)
    )
    attn_part = jnp.dot(context, w_attn_out, preferred_element_type=jnp.float32)
    gate_z = stored(jnp.dot(normed_input, w_gate_z, preferred_element_type=jnp.float32))
    ssm_in = stored(jnp.dot(normed_input, w_ssm_in, preferred_element_type=jnp.float32))
    bc_in = stored(jnp.dot(normed_input, w_bc, preferred_element_type=jnp.float32))
    step_raw = jnp.dot(normed_input, w_dt, preferred_element_type=jnp.float32)
    head_count = w_dt.shape[1]
    ssm_x = stored(short_conv(conv_x_state[0], ssm_in, conv_w_x)).reshape(row_count, head_count, MP)
    bc_rows = stored(short_conv(conv_bc_state[0], bc_in, conv_w_bc))
    b_vectors = bc_rows[:, :MN]
    c_vectors = bc_rows[:, MN:]
    step_size = jax.nn.softplus(step_raw + dt_bias)
    cumulative = jnp.cumsum(-step_size * decay_rate, axis=0)
    gap = cumulative.T[:, :, None] - cumulative.T[:, None, :]
    inner = jnp.dot(c_vectors, b_vectors.T, preferred_element_type=jnp.float32)
    mixing = stored(jnp.where(causal[None], jnp.exp(jnp.minimum(gap, 0.0)), 0.0) * inner[None])
    x_float = ssm_x.astype(jnp.float32)
    moved_float = x_float * step_size[:, :, None]
    moved = stored(moved_float)
    intra = jnp.einsum("hij,jhp->ihp", mixing, moved, preferred_element_type=jnp.float32)
    state_in = ssm_state[0]
    carried = jnp.exp(cumulative)[:, :, None] * jnp.einsum(
        "in,hpn->ihp", c_vectors.astype(jnp.float32), state_in, precision=lax.Precision.HIGHEST
    )
    ssm_y = intra + carried + skip_gain[None, :, None] * x_float
    tail_fade = jnp.exp(cumulative[-1][None, :] - cumulative)
    tail_moved = stored(moved_float * tail_fade[:, :, None])
    last_state = jnp.exp(cumulative[-1])[:, None, None] * state_in + jnp.einsum(
        "jhp,jn->hpn", tail_moved, b_vectors, preferred_element_type=jnp.float32
    )
    gated = ssm_y.reshape(row_count, -1) * jax.nn.silu(gate_z.astype(jnp.float32))
    local_sq = jnp.sum(gated * gated, axis=-1)
    total_sq = lax.psum(local_sq, "tp")
    normed_y = (gated * lax.rsqrt(total_sq / DSSM + EPSILON)[:, None] * mixer_gain).astype(
        jnp.bfloat16
    )
    ssm_part = jnp.dot(normed_y, w_mixer_out, preferred_element_type=jnp.float32)
    summed = lax.psum_scatter(
        (attn_part + ssm_part).astype(jnp.bfloat16), "tp", scatter_dimension=1, tiled=True
    )
    return (summed, last_state[None])


def solution(mesh):
    return jax.shard_map(
        shards,
        mesh=mesh,
        in_specs=(
            P("req", "tp"),
            P(),
            P(None, "tp"),
            P(None, "tp"),
            P(None, "tp"),
            P("tp", None),
            P("req", None, "tp", None, None),
            P("req", None),
            P("req"),
            P(None, "tp"),
            P(None, "tp"),
            P(),
            P(None, "tp"),
            P(None, "tp"),
            P(),
            P("req", None, "tp"),
            P("req", None, None),
            P("tp"),
            P("tp"),
            P("tp"),
            P("tp"),
            P("tp", None),
            P("req", "tp", None, None),
        ),
        out_specs=(P("req", "tp"), P("req", "tp", None, None)),
        check_vma=False,
    )
```

profile of v0, /device:TPU:13, one launch (start us, length us, event | category | flops | bytes accessed | tf_op | source)
XLA Modules:
  0.0 189.3 jit_solution(1598359645610734830)
XLA Ops:
  10.5 6.6 %all-to-all-start = ((s32[16,1,2]{2,1,0:T(1,128)}), s32[16,1,2]{2,1,0:T(1,128)S(1)}, u32[]{:S(2)}, u32[]{:S(2)}) async-start(s32[16,1,2]{2,1,0:T(1,128)} %copy.97), calls=%async_computation | async-start | bytes 16384 | tf_op jit(solution)/shard_map/all_to_all | solution.py:136
  24.3 3.7 %gather_fusion = bf16[32,2,128,128]{3,2,1,0:T(8,128)(2,1)} fusion(bf16[32,2,128,128]{3,2,1,0:T(8,128)(2,1)} %bitcast.133, s32[1024]{0:T(1024)S(1)} %pad_clamp_fusion), kind=kCustom, calls=%fused_computation | custom fusion | bytes 4194432 | tf_op jit(solution)/shard_map/gather | solution.py:137
  28.0 3.2 %copy.98 = bf16[16,2,2,1,128,128]{5,4,1,3,2,0:T(8,128)(2,1)} copy(bf16[16,2,2,1,128,128]{5,4,2,1,0,3:T(8,128)(2,1)} %bitcast.128) | data formatting | bytes 4194304 | tf_op jit(solution)/shard_map/reshape | solution.py:137
  31.2 6.5 %all-to-all-start.1 = ((bf16[16,2,2,1,128,128]{5,4,1,3,2,0:T(8,128)(2,1)}), bf16[16,2,2,1,128,128]{5,4,1,3,2,0:T(8,128)(2,1)}, u32[]{:S(2)}, u32[]{:S(2)}) async-start(bf16[16,2,2,1,128,128]{5,4,1,3,2,0:T(8,128)(2,1)} %copy.98), calls=%async_computation.1 | async-start | bytes 4194304 | tf_op jit(solution)/shard_map/all_to_all | solution.py:138
  46.0 4.3 %convolution_convert_fusion.1 = bf16[512,768]{1,0:T(8,128)(2,1)S(1)} fusion(bf16[512,2048]{1,0:T(8,128)(2,1)} %fusion.20, bf16[2048,768]{1,0:T(8,128)(2,1)} %param.35), kind=kOutput, calls=%fused_computation.46 | convolution fusion | flops 1611005952 | bytes 6029312 | tf_op jit(solution)/shard_map/dot_general | solution.py:175
  61.7 3.3 %multiply_convert_fusion = bf16[12,512,512]{2,1,0:T(8,128)(2,1)S(1)} fusion(f32[512,512]{1,0:T(8,128)S(1)} %fusion.45, f32[12,512]{1,0:T(8,128)S(1)} %bitcast.138, pred[512,512]{1,0:T(8,128)(4,1)S(1)} %iota_compare_fusion), kind=kLoop, calls=%fused_computation.17 | loop fusion | flops 15728640 | bytes 7626752 | tf_op jit(solution)/shard_map/convert_element_type | solution.py:25
  72.4 5.2 %convolution_convert_fusion = bf16[512,768]{1,0:T(8,128)(2,1)} fusion(bf16[512,2048]{1,0:T(8,128)(2,1)} %fusion.20, bf16[2048,768]{1,0:T(8,128)(2,1)} %param.34), kind=kOutput, calls=%fused_computation.45 | convolution fusion | flops 1611005952 | bytes 6029312 | tf_op jit(solution)/shard_map/dot_general | solution.py:174
  83.9 4.5 %fusion.65 = f32[512,512]{0,1:T(8,128)} fusion(bf16[512,2048]{1,0:T(8,128)(2,1)} %fusion.20, bf16[2048,512]{1,0:T(8,128)(2,1)} %param.27), kind=kOutput, calls=%fused_computation.145 | convolution fusion | flops 1073741824 | bytes 5242880 | tf_op jit(solution)/shard_map/dot_general | solution.py:111
  93.9 3.9 %psum.7 = f32[512]{0:T(512)S(1)} all-reduce(f32[512]{0:T(512)S(1)} %multiply_reduce_fusion), channel_id=1, replica_groups=mesh['req'=16,'tp'=2] {'tp'}, use_global_device_ids=true, to_apply=%region_12.13 | all-reduce | flops 512 | bytes 4096 | tf_op jit(solution)/shard_map/psum | solution.py:204
  104.2 4.1 %fusion.35 = f32[512,2048]{1,0:T(8,128)} fusion(bf16[768,2048]{1,0:T(8,128)(2,1)S(1)} %copy-done, f32[768]{0:T(1024)S(1)} %copy-done.31, f32[512]{0:T(512)S(1)} %add_rsqrt_fusion, f32[512,768]{1,0:T(8,128)S(1)} %copy-done.6, bf16[512,768]{1,0:T(8,128)(2,1)S(1)} %copy-done.11), kind=kOutput, calls=%fused_computation.68 | convolution fusion | flops 1614151680 | bytes 9704448 | tf_op jit(solution)/shard_map/dot_general | solution.py:208
  112.1 53.7 %while.10 = (s32[]{:T(128)}, bf16[4,512,128]{1,2,0:T(8,128)(2,1)}, bf16[4,512,128]{2,1,0:T(8,128)(2,1)}, bf16[4608,128]{1,0:T(8,128)(2,1)S(1)}, pred[512,4608]{1...) while((s32[]{:T(128)}, bf16[4,512,128]{1,2,0:T(8,128)(2,1)}, bf16[4,512,128]{2,1,0:T(8,128)(2,1)}, ...), condition=%wide.region_8.9_spmd, body=%wide.region_5.8_spmd.sunk | while | flops 1238760448 | bytes 43265128 | solution.py:169
  112.1 3.1 %fusion.99 = (f32[512]{0:T(512)S(1)}, f32[512,4608]{1,0:T(8,128)S(1)}) fusion(pred[512,4608]{1,0:T(32,128)(4,1)S(1)} %get-tuple-element.139, bf16[4608,128]{1,0:T(8,128)(2,1)S(1)} %get-tuple-element.138, bf16[4,512,128]{2,1,0:T(8,128)(2,1)} %get-tuple-element.137, s32[]{:T(128)} %get-tuple-element.128), kind=kOutput, calls=%fused_computation.3.clone.1 | convolution fusion | flops 611057152 | bytes 13109760 | tf_op jit(solution)/shard_map/while/body/eval_jaxpr/rd,kd->rk/dot_general | solution.py:68
  115.3 3.1 %fusion.100 = f32[512]{0:T(512)S(1)} fusion(pred[512,4608]{1,0:T(32,128)(4,1)S(1)} %get-tuple-element.139, f32[512,4608]{1,0:T(8,128)S(1)} %get-tuple-element.119, f32[512]{0:T(512)S(1)} %get-tuple-element.120), kind=kLoop, calls=%fused_computation.4.clone.1 | loop fusion | flops 11795968 | bytes 11800576 | tf_op jit(solution)/shard_map/while/body/eval_jaxpr/reduce_sum | solution.py:74
  118.4 3.9 %fusion.101 = bf16[1,512,128]{2,1,0:T(8,128)(2,1)} fusion(bf16[4608,128]{1,0:T(8,128)(2,1)S(1)} %copy-done.9, pred[512,4608]{1,0:T(32,128)(4,1)S(1)} %get-tuple-element.139, f32[512,4608]{1,0:T(8,128)S(1)} %get-tuple-element.119, f32[512]{0:T(512)S(1)} %get-tuple-element.120, f32[512]{0:T(512)S(1)} %fusion.100), kind=kOutput, calls=%fused_computation.8.clone.1 | convolution fusion | flops 615907328 | bytes 13111296 | tf_op jit(solution)/shard_map/while/body/eval_jaxpr/dot_general | solution.py:75
  125.6 3.1 %fusion.99 = (f32[512]{0:T(512)S(1)}, f32[512,4608]{1,0:T(8,128)S(1)}) fusion(pred[512,4608]{1,0:T(32,128)(4,1)S(1)} %get-tuple-element.139, bf16[4608,128]{1,0:T(8,128)(2,1)S(1)} %get-tuple-element.138, bf16[4,512,128]{2,1,0:T(8,128)(2,1)} %get-tuple-element.137, s32[]{:T(128)} %get-tuple-element.128), kind=kOutput, calls=%fused_computation.3.clone.1 | convolution fusion | flops 611057152 | bytes 13109760 | tf_op jit(solution)/shard_map/while/body/eval_jaxpr/rd,kd->rk/dot_general | solution.py:68
  128.7 3.1 %fusion.100 = f32[512]{0:T(512)S(1)} fusion(pred[512,4608]{1,0:T(32,128)(4,1)S(1)} %get-tuple-element.139, f32[512,4608]{1,0:T(8,128)S(1)} %get-tuple-element.119, f32[512]{0:T(512)S(1)} %get-tuple-element.120), kind=kLoop, calls=%fused_computation.4.clone.1 | loop fusion | flops 11795968 | bytes 11800576 | tf_op jit(solution)/shard_map/while/body/eval_jaxpr/reduce_sum | solution.py:74
  131.8 3.9 %fusion.101 = bf16[1,512,128]{2,1,0:T(8,128)(2,1)} fusion(bf16[4608,128]{1,0:T(8,128)(2,1)S(1)} %copy-done.9, pred[512,4608]{1,0:T(32,128)(4,1)S(1)} %get-tuple-element.139, f32[512,4608]{1,0:T(8,128)S(1)} %get-tuple-element.119, f32[512]{0:T(512)S(1)} %get-tuple-element.120, f32[512]{0:T(512)S(1)} %fusion.100), kind=kOutput, calls=%fused_computation.8.clone.1 | convolution fusion | flops 615907328 | bytes 13111296 | tf_op jit(solution)/shard_map/while/body/eval_jaxpr/dot_general | solution.py:75
  139.0 3.1 %fusion.99 = (f32[512]{0:T(512)S(1)}, f32[512,4608]{1,0:T(8,128)S(1)}) fusion(pred[512,4608]{1,0:T(32,128)(4,1)S(1)} %get-tuple-element.139, bf16[4608,128]{1,0:T(8,128)(2,1)S(1)} %get-tuple-element.138, bf16[4,512,128]{2,1,0:T(8,128)(2,1)} %get-tuple-element.137, s32[]{:T(128)} %get-tuple-element.128), kind=kOutput, calls=%fused_computation.3.clone.1 | convolution fusion | flops 611057152 | bytes 13109760 | tf_op jit(solution)/shard_map/while/body/eval_jaxpr/rd,kd->rk/dot_general | solution.py:68
  142.1 3.1 %fusion.100 = f32[512]{0:T(512)S(1)} fusion(pred[512,4608]{1,0:T(32,128)(4,1)S(1)} %get-tuple-element.139, f32[512,4608]{1,0:T(8,128)S(1)} %get-tuple-element.119, f32[512]{0:T(512)S(1)} %get-tuple-element.120), kind=kLoop, calls=%fused_computation.4.clone.1 | loop fusion | flops 11795968 | bytes 11800576 | tf_op jit(solution)/shard_map/while/body/eval_jaxpr/reduce_sum | solution.py:74
  145.3 3.9 %fusion.101 = bf16[1,512,128]{2,1,0:T(8,128)(2,1)} fusion(bf16[4608,128]{1,0:T(8,128)(2,1)S(1)} %copy-done.9, pred[512,4608]{1,0:T(32,128)(4,1)S(1)} %get-tuple-element.139, f32[512,4608]{1,0:T(8,128)S(1)} %get-tuple-element.119, f32[512]{0:T(512)S(1)} %get-tuple-element.120, f32[512]{0:T(512)S(1)} %fusion.100), kind=kOutput, calls=%fused_computation.8.clone.1 | convolution fusion | flops 615907328 | bytes 13111296 | tf_op jit(solution)/shard_map/while/body/eval_jaxpr/dot_general | solution.py:75
  155.6 3.1 %fusion.100 = f32[512]{0:T(512)S(1)} fusion(pred[512,4608]{1,0:T(32,128)(4,1)S(1)} %get-tuple-element.139, f32[512,4608]{1,0:T(8,128)S(1)} %get-tuple-element.119, f32[512]{0:T(512)S(1)} %get-tuple-element.120), kind=kLoop, calls=%fused_computation.4.clone.1 | loop fusion | flops 11795968 | bytes 11800576 | tf_op jit(solution)/shard_map/while/body/eval_jaxpr/reduce_sum | solution.py:74
  158.7 3.9 %fusion.101 = bf16[1,512,128]{2,1,0:T(8,128)(2,1)} fusion(bf16[4608,128]{1,0:T(8,128)(2,1)S(1)} %copy-done.9, pred[512,4608]{1,0:T(32,128)(4,1)S(1)} %get-tuple-element.139, f32[512,4608]{1,0:T(8,128)S(1)} %get-tuple-element.119, f32[512]{0:T(512)S(1)} %get-tuple-element.120, f32[512]{0:T(512)S(1)} %fusion.100), kind=kOutput, calls=%fused_computation.8.clone.1 | convolution fusion | flops 615907328 | bytes 13111296 | tf_op jit(solution)/shard_map/while/body/eval_jaxpr/dot_general | solution.py:75
  165.9 5.6 %add_convert_fusion = bf16[512,2048]{1,0:T(8,128)(2,1)} fusion(f32[512,2048]{1,0:T(8,128)} %fusion.35, bf16[512,512]{0,1:T(8,128)(2,1)} %bitcast.134, bf16[512,2048]{1,0:T(8,128)(2,1)} %param.30), kind=kOutput, calls=%fused_computation.24 | convolution fusion | flops 1075838976 | bytes 8912896 | tf_op jit(solution)/shard_map/dot_general | solution.py:173
  175.1 7.4 %reduce-scatter.2.cloned.1.call-done = bf16[512,1024]{1,0:T(8,128)(2,1)} async-done(((bf16[512,2048]{1,0:T(8,128)(2,1)}), bf16[512,1024]{1,0:T(8,128)(2,1)}) %reduce-scatter.2.cloned.1.call-update) | async-done | bytes 1048592 | tf_op jit(solution)/shard_map/reduce_scatter | solution.py:209
  (157 shorter events, 78.0 us)
Async XLA Ops:
  7.2 97.0 %copy-start = (bf16[768,2048]{1,0:T(8,128)(2,1)S(1)}, bf16[768,2048]{1,0:T(8,128)(2,1)}, u32[]{:S(2)}) copy-start(bf16[768,2048]{1,0:T(8,128)(2,1)} %param.46) | copy-start | bytes 9437188
  7.2 15.8 %copy-start.19 = (f32[4,768]{1,0:T(4,128)S(1)}, f32[4,768]{1,0:T(4,128)}, u32[]{:S(2)}) copy-start(f32[4,768]{1,0:T(4,128)} %param.38) | copy-start | bytes 36868
  7.2 30.6 %all-gather.2.cloned.1.call-start = ((), (), s32[]{:S(2)}) async-start(), calls=%async_computation.3 | async-start | bytes 3145728 | tf_op jit(solution)/shard_map/all_gather | solution.py:104
  10.5 12.5 %all-to-all-start = ((s32[16,1,2]{2,1,0:T(1,128)}), s32[16,1,2]{2,1,0:T(1,128)S(1)}, u32[]{:S(2)}, u32[]{:S(2)}) async-start(s32[16,1,2]{2,1,0:T(1,128)} %copy.97), calls=%async_computation | async-start | bytes 16384 | tf_op jit(solution)/shard_map/all_to_all | solution.py:136
  31.2 8.8 %copy-start.20 = (f32[2048]{0:T(1024)S(1)}, f32[2048]{0:T(1024)}, u32[]{:S(2)}) copy-start(f32[2048]{0:T(1024)} %param.26) | copy-start | bytes 24580
  31.2 77.1 %all-to-all-start.1 = ((bf16[16,2,2,1,128,128]{5,4,1,3,2,0:T(8,128)(2,1)}), bf16[16,2,2,1,128,128]{5,4,1,3,2,0:T(8,128)(2,1)}, u32[]{:S(2)}, u32[]{:S(2)}) async-start(bf16[16,2,2,1,128,128]{5,4,1,3,2,0:T(8,128)(2,1)} %copy.98), calls=%async_computation.1 | async-start | bytes 4194304 | tf_op jit(solution)/shard_map/all_to_all | solution.py:138
  37.7 144.8 %reduce-scatter.2.cloned.1.call-start = ((), (), s32[]{:S(2)}) async-start(), calls=%async_computation.4 | async-start | bytes 3145728 | tf_op jit(solution)/shard_map/reduce_scatter | solution.py:209
  45.9 8.9 %copy-start.25 = (f32[12]{0:T(128)}, f32[12]{0:T(128)S(1)}, u32[]{:S(2)}) copy-start(f32[12]{0:T(128)S(1)} %slice_reduce_fusion.1) | copy-start | bytes 148
  46.0 4.3 %copy-start.23 = (bf16[1,3,768]{2,1,0:T(4,128)(2,1)S(1)}, bf16[1,3,768]{2,1,0:T(4,128)(2,1)}, u32[]{:S(2)}) copy-start(bf16[1,3,768]{2,1,0:T(4,128)(2,1)} %param.40) | copy-start | bytes 13828
  54.9 2.8 %copy-start.30 = (bf16[2048,512]{1,0:T(8,128)(2,1)S(1)}, bf16[2048,512]{1,0:T(8,128)(2,1)}, u32[]{:S(2)}) copy-start(bf16[2048,512]{1,0:T(8,128)(2,1)} %param.36) | copy-start | bytes 6291460
  57.7 2.9 %copy-start.24 = (bf16[1,3,512]{2,1,0:T(4,128)(2,1)S(1)}, bf16[1,3,512]{2,1,0:T(4,128)(2,1)}, u32[]{:S(2)}) copy-start(bf16[1,3,512]{2,1,0:T(4,128)(2,1)} %param.41) | copy-start | bytes 9220
  57.7 3.0 %copy-start.21 = (f32[1,512]{1,0:T(1,128)S(1)}, f32[1,512]{1,0:T(1,128)}, u32[]{:S(2)}) copy-start(f32[1,512]{1,0:T(1,128)} %get-tuple-element.71) | copy-start | bytes 6148
  57.7 3.1 %copy-start.22 = (f32[1,512]{1,0:T(1,128)S(1)}, f32[1,512]{1,0:T(1,128)}, u32[]{:S(2)}) copy-start(f32[1,512]{1,0:T(1,128)} %get-tuple-element.72) | copy-start | bytes 6148
  61.4 5.6 %copy-start.7 = (bf16[512,512]{1,0:T(8,128)(2,1)}, bf16[512,512]{1,0:T(8,128)(2,1)S(1)}, u32[]{:S(2)}) copy-start(bf16[512,512]{1,0:T(8,128)(2,1)S(1)} %multiply_convert_fusion.5) | copy-start | bytes 1572868
  72.4 5.2 %copy-start.13 = (bf16[2048,128]{1,0:T(8,128)(2,1)S(1)}, bf16[2048,128]{1,0:T(8,128)(2,1)}, u32[]{:S(2)}) copy-start(bf16[2048,128]{1,0:T(8,128)(2,1)} %param.28) | copy-start | bytes 1572868
  77.6 2.5 %copy-start.16 = (f32[512,64]{0,1:T(8,128)S(1)}, f32[512,64]{0,1:T(8,128)}, u32[]{:S(2)}) copy-start(f32[512,64]{0,1:T(8,128)} %get-tuple-element.74) | copy-start | bytes 393220
  101.1 3.1 %copy-start.6 = (f32[512,768]{1,0:T(8,128)S(1)}, f32[512,768]{1,0:T(8,128)}, u32[]{:S(2)}) copy-start(f32[512,768]{1,0:T(8,128)} %copy.106) | copy-start | bytes 4718596
  101.1 3.1 %copy-start.11 = (bf16[512,768]{1,0:T(8,128)(2,1)S(1)}, bf16[512,768]{1,0:T(8,128)(2,1)}, u32[]{:S(2)}) copy-start(bf16[512,768]{1,0:T(8,128)(2,1)} %convolution_convert_fusion) | copy-start | bytes 2359300
  101.1 3.1 %copy-start.31 = (f32[768]{0:T(1024)S(1)}, f32[768]{0:T(1024)}, u32[]{:S(2)}) copy-start(f32[768]{0:T(1024)} %param.45) | copy-start | bytes 9220
  115.3 3.1 %copy-start.9 = (bf16[4608,128]{1,0:T(8,128)(2,1)S(1)}, bf16[4608,128]{1,0:T(8,128)(2,1)}, u32[]{:S(2)}) copy-start(bf16[4608,128]{1,0:T(8,128)(2,1)} %get-tuple-element.140) | copy-start | bytes 3538948 | tf_op jit(solution)/shard_map/while
  128.7 3.1 %copy-start.9 = (bf16[4608,128]{1,0:T(8,128)(2,1)S(1)}, bf16[4608,128]{1,0:T(8,128)(2,1)}, u32[]{:S(2)}) copy-start(bf16[4608,128]{1,0:T(8,128)(2,1)} %get-tuple-element.140) | copy-start | bytes 3538948 | tf_op jit(solution)/shard_map/while
  142.1 3.1 %copy-start.9 = (bf16[4608,128]{1,0:T(8,128)(2,1)S(1)}, bf16[4608,128]{1,0:T(8,128)(2,1)}, u32[]{:S(2)}) copy-start(bf16[4608,128]{1,0:T(8,128)(2,1)} %get-tuple-element.140) | copy-start | bytes 3538948 | tf_op jit(solution)/shard_map/while
  155.6 3.1 %copy-start.9 = (bf16[4608,128]{1,0:T(8,128)(2,1)S(1)}, bf16[4608,128]{1,0:T(8,128)(2,1)}, u32[]{:S(2)}) copy-start(bf16[4608,128]{1,0:T(8,128)(2,1)} %get-tuple-element.140) | copy-start | bytes 3538948 | tf_op jit(solution)/shard_map/while
  171.5 11.0 %copy-start.1 = (bf16[768,2048]{1,0:T(8,128)(2,1)S(1)}, bf16[768,2048]{1,0:T(8,128)(2,1)}, u32[]{:S(2)}) copy-start(bf16[768,2048]{1,0:T(8,128)(2,1)} %param.46) | copy-start | bytes 9437188
  (15 other events, 27.1 us)
Sparse Core Ops, SparseCore 0:
  9.6 12.4 all-gather.1
  171.6 10.8 reduce-scatter.1
where the time goes:
time: 191 us; the launch traced here: 189 us
  matrix products  70.3 us (37%)
  other arithmetic  40.3 us (21%)
  local copies, waits for them, and re-layouts  38.2 us (20%)
  between operations  15.2 us (8%)
  starting transfers between devices  13.2 us (7%)
  waiting for transfers between devices  8.15 us (4%)
  blocking collectives  3.94 us (2%)
    dot_general x4, matrix products, attend(): jnp.dot(weights.astype(jnp.bfloat16), value_rows, preferred_element_type=...  15.8 us
    dynamic_update_slice x8, local copies, waits for them, and re-layouts, shards(): contexts = [lax.map(one_head, head_queries)]  12.9 us
    reduce_sum x4, other arithmetic, attend(): weight_sum = jnp.sum(weights, axis=-1, keepdims=True)  12.5 us
    dot_general x4, matrix products, attend(): jnp.einsum('rd,kd->rk', query_rows, key_rows, preferred_element_type=jnp....  12.5 us
    convert_element_type x4, other arithmetic, stored(): return lax.optimization_barrier(value_vectors.astype(jnp.bfloat16))  8.47 us
    reduce_scatter x1, waiting for transfers between devices, shards(): lax.psum_scatter((attn_part + ssm_part).astype(jnp.bfloat16), 'tp', scatt...  7.43 us
    all_to_all x1, starting transfers between devices, shards(): lax.all_to_all(want_slot, 'req', split_axis=0, concat_axis=0, tiled=True)  6.61 us
    all_to_all x1, starting transfers between devices, shards(): lax.all_to_all(fetched, 'req', split_axis=0, concat_axis=0, tiled=True)  6.49 us
  transfers between devices with their start and end apart: 4, of which 1 were waited for; matrix products, arithmetic and copies ran while one was open for 45% of the time, Pallas kernels for 0%

commit v1 on v0

v1 whole, which is shorter than its diff:
```python
import functools

import jax
import jax.numpy as jnp
from jax import lax
from jax.experimental import pallas as pl
from jax.experimental.pallas import tpu as pltpu
from jax.sharding import PartitionSpec as P

HEAD_SIZE = 128
MP = 64
MN = 256
DSSM = 1536

EPSILON = 1e-05
ROPE_BASE = 100000.0
NEG_FILL = -1e30
LOG2E = 1.4426950408889634
SCORE_SCALE = HEAD_SIZE ** (-0.5) * LOG2E
VMEM_BYTES = 56 * 2**20

VMEM = pl.BlockSpec(memory_space=pltpu.VMEM)
SMEM = pl.BlockSpec(memory_space=pltpu.SMEM)
ANY = pl.BlockSpec(memory_space=pl.ANY)
F32 = jnp.float32
BF16 = jnp.bfloat16


def params(*semantics):
    return pltpu.CompilerParams(
        vmem_limit_bytes=VMEM_BYTES, dimension_semantics=semantics or None
    )


def rope_tables(token_positions):
    half_width = HEAD_SIZE // 2
    inverse = ROPE_BASE ** (-2.0 * jnp.arange(half_width, dtype=F32) / HEAD_SIZE)
    angles = token_positions.astype(F32)[:, None] * inverse[None, :]
    cosine, sine = jnp.cos(angles), jnp.sin(angles)
    return (
        jnp.concatenate([cosine, cosine], axis=-1),
        jnp.concatenate([-sine, sine], axis=-1),
    )


def pick_pages(table_row, devices, pages_dev, capacity):
    owners = table_row // pages_dev
    local_slot = table_row % pages_dev
    page_index = jnp.arange(table_row.shape[0], dtype=jnp.int32)
    earlier = (page_index[None, :] < page_index[:, None]) & (owners[None, :] == owners[:, None])
    ranks = jnp.sum(earlier.astype(jnp.int32), axis=1)
    targets = jnp.arange(devices, dtype=jnp.int32)
    places = jnp.arange(capacity, dtype=jnp.int32)
    chosen = (
        (owners[None, None, :] == targets[:, None, None])
        & (ranks[None, None, :] == places[None, :, None])
    ).astype(jnp.int32)
    return (
        jnp.sum(chosen * local_slot, axis=-1),
        jnp.sum(chosen * page_index, axis=-1),
        jnp.sum(chosen, axis=-1),
    )


def gather_kernel(count, want_ref, pages_ref, out_ref, sems):
    copies = [
        pltpu.make_async_copy(pages_ref.at[want_ref[i]], out_ref.at[i], sems.at[i])
        for i in range(count)
    ]
    for copy in copies:
        copy.start()
    for copy in copies:
        copy.wait()


def gather_pages(want, kv_pages):
    count = want.shape[0]
    return pl.pallas_call(
        functools.partial(gather_kernel, count),
        out_shape=jax.ShapeDtypeStruct((count,) + kv_pages.shape[1:], kv_pages.dtype),
        in_specs=[SMEM, ANY],
        out_specs=ANY,
        scratch_shapes=[pltpu.SemaphoreType.DMA((count,))],
        compiler_params=params(),
        cost_estimate=pl.CostEstimate(flops=0, bytes_accessed=8 * 2**20, transcendentals=0),
        name="gather_pages",
    )(want, kv_pages)


def project_kernel(
    core_ref, mine_ref, other_ref, gain_ref, cos_ref, sin_ref,
    wq_hbm, wk_hbm, wv_hbm, wx_hbm, wbc_hbm, wdt_hbm, wz_hbm,
    q_ref, k_ref, v_ref, x_ref, bc_ref, dt_ref, z_ref,
    normed, wq, wkv, wx, wbc, wdt, wz, sems,
):
    copies = [
        pltpu.make_async_copy(source, target, sems.at[i])
        for i, (source, target) in enumerate(
            (
                (wq_hbm, wq),
                (wk_hbm, wkv.at[:, 0:HEAD_SIZE]),
                (wv_hbm, wkv.at[:, HEAD_SIZE : 2 * HEAD_SIZE]),
                (wbc_hbm, wbc),
                (wdt_hbm, wdt),
                (wx_hbm, wx),
                (wz_hbm, wz),
            )
        )
    ]
    for copy in copies:
        copy.start()
    rows, half = mine_ref.shape
    core = core_ref[0]
    here = pl.ds(pl.multiple_of(core * half, half), half)
    there = pl.ds(pl.multiple_of((1 - core) * half, half), half)
    step = 64

    def norm_rows(i, carry):
        block = pl.ds(pl.multiple_of(i * step, step), step)
        mine = mine_ref[block, :].astype(F32)
        other = other_ref[block, :].astype(F32)
        total = jnp.sum(mine * mine + other * other, axis=-1, keepdims=True)
        scale = lax.rsqrt(total / (2 * half) + EPSILON)
        normed[block, here] = (mine * scale * gain_ref[:, here]).astype(BF16)
        normed[block, there] = (other * scale * gain_ref[:, there]).astype(BF16)
        return carry

    lax.fori_loop(0, rows // step, norm_rows, 0)

    def rope(vectors):
        return vectors * cos_ref[...] + pltpu.roll(vectors, HEAD_SIZE // 2, 1) * sin_ref[...]

    copies[0].wait()
    for tile in range(wq.shape[1] // 256):
        two = jnp.dot(
            normed[...], wq[:, tile * 256 : tile * 256 + 256], preferred_element_type=F32
        )
        for side in range(2):
            head = 2 * tile + side
            q_ref[head * rows : (head + 1) * rows, :] = rope(
                two[:, side * HEAD_SIZE : (side + 1) * HEAD_SIZE]
            ).astype(BF16)
    copies[1].wait()
    copies[2].wait()
    two = jnp.dot(normed[...], wkv[...], preferred_element_type=F32)
    k_ref[...] = rope(two[:, :HEAD_SIZE]).astype(BF16)
    v_ref[...] = two[:, HEAD_SIZE:].astype(BF16)
    for index, weight, target in ((3, wbc, bc_ref), (4, wdt, dt_ref), (5, wx, x_ref), (6, wz, z_ref)):
        copies[index].wait()
        width = weight.shape[1]
        for start in range(0, width, 256):
            stop = min(start + 256, width)
            target[:, start:stop] = jnp.dot(
                normed[...], weight[:, start:stop], preferred_element_type=F32
            ).astype(target.dtype)


def project(core, mine, other, gain, cosine, sine, wq, wk, wv, wx, wbc, wdt, wz):
    rows, half = mine.shape
    width = 2 * half

    def out(shape, dtype=BF16):
        return jax.ShapeDtypeStruct(shape, dtype)

    return pl.pallas_call(
        project_kernel,
        out_shape=(
            out((wq.shape[1] // HEAD_SIZE * rows, HEAD_SIZE)),
            out((rows, wk.shape[1])),
            out((rows, wv.shape[1])),
            out((rows, wx.shape[1])),
            out((rows, wbc.shape[1])),
            out((rows, wdt.shape[1]), F32),
            out((rows, wz.shape[1])),
        ),
        in_specs=[SMEM] + [VMEM] * 5 + [ANY] * 7,
        out_specs=(VMEM,) * 7,
        scratch_shapes=[
            pltpu.VMEM((rows, width), BF16),
            pltpu.VMEM(wq.shape, BF16),
            pltpu.VMEM((width, 2 * HEAD_SIZE), BF16),
            pltpu.VMEM(wx.shape, BF16),
            pltpu.VMEM(wbc.shape, BF16),
            pltpu.VMEM(wdt.shape, BF16),
            pltpu.VMEM(wz.shape, BF16),
            pltpu.SemaphoreType.DMA((7,)),
        ],
        compiler_params=params(),
        cost_estimate=pl.CostEstimate(
            flops=6 * 10**9, bytes_accessed=17 * 2**20, transcendentals=0
        ),
        name="project",
    )(core, mine, other, gain, cosine, sine, wq, wk, wv, wx, wbc, wdt, wz)


def silu(value):
    return value / (1.0 + jnp.exp(-value))


def mixer_kernel(
    x_ref, z_ref, bc_ref, dt_ref, histx_ref, histbc_ref, convx_ref, convbc_ref,
    bias_ref, rate_ref, skip_ref, gain_ref, state_ref,
    gated_ref, square_ref, last_ref,
    padded, inner, cum, cum_t, step_size, b_ref, c_ref,
):
    rows = x_ref.shape[0]
    taps = convx_ref.shape[0]
    heads = dt_ref.shape[1]
    group = 2 * MP
    half = rows // 2

    def conv(history, fresh, kernel):
        width = fresh.shape[1]
        padded[0:8, 0:width] = jnp.zeros((8, width), F32)
        padded[8 - (taps - 1) : 8, 0:width] = history.astype(F32)
        padded[8 : 8 + rows, 0:width] = fresh.astype(F32)
        summed = padded[9 - taps : 9 - taps + rows, 0:width] * kernel[0:1, :]
        for tap in range(1, taps):
            begin = 9 - taps + tap
            summed = summed + padded[begin : begin + rows, 0:width] * kernel[tap : tap + 1, :]
        return silu(summed).astype(BF16)

    for start in range(0, 2 * MN, group):
        part = conv(
            histbc_ref[0, :, start : start + group],
            bc_ref[:, start : start + group],
            convbc_ref[:, start : start + group],
        )
        if start < MN:
            b_ref[:, start : start + group] = part
        else:
            c_ref[:, start - MN : start - MN + group] = part

    raw = dt_ref[...] + bias_ref[...]
    size = jnp.maximum(raw, 0.0) + jnp.log1p(jnp.exp(-jnp.abs(raw)))
    step_size[:, 0:heads] = size
    row_index = lax.broadcasted_iota(jnp.int32, (rows, rows), 0)
    column_index = lax.broadcasted_iota(jnp.int32, (rows, rows), 1)
    causal = column_index <= row_index
    drop = jnp.zeros((rows, 128), F32)
    cum[...] = drop
    cum[:, 0:heads] = -size * (rate_ref[...] * LOG2E)
    cum[...] = jnp.dot(
        causal.astype(F32), cum[...], precision=lax.Precision.HIGHEST, preferred_element_type=F32
    )
    cum_t[...] = cum[...].T
    inner[...] = jnp.where(
        causal,
        lax.dot_general(
            c_ref[...], b_ref[...], (((1,), (1,)), ((), ())), preferred_element_type=F32
        ),
        0.0,
    )
    lane = lax.broadcasted_iota(jnp.int32, (1, group), 1)
    first = lane < MP
    first_rows = lax.broadcasted_iota(jnp.int32, (group, 1), 0) < MP
    squares = jnp.zeros((rows, group), F32)
    for pair in range(heads // 2):
        cols = slice(pair * group, (pair + 1) * group)
        one, two = 2 * pair, 2 * pair + 1
        x_rows = conv(histx_ref[0, :, cols], x_ref[:, cols], convx_ref[:, cols]).astype(F32)
        sizes = jnp.where(first, step_size[:, one : one + 1], step_size[:, two : two + 1])
        fades = jnp.where(first, cum[:, one : one + 1], cum[:, two : two + 1])
        last_fade = fades[rows - 1 : rows, :]
        moved_float = x_rows * sizes
        moved = moved_float.astype(BF16)
        tail_moved = moved_float * jnp.exp2(last_fade - fades)
        state = state_ref[cols, :]
        state_high = state.astype(BF16)
        state_low = (state - state_high.astype(F32)).astype(BF16)
        contract = (((1,), (1,)), ((), ()))
        carried = lax.dot_general(
            c_ref[...], state_high, contract, preferred_element_type=F32
        ) + lax.dot_general(c_ref[...], state_low, contract, preferred_element_type=F32)
        blocks = []
        for begin in (0, half):
            end = begin + half
            sides = []
            for head in (one, two):
                gap = cum[begin:end, head : head + 1] - cum_t[head : head + 1, 0:end]
                mixing = (jnp.exp2(jnp.minimum(gap, 0.0)) * inner[begin:end, 0:end]).astype(BF16)
                sides.append(jnp.dot(mixing, moved[0:end, :], preferred_element_type=F32))
            blocks.append(jnp.where(first, sides[0], sides[1]))
        ssm_y = (
            jnp.concatenate(blocks, axis=0)
            + carried * jnp.exp2(fades)
            + skip_ref[:, cols] * x_rows
        )
        gated = ssm_y * silu(z_ref[:, cols].astype(F32))
        squares = squares + gated * gated
        gated_ref[:, cols] = (gated * gain_ref[:, cols]).astype(BF16)
        added = jnp.dot(tail_moved.T.astype(BF16), b_ref[...], preferred_element_type=F32)
        ends = jnp.exp2(cum_t[one : two + 1, rows - 1 : rows])
        keep = jnp.where(first_rows, ends[0:1, :], ends[1:2, :])
        last_ref[cols, :] = keep * state + added
    square_ref[...] = jnp.sum(squares.T, axis=0, keepdims=True)


def mixer(x, z, bc, dt, histx, histbc, convx, convbc, bias, rate, skip, gain, state):
    rows, width = x.shape
    return pl.pallas_call(
        mixer_kernel,
        out_shape=(
            jax.ShapeDtypeStruct((rows, width), BF16),
            jax.ShapeDtypeStruct((1, rows), F32),
            jax.ShapeDtypeStruct(state.shape, F32),
        ),
        in_specs=[VMEM] * 13,
        out_specs=(VMEM,) * 3,
        scratch_shapes=[
            pltpu.VMEM((rows + 8, 2 * MP), F32),
            pltpu.VMEM((rows, rows), F32),
            pltpu.VMEM((rows, 128), F32),
            pltpu.VMEM((128, rows), F32),
            pltpu.VMEM((rows, 128), F32),
            pltpu.VMEM((rows, MN), BF16),
            pltpu.VMEM((rows, MN), BF16),
        ],
        compiler_params=params(),
        cost_estimate=pl.CostEstimate(
            flops=4 * 10**9, bytes_accessed=8 * 2**20, transcendentals=4 * 10**6
        ),
        name="mixer",
    )(x, z, bc, dt, histx, histbc, convx, convbc, bias, rate, skip, gain, state)


def attend_kernel(
    seen_ref, q_ref, fresh_k_ref, fresh_v_ref, kv_hbm, out_ref, keys, values, sems,
):
    pages, _, page_size, _ = kv_hbm.shape
    block = q_ref.shape[0]
    rows = fresh_k_ref.shape[0]
    chunk = 4 * page_size
    index = pl.program_id(0)
    lane_zero = lax.broadcasted_iota(jnp.int32, (page_size, HEAD_SIZE), 1) == 0

    @pl.when(index == 0)
    def _():
        copies = []
        for page in range(pages):
            place = pl.ds(page * page_size, page_size)
            for which, target in ((0, keys), (1, values)):
                copies.append(
                    pltpu.make_async_copy(
                        kv_hbm.at[page, which],
                        target.at[place, 0:HEAD_SIZE],
                        sems.at[2 * page + which],
                    )
                )
        for copy in copies:
            copy.start()
        token = lax.broadcasted_iota(jnp.int32, (page_size, HEAD_SIZE), 0)
        values[:, HEAD_SIZE:] = jnp.ones((pages * page_size, HEAD_SIZE), BF16)
        for page in range(pages):
            hidden = lane_zero & (token >= seen_ref[page])
            keys[page * page_size : (page + 1) * page_size, HEAD_SIZE:] = jnp.where(
                hidden, NEG_FILL, 0.0
            ).astype(BF16)
        for copy in copies:
            copy.wait()

    query = q_ref[...]
    contract = (((1,), (1,)), ((), ()))
    row = lax.broadcasted_iota(jnp.int32, (block, rows), 0) + lax.rem(index * block, rows)
    column = lax.broadcasted_iota(jnp.int32, (block, rows), 1)
    scores = lax.dot_general(query, fresh_k_ref[...], contract, preferred_element_type=F32)
    scores = jnp.where(column <= row, scores, NEG_FILL)
    top = jnp.max(scores, axis=-1, keepdims=True)
    weights = jnp.exp2((scores - top) * SCORE_SCALE).astype(BF16)
    fresh = jnp.concatenate([fresh_v_ref[...], jnp.ones((rows, HEAD_SIZE), BF16)], axis=1)
    total = jnp.dot(weights, fresh, preferred_element_type=F32)
    one_hot = (lax.broadcasted_iota(jnp.int32, (block, HEAD_SIZE), 1) == 0).astype(BF16)
    wide_query = jnp.concatenate([query, one_hot], axis=1)
    for start in range(0, pages * page_size, chunk):
        span = slice(start, min(start + chunk, pages * page_size))
        scores = lax.dot_general(wide_query, keys[span, :], contract, preferred_element_type=F32)
        new_top = jnp.maximum(top, jnp.max(scores, axis=-1, keepdims=True))
        fade = jnp.exp2((top - new_top) * SCORE_SCALE)
        weights = jnp.exp2((scores - new_top) * SCORE_SCALE).astype(BF16)
        total = total * fade + jnp.dot(weights, values[span, :], preferred_element_type=F32)
        top = new_top
    out_ref[...] = (total[:, :HEAD_SIZE] / total[:, HEAD_SIZE:]).astype(BF16)


def attend(seen, queries, fresh_keys, fresh_values, kv):
    pages, _, page_size, _ = kv.shape
    rows = fresh_keys.shape[0]
    block = rows // 2
    per_head = rows // block
    return pl.pallas_call(
        attend_kernel,
        out_shape=jax.ShapeDtypeStruct((rows, queries.shape[0] // rows * HEAD_SIZE), BF16),
        grid=(queries.shape[0] // block,),
        in_specs=[
            SMEM,
            pl.BlockSpec((block, HEAD_SIZE), lambda i: (i, 0)),
            pl.BlockSpec((rows, HEAD_SIZE), lambda i: (0, 0)),
            pl.BlockSpec((rows, HEAD_SIZE), lambda i: (0, 0)),
            ANY,
        ],
        out_specs=pl.BlockSpec((block, HEAD_SIZE), lambda i: (i % per_head, i // per_head)),
        scratch_shapes=[
            pltpu.VMEM((pages * page_size, 2 * HEAD_SIZE), BF16),
            pltpu.VMEM((pages * page_size, 2 * HEAD_SIZE), BF16),
            pltpu.SemaphoreType.DMA((2 * pages,)),
        ],
        compiler_params=params("arbitrary"),
        cost_estimate=pl.CostEstimate(
            flops=16 * 10**9, bytes_accessed=4 * 2**20, transcendentals=10**7
        ),
        name="attend",
    )(seen, queries, fresh_keys, fresh_values, kv)


def mixer_out_kernel(gated_ref, scale_ref, weight_ref, out_ref):
    out_ref[...] = (
        jnp.dot(gated_ref[...], weight_ref[...], preferred_element_type=F32) * scale_ref[...]
    )


def mixer_out(gated, scale, weight):
    rows, depth = gated.shape
    width = weight.shape[1]
    tile = 256
    return pl.pallas_call(
        mixer_out_kernel,
        out_shape=jax.ShapeDtypeStruct((rows, width), F32),
        grid=(width // tile,),
        in_specs=[
            pl.BlockSpec((rows, depth), lambda i: (0, 0)),
            pl.BlockSpec((rows, 1), lambda i: (0, 0)),
            pl.BlockSpec((depth, tile), lambda i: (0, i)),
        ],
        out_specs=pl.BlockSpec((rows, tile), lambda i: (0, i)),
        compiler_params=params("arbitrary"),
        cost_estimate=pl.CostEstimate(
            flops=2 * rows * depth * width, bytes_accessed=8 * 2**20, transcendentals=0
        ),
        name="mixer_out",
    )(gated, scale, weight)


def attn_out_kernel(core_ref, context_ref, weight_ref, part_ref, out_ref):
    out_ref[...] = (
        jnp.dot(context_ref[...], weight_ref[...], preferred_element_type=F32) + part_ref[...]
    ).astype(out_ref.dtype)


def attn_out(core, context, weight, part, dtype):
    rows, depth = context.shape
    tile = 256
    tiles = weight.shape[1] // 2 // tile
    return pl.pallas_call(
        attn_out_kernel,
        out_shape=jax.ShapeDtypeStruct((rows, weight.shape[1] // 2), dtype),
        grid_spec=pltpu.PrefetchScalarGridSpec(
            num_scalar_prefetch=1,
            grid=(tiles,),
            in_specs=[
                pl.BlockSpec((rows, depth), lambda i, core: (0, 0)),
                pl.BlockSpec((depth, tile), lambda i, core: (0, core[0] * tiles + i)),
                pl.BlockSpec((rows, tile), lambda i, core: (0, core[0] * tiles + i)),
            ],
            out_specs=pl.BlockSpec((rows, tile), lambda i, core: (0, i)),
        ),
        compiler_params=params("arbitrary"),
        cost_estimate=pl.CostEstimate(
            flops=rows * depth * weight.shape[1], bytes_accessed=4 * 2**20, transcendentals=0
        ),
        name="attn_out",
    )(core, context, weight, part)


def shards(
    tokens,
    attn_gain,
    w_query,
    key_weight,
    value_weight,
    w_attn_out,
    kv_pages,
    page_table,
    cached_len,
    w_gate_z,
    w_ssm_in,
    w_bc,
    w_dt,
    conv_w_x,
    conv_w_bc,
    conv_x_state,
    conv_bc_state,
    dt_bias,
    decay_rate,
    skip_gain,
    mixer_gain,
    w_mixer_out,
    ssm_state,
):
    swap = [(0, 1), (1, 0)]
    core = lax.axis_index("tp").astype(jnp.int32).reshape(1)
    row_count = tokens.shape[0]
    devices = lax.axis_size("req")
    pages_dev = kv_pages.shape[0]
    capacity = pages_dev // devices
    page_size = kv_pages.shape[3]
    length = cached_len[0]

    want_slot, page_of, present = pick_pages(page_table[0], devices, pages_dev, capacity)
    requested = lax.all_to_all(want_slot, "req", split_axis=0, concat_axis=0, tiled=True)
    other = lax.ppermute(tokens, "tp", swap)
    fetched = gather_pages(
        requested.reshape(-1), kv_pages.reshape((pages_dev, 2, page_size, HEAD_SIZE))
    )
    arrived = lax.all_to_all(
        fetched.reshape((devices, capacity, 2, page_size, HEAD_SIZE)),
        "req",
        split_axis=0,
        concat_axis=0,
        tiled=True,
    ).reshape((devices * capacity, 2, page_size, HEAD_SIZE))
    seen = (present * jnp.clip(length - page_of * page_size, 0, page_size)).reshape(-1)

    cosine, sine = rope_tables(length + jnp.arange(row_count, dtype=jnp.int32))
    queries, fresh_keys, fresh_values, ssm_in, bc_in, step_raw, gate_z = project(
        core, tokens, other, attn_gain[None, :], cosine, sine,
        w_query, key_weight, value_weight, w_ssm_in, w_bc, w_dt, w_gate_z,
    )
    heads = w_dt.shape[1]
    gated, squares, last_state = mixer(
        ssm_in, gate_z, bc_in, step_raw, conv_x_state, conv_bc_state, conv_w_x, conv_w_bc,
        dt_bias[None, :], decay_rate[None, :], jnp.repeat(skip_gain, MP)[None, :],
        mixer_gain[None, :], ssm_state.reshape((heads * MP, MN)),
    )
    total = squares + lax.ppermute(squares, "tp", swap)
    scale = lax.rsqrt(total.reshape((row_count, 1)) / DSSM + EPSILON)
    part = mixer_out(gated, scale, w_mixer_out)

    context = attend(seen, queries, fresh_keys, fresh_values, arrived)
    theirs = attn_out(1 - core, context, w_attn_out, part, BF16)
    ours = attn_out(core, context, w_attn_out, part, F32)
    received = lax.ppermute(theirs, "tp", swap)
    mixed = (ours + received.astype(F32)).astype(BF16)
    return (mixed, last_state.reshape(ssm_state.shape))


def solution(mesh):
    return jax.shard_map(
        shards,
        mesh=mesh,
        in_specs=(
            P("req", "tp"),
            P(),
            P(None, "tp"),
            P(None, "tp"),
            P(None, "tp"),
            P("tp", None),
            P("req", None, "tp", None, None),
            P("req", None),
            P("req"),
            P(None, "tp"),
            P(None, "tp"),
            P(),
            P(None, "tp"),
            P(None, "tp"),
            P(),
            P("req", None, "tp"),
            P("req", None, None),
            P("tp"),
            P("tp"),
            P("tp"),
            P("tp"),
            P("tp", None),
            P("req", "tp", None, None),
        ),
        out_specs=(P("req", "tp"), P("req", "tp", None, None)),
        check_vma=False,
    )
```

time: 191 us -> 168 us (0.88)
  Pallas kernels: 0 us -> 126 us
  matrix products: 70.3 us -> 0 us
  other arithmetic: 40.3 us -> 7.99 us
  local copies, waits for them, and re-layouts: 38.2 us -> 6.53 us
  between operations: 15.2 us -> 1.38 us
  blocking collectives: 3.94 us -> 10.6 us
  starting transfers between devices: 13.2 us -> 9.68 us
  waiting for transfers between devices: 8.15 us -> 5.53 us
    pallas_call x0 -> x7, Pallas kernels: none -> 126 us  [the longest x1 65.6 us: gather_pages(): pl.pallas_call(functools.partial(gather_kernel, count), out_shape=jax.Sha...]
    dot_general x21 -> x0, matrix products: 70.3 us -> none  [the longest x4 15.8 us: attend(): jnp.dot(weights.astype(jnp.bfloat16), value_rows, preferred_element_type=...]
    reduce_sum x7 -> x1, other arithmetic: 17.1 us -> 0.2 us  [pick_pages(): jnp.sum(chosen * local_slot, axis=-1)]
    dynamic_update_slice x8 -> x0, local copies, waits for them, and re-layouts: 12.9 us -> none  [shards(): contexts = [lax.map(one_head, head_queries)]]
    all_to_all x0 -> x1, blocking collectives: none -> 10.6 us  [shards(): lax.all_to_all(want_slot, 'req', split_axis=0, concat_axis=0, tiled=True)]
    reshape x5 -> x0, local copies, waits for them, and re-layouts: 8.86 us -> none  [the longest x1 3.21 us: shards(): kv_pages[requested.reshape(-1)]]
    convert_element_type x9 -> x2, other arithmetic: 11.5 us -> 2.91 us  [the longest x1 2.91 us: shards(): mixed = (ours + received.astype(F32)).astype(BF16)]
    reduce_scatter x1 -> x0, waiting for transfers between devices: 7.43 us -> none  [shards(): lax.psum_scatter((attn_part + ssm_part).astype(jnp.bfloat16), 'tp', scatt...]
  transfers between devices with their start and end apart: 4 -> 4, of which waited for: 1 -> 2; matrix products, arithmetic and copies ran while one was open for 45% -> 4% of each run, Pallas kernels for 0% -> 22%
where the time goes in v1:
time: 168 us; the launch traced here: 167 us
  Pallas kernels  126 us (75%)
  blocking collectives  10.6 us (6%)
  starting transfers between devices  9.68 us (6%)
  other arithmetic  7.99 us (5%)
  local copies, waits for them, and re-layouts  6.53 us (4%)
  waiting for transfers between devices  5.53 us (3%)
    pallas_call x1, Pallas kernels, gather_pages(): pl.pallas_call(functools.partial(gather_kernel, count), out_shape=jax.Sha...  65.6 us
    pallas_call x1, Pallas kernels, attend(): pl.pallas_call(attend_kernel, out_shape=jax.ShapeDtypeStruct((rows, queri...  18 us
    pallas_call x1, Pallas kernels, project(): pl.pallas_call(project_kernel, out_shape=(out((wq.shape[1] // HEAD_SIZE *...  14.2 us
    pallas_call x1, Pallas kernels, mixer(): pl.pallas_call(mixer_kernel, out_shape=(jax.ShapeDtypeStruct((rows, width...  10.6 us
    all_to_all x1, blocking collectives, shards(): lax.all_to_all(want_slot, 'req', split_axis=0, concat_axis=0, tiled=True)  10.6 us
    pallas_call x2, Pallas kernels, attn_out(): pl.pallas_call(attn_out_kernel, out_shape=jax.ShapeDtypeStruct((rows, wei...  9.26 us
    pallas_call x1, Pallas kernels, mixer_out(): pl.pallas_call(mixer_out_kernel, out_shape=jax.ShapeDtypeStruct((rows, wi...  8.11 us
    all_to_all x1, starting transfers between devices, shards(): lax.all_to_all(fetched.reshape((devices, capacity, 2, page_size, HEAD_SIZ...  5.74 us
  transfers between devices with their start and end apart: 4, of which 2 were waited for; matrix products, arithmetic and copies ran while one was open for 4% of the time, Pallas kernels for 22%

profile of v1, /device:TPU:13, one launch (start us, length us, event | category | flops | bytes accessed | tf_op | source)
XLA Modules:
  0.0 167.4 jit_solution(9798200567237185907)
XLA Ops:
  0.6 0.7 fusion.5
  1.3 0.7 and_select_fusion.4
  2.4 10.6 %all_to_all.14 = s32[16,1,2]{2,1,0:T(1,128)S(1)} all-to-all(s32[16,1,2]{2,1,0:T(1,128)S(1)} %copy.35), channel_id=1, replica_groups=mesh['req'=16,'tp'=2] {'req'}, dimensions={0} | all-to-all | bytes 256 | tf_op jit(solution)/shard_map/all_to_all | solution.py:509
  13.5 0.7 reduce.3
  14.8 65.6 %gather_pages.1 = bf16[32,2,128,128]{3,2,1,0:T(8,128)(2,1)} custom-call(s32[32]{0:T(128)} %reshape.200.want_ref, bf16[32,2,128,128]{3,2,1,0:T(8,128)(2,1)} %bitcast.33), custom_call_target="tpu_custom_call" | custom-call | bytes 8388608 | tf_op jit(solution)/shard_map/gather_pages/pallas_call | solution.py:78
  80.4 5.7 %all-to-all-start.1 = ((bf16[16,2,2,128,128]{4,3,2,1,0:T(8,128)(2,1)}), bf16[16,2,2,128,128]{4,3,2,1,0:T(8,128)(2,1)S(1)}, u32[]{:S(2)}, u32[]{:S(2)}) async-start(bf16[16,2,2,128,128]{4,3,2,1,0:T(8,128)(2,1)} %bitcast.32), calls=%async_computation.1 | async-start | bytes 4194304 | tf_op jit(solution)/shard_map/all_to_all | solution.py:514
  86.2 2.5 %collective-permute-start = (bf16[512,1024]{1,0:T(8,128)(2,1)S(1)}, bf16[512,1024]{1,0:T(8,128)(2,1)}, u32[]{:S(2)}, u32[]{:S(2)}) collective-permute-start(bf16[512,1024]{1,0:T(8,128)(2,1)S(1)} %copy-done.4), channel_id=1, source_target_pairs={{0,1},{1,0},{2,3},{3,2},{4,5},{5,4},{6,7},{7,6},{8,9},{9,8},{10,11... | collective-permute-start | bytes 3145736 | tf_op jit(solution)/shard_map/ppermute | solution.py:510
  90.0 0.7 broadcast_in_dim_reshape.3.skip_ref
  90.6 1.0 copy.34.wdt_hbm
  91.7 1.0 fusion
  92.7 1.0 pad_maximum_fusion
  93.7 14.2 %project.1 = (bf16[2048,128]{1,0:T(8,128)(2,1)}, bf16[512,128]{1,0:T(8,128)(2,1)}, bf16[512,128]{1,0:T(8,128)(2,1)}, bf16[512,768]{1,0:T(8,128)(2,1)}, bf16[512,...) custom-call(s32[1]{0:T(128)} %bitcast.core_ref, bf16[512,1024]{1,0:T(8,128)(2,1)} %mine_ref.1, ...), custom_call_target="tpu_custom_call" | custom-call | flops 6000000000 | bytes 17825792 | tf_op jit(solution)/shard_map/project/pallas_call | solution.py:165
  107.9 10.6 %mixer.1 = (bf16[512,768]{1,0:T(8,128)(2,1)}, f32[1,512]{1,0:T(1,128)}, f32[768,256]{1,0:T(8,128)}) custom-call(bf16[512,768]{1,0:T(8,128)(2,1)} %get-tuple-element.15.x_ref, bf16[512,768]{1,0:T(8,128)(2,1)} %get-tuple-element.16.z_ref, bf16[512,512]{1,0:T(8,128)(2,1)} %get-tuple-element.17.bc_ref, f32[512,12]{1,0:T(8,128)} %get-tuple-element.18.dt_ref, ...), custom_call_target="tpu_custom_call" | custom-call | flops 4000000000 | bytes 8388608 | tf_op jit(solution)/shard_map/mixer/pallas_call | solution.py:301
  118.6 0.7 mul.49.seen_ref
  119.9 0.7 rsqrt_bitcast_fusion
  120.5 0.9 copy.36.scale_ref
  121.4 8.1 %mixer_out.1.part_ref = f32[512,2048]{1,0:T(8,128)} custom-call(bf16[512,768]{1,0:T(8,128)(2,1)} %get-tuple-element.19.gated_ref, f32[512,1]{1,0:T(8,128)} %copy.36.scale_ref, bf16[768,2048]{1,0:T(8,128)(2,1)} %weight_ref.3), custom_call_target="tpu_custom_call" | custom-call | flops 1610612736 | bytes 8388608 | tf_op jit(solution)/shard_map/mixer_out/pallas_call | solution.py:425
  129.5 4.9 %all-to-all-done.1 = bf16[16,2,2,128,128]{4,3,2,1,0:T(8,128)(2,1)S(1)} async-done(((bf16[16,2,2,128,128]{4,3,2,1,0:T(8,128)(2,1)}), bf16[16,2,2,128,128]{4,3,2,1,0:T(8,128)(2,1)S(1)}, u32[]{:S(2)}, u32[]{:S(2)}) %all-to-all-start.1) | async-done | bytes 2097184 | tf_op jit(solution)/shard_map/all_to_all | solution.py:514
  134.4 1.3 copy-done
  135.7 18.0 %attend.1.context_ref = bf16[512,512]{1,0:T(8,128)(2,1)} custom-call(s32[32]{0:T(128)} %mul.49.seen_ref, bf16[2048,128]{1,0:T(8,128)(2,1)} %get-tuple-element.12.q_ref, bf16[512,128]{1,0:T(8,128)(2,1)} %get-tuple-element.13.fresh_k_ref, bf16[512,128]{1,0:T(8,128)(2,1)} %get-tuple-element.14.fresh_v_ref, bf16[32,2,128,128]{3,2,1,0:T(8,128)(2,1)} %bitcast.34), custom_call_target="tpu_custom_call" | custom-call | flops 16000000000 | bytes 4194304 | tf_op jit(solution)/shard_map/attend/pallas_call | solution.py:390
  153.7 4.5 %attn_out.3 = bf16[512,1024]{1,0:T(8,128)(2,1)} custom-call(s32[1]{0:T(128)S(6)} %sub.23.core_ref, bf16[512,512]{1,0:T(8,128)(2,1)} %attend.1.context_ref, bf16[512,2048]{1,0:T(8,128)(2,1)} %weight_ref.5, f32[512,2048]{1,0:T(8,128)} %mixer_out.1.part_ref), custom_call_target="tpu_custom_call" | custom-call | flops 536870912 | bytes 4194304 | tf_op jit(solution)/shard_map/attn_out/pallas_call | solution.py:453
  158.2 1.5 collective-permute-start.2
  159.7 4.7 %attn_out.2 = f32[512,1024]{1,0:T(8,128)} custom-call(s32[1]{0:T(128)} %bitcast.core_ref, bf16[512,512]{1,0:T(8,128)(2,1)} %attend.1.context_ref, bf16[512,2048]{1,0:T(8,128)(2,1)} %weight_ref.5, f32[512,2048]{1,0:T(8,128)} %mixer_out.1.part_ref), custom_call_target="tpu_custom_call" | custom-call | flops 536870912 | bytes 4194304 | tf_op jit(solution)/shard_map/attn_out/pallas_call | solution.py:453
  164.5 2.9 %add_convert_fusion = bf16[512,1024]{1,0:T(8,128)(2,1)} fusion(f32[512,1024]{1,0:T(8,128)} %attn_out.2, bf16[512,1024]{1,0:T(8,128)(2,1)S(1)} %collective-permute-done.2), kind=kLoop, calls=%fused_computation | loop fusion | flops 1572864 | bytes 4194304 | tf_op jit(solution)/shard_map/convert_element_type | solution.py:542
  (26 shorter events, 3.0 us)
Async XLA Ops:
  80.4 5.8 %copy-start.4 = (bf16[512,1024]{1,0:T(8,128)(2,1)S(1)}, bf16[512,1024]{1,0:T(8,128)(2,1)}, u32[]{:S(2)}) copy-start(bf16[512,1024]{1,0:T(8,128)(2,1)} %mine_ref.1) | copy-start | bytes 3145732
  80.4 8.9 %copy-start.2 = (f32[768]{0:T(1024)S(1)}, f32[768]{0:T(1024)}, u32[]{:S(2)}) copy-start(f32[768]{0:T(1024)} %param.43) | copy-start | bytes 9220
  80.4 9.5 %copy-start.3 = (f32[12]{0:T(128)S(1)}, f32[12]{0:T(128)}, u32[]{:S(2)}) copy-start(f32[12]{0:T(128)} %param.42) | copy-start | bytes 148
  80.4 10.2 %copy-start.1 = (bf16[2048,12]{0,1:T(8,128)(2,1)S(1)}, bf16[2048,12]{0,1:T(8,128)(2,1)}, u32[]{:S(2)}) copy-start(bf16[2048,12]{0,1:T(8,128)(2,1)} %param.35) | copy-start | bytes 147460
  80.4 54.0 %all-to-all-start.1 = ((bf16[16,2,2,128,128]{4,3,2,1,0:T(8,128)(2,1)}), bf16[16,2,2,128,128]{4,3,2,1,0:T(8,128)(2,1)S(1)}, u32[]{:S(2)}, u32[]{:S(2)}) async-start(bf16[16,2,2,128,128]{4,3,2,1,0:T(8,128)(2,1)} %bitcast.32), calls=%async_computation.1 | async-start | bytes 4194304 | tf_op jit(solution)/shard_map/all_to_all | solution.py:514
  86.2 7.5 %collective-permute-start = (bf16[512,1024]{1,0:T(8,128)(2,1)S(1)}, bf16[512,1024]{1,0:T(8,128)(2,1)}, u32[]{:S(2)}, u32[]{:S(2)}) collective-permute-start(bf16[512,1024]{1,0:T(8,128)(2,1)S(1)} %copy-done.4), channel_id=1, source_target_pairs={{0,1},{1,0},{2,3},{3,2},{4,5},{5,4},{6,7},{7,6},{8,9},{9,8},{10,11... | collective-permute-start | bytes 3145736 | tf_op jit(solution)/shard_map/ppermute | solution.py:510
  118.5 1.4 collective-permute-start.1
  134.4 1.3 copy-start
  158.2 6.2 %collective-permute-start.2 = (bf16[512,1024]{1,0:T(8,128)(2,1)}, bf16[512,1024]{1,0:T(8,128)(2,1)S(1)}, u32[]{:S(2)}, u32[]{:S(2)}) collective-permute-start(bf16[512,1024]{1,0:T(8,128)(2,1)} %attn_out.3), channel_id=1, source_target_pairs={{0,1},{1,0},{2,3},{3,2},{4,5},{5,4},{6,7},{7,6},{8,9},{9,8},{10,11... | collective-permute-start | bytes 3145736 | tf_op jit(solution)/shard_map/ppermute | solution.py:541

commit v2 on v1

v2 whole, which is shorter than its diff:
```python
import functools

import jax
import jax.numpy as jnp
from jax import lax
from jax.experimental import pallas as pl
from jax.experimental.pallas import tpu as pltpu
from jax.sharding import PartitionSpec as P

HEAD_SIZE = 128
MP = 64
MN = 256
DSSM = 1536

EPSILON = 1e-05
ROPE_BASE = 100000.0
NEG_FILL = -1e30
LOG2E = 1.4426950408889634
SCORE_SCALE = HEAD_SIZE ** (-0.5) * LOG2E

VMEM = pl.BlockSpec(memory_space=pltpu.VMEM)
SMEM = pl.BlockSpec(memory_space=pltpu.SMEM)
HBM = pl.BlockSpec(memory_space=pltpu.HBM)
F32 = jnp.float32
BF16 = jnp.bfloat16


def params(mebibytes):
    return pltpu.CompilerParams(vmem_limit_bytes=mebibytes * 2**20)


def rope_tables(token_positions):
    half_width = HEAD_SIZE // 2
    inverse = ROPE_BASE ** (-2.0 * jnp.arange(half_width, dtype=F32) / HEAD_SIZE)
    angles = token_positions.astype(F32)[:, None] * inverse[None, :]
    cosine, sine = jnp.cos(angles), jnp.sin(angles)
    return (
        jnp.concatenate([cosine, cosine], axis=-1),
        jnp.concatenate([-sine, sine], axis=-1),
    )


def want_kernel(pages_dev, capacity, page_size, table_ref, length_ref, want_ref, seen_ref, counts):
    for i in range(counts.shape[0]):
        counts[i] = 0
    for i in range(want_ref.shape[1]):
        want_ref[0, i] = 0
        seen_ref[i] = 0
    for page in range(table_ref.shape[1]):
        entry = table_ref[0, page]
        owner = entry // pages_dev
        rank = counts[owner]
        counts[owner] = rank + 1
        place = owner * capacity + rank
        want_ref[0, place] = entry - owner * pages_dev
        seen_ref[place] = jnp.clip(length_ref[0] - page * page_size, 0, page_size)


def wanted(table, length, devices, pages_dev, page_size):
    capacity = pages_dev // devices
    return pl.pallas_call(
        functools.partial(want_kernel, pages_dev, capacity, page_size),
        out_shape=(
            jax.ShapeDtypeStruct((1, devices * capacity), jnp.int32),
            jax.ShapeDtypeStruct((devices * capacity,), jnp.int32),
        ),
        in_specs=[SMEM, SMEM],
        out_specs=(SMEM, SMEM),
        scratch_shapes=[pltpu.SMEM((devices,), jnp.int32)],
        name="wanted",
    )(table, length)


def share_wants(want, axis, devices):
    low = 1 << ((devices.bit_length() - 1) // 2)

    def swapped(rows, mask):
        return lax.ppermute(rows, axis, [(i, i ^ mask) for i in range(devices)])

    columns = [want] + [swapped(want, j * low) for j in range(1, devices // low)]
    mine = jnp.concatenate(columns, axis=0)
    return [mine] + [swapped(mine, i) for i in range(1, low)]


def gather_kernel(capacity, cuts, low, me_ref, *refs):
    lists, pages_ref = refs[:low], refs[low]
    outs = refs[low + 1 : low + 1 + len(cuts)]
    held, sems_in, sems_out = refs[low + 1 + len(cuts) :]
    high = lists[0].shape[0]
    me = me_ref[0]
    places = []
    for i in range(low):
        for j in range(high):
            for rank in range(capacity):
                slot = lists[i][j, me * capacity + rank]
                target = (me ^ (i + low * j)) * capacity + rank
                index = len(places)
                copy = pltpu.make_async_copy(pages_ref.at[slot], held.at[index], sems_in.at[index])
                copy.start()
                places.append((copy, target))
    sends = []
    for index, (copy, target) in enumerate(places):
        copy.wait()
        for piece, (start, stop) in enumerate(cuts):
            send = pltpu.make_async_copy(
                held.at[index, :, start:stop, :], outs[piece].at[target], sems_out.at[piece, index]
            )
            send.start()
            sends.append(send)
    for send in sends:
        send.wait()


def gather_pages(me, lists, kv_pages, capacity, cuts):
    low = len(lists)
    count = low * lists[0].shape[0] * capacity
    _, two, page_size, width = kv_pages.shape
    return pl.pallas_call(
        functools.partial(gather_kernel, capacity, cuts, low),
        out_shape=tuple(
            jax.ShapeDtypeStruct((count, two, stop - start, width), kv_pages.dtype)
            for start, stop in cuts
        ),
        in_specs=[SMEM] * (low + 1) + [HBM],
        out_specs=(HBM,) * len(cuts),
        scratch_shapes=[
            pltpu.VMEM((count, two, page_size, width), kv_pages.dtype),
            pltpu.SemaphoreType.DMA((count,)),
            pltpu.SemaphoreType.DMA((len(cuts), count)),
        ],
        compiler_params=params(60),
        cost_estimate=pl.CostEstimate(flops=0, bytes_accessed=8 * 2**20, transcendentals=0),
        name="gather_pages",
    )(me, *lists, kv_pages)


def silu(value):
    return value / (1.0 + jnp.exp(-value))


def front_kernel(
    core_ref, mine_ref, other_ref, gain_ref, cos_ref, sin_ref,
    histx_ref, histbc_ref, convx_ref, convbc_ref, bias_ref, rate_ref, skip_ref, mixer_gain_ref,
    wdt_hbm, wbc_hbm, wx_hbm, wz_hbm, wq_hbm, wk_hbm, wv_hbm, state_hbm,
    q_ref, k_ref, v_ref, gated_ref, square_ref, last_hbm,
    normed, wdt, wbc, wx, wz, wq, wkv, state_ref, last_ref, sems,
    x_ref, z_ref, bc_ref, padded, inner, cum, cum_t, step_size, b_ref, c_ref,
):
    copies = [
        pltpu.make_async_copy(source, target, sems.at[i])
        for i, (source, target) in enumerate(
            (
                (wdt_hbm, wdt),
                (wbc_hbm, wbc),
                (wx_hbm, wx),
                (wz_hbm, wz),
                (state_hbm, state_ref),
                (wq_hbm, wq),
                (wk_hbm, wkv.at[:, 0:HEAD_SIZE]),
                (wv_hbm, wkv.at[:, HEAD_SIZE : 2 * HEAD_SIZE]),
            )
        )
    ]
    for copy in copies:
        copy.start()

    rows, half = mine_ref.shape
    core = core_ref[0]
    here = pl.ds(pl.multiple_of(core * half, half), half)
    there = pl.ds(pl.multiple_of((1 - core) * half, half), half)
    step = 64

    def norm_rows(i, carry):
        block = pl.ds(pl.multiple_of(i * step, step), step)
        mine = mine_ref[block, :].astype(F32)
        other = other_ref[block, :].astype(F32)
        total = jnp.sum(mine * mine + other * other, axis=-1, keepdims=True)
        scale = lax.rsqrt(total / (2 * half) + EPSILON)
        normed[block, here] = (mine * scale * gain_ref[:, here]).astype(BF16)
        normed[block, there] = (other * scale * gain_ref[:, there]).astype(BF16)
        return carry

    lax.fori_loop(0, rows // step, norm_rows, 0)

    def dense(weight, target):
        for start in range(0, weight.shape[1], 256):
            tile = slice(start, start + 256)
            target[:, tile] = jnp.dot(
                normed[...], weight[:, tile], preferred_element_type=F32
            ).astype(BF16)

    copies[0].wait()
    raw = lax.dot_general(
        normed[...], wdt[...], (((1,), (1,)), ((), ())), preferred_element_type=F32
    ) + bias_ref[...]
    heads = raw.shape[1]
    copies[1].wait()
    dense(wbc, bc_ref)
    copies[2].wait()
    dense(wx, x_ref)
    copies[3].wait()
    dense(wz, z_ref)

    taps = convx_ref.shape[0]
    group = 2 * MP
    middle = rows // 2

    def conv(history, fresh, kernel):
        width = fresh.shape[1]
        padded[0:8, 0:width] = jnp.zeros((8, width), F32)
        padded[8 - (taps - 1) : 8, 0:width] = history.astype(F32)
        padded[8 : 8 + rows, 0:width] = fresh.astype(F32)
        summed = padded[9 - taps : 9 - taps + rows, 0:width] * kernel[0:1, :]
        for tap in range(1, taps):
            begin = 9 - taps + tap
            summed = summed + padded[begin : begin + rows, 0:width] * kernel[tap : tap + 1, :]
        return silu(summed).astype(BF16)

    for start in range(0, 2 * MN, group):
        part = conv(
            histbc_ref[0, :, start : start + group],
            bc_ref[:, start : start + group],
            convbc_ref[:, start : start + group],
        )
        if start < MN:
            b_ref[:, start : start + group] = part
        else:
            c_ref[:, start - MN : start - MN + group] = part

    size = jnp.maximum(raw, 0.0) + jnp.log1p(jnp.exp(-jnp.abs(raw)))
    step_size[:, 0:heads] = size
    row_index = lax.broadcasted_iota(jnp.int32, (rows, rows), 0)
    column_index = lax.broadcasted_iota(jnp.int32, (rows, rows), 1)
    causal = column_index <= row_index
    cum[...] = jnp.zeros((rows, 128), F32)
    cum[:, 0:heads] = -size * (rate_ref[...] * LOG2E)
    cum[...] = jnp.dot(
        causal.astype(F32), cum[...], precision=lax.Precision.HIGHEST, preferred_element_type=F32
    )
    cum_t[...] = cum[...].T
    inner[...] = jnp.where(
        causal,
        lax.dot_general(c_ref[...], b_ref[...], CONTRACT_LAST, preferred_element_type=F32),
        0.0,
    )
    copies[4].wait()
    first = lax.broadcasted_iota(jnp.int32, (1, group), 1) < MP
    first_rows = lax.broadcasted_iota(jnp.int32, (group, 1), 0) < MP
    squares = jnp.zeros((rows, group), F32)
    for pair in range(heads // 2):
        cols = slice(pair * group, (pair + 1) * group)
        one, two = 2 * pair, 2 * pair + 1
        x_rows = conv(histx_ref[0, :, cols], x_ref[:, cols], convx_ref[:, cols]).astype(F32)
        sizes = jnp.where(first, step_size[:, one : one + 1], step_size[:, two : two + 1])
        fades = jnp.where(first, cum[:, one : one + 1], cum[:, two : two + 1])
        last_fade = fades[rows - 1 : rows, :]
        moved_float = x_rows * sizes
        moved = moved_float.astype(BF16)
        tail_moved = moved_float * jnp.exp2(last_fade - fades)
        state = state_ref[cols, :]
        state_high = state.astype(BF16)
        state_low = (state - state_high.astype(F32)).astype(BF16)
        carried = lax.dot_general(
            c_ref[...], state_high, CONTRACT_LAST, preferred_element_type=F32
        ) + lax.dot_general(c_ref[...], state_low, CONTRACT_LAST, preferred_element_type=F32)
        blocks = []
        for begin in (0, middle):
            end = begin + middle
            sides = []
            for head in (one, two):
                gap = cum[begin:end, head : head + 1] - cum_t[head : head + 1, 0:end]
                mixing = (jnp.exp2(jnp.minimum(gap, 0.0)) * inner[begin:end, 0:end]).astype(BF16)
                sides.append(jnp.dot(mixing, moved[0:end, :], preferred_element_type=F32))
            blocks.append(jnp.where(first, sides[0], sides[1]))
        ssm_y = (
            jnp.concatenate(blocks, axis=0)
            + carried * jnp.exp2(fades)
            + skip_ref[:, cols] * x_rows
        )
        gated = ssm_y * silu(z_ref[:, cols].astype(F32))
        squares = squares + gated * gated
        gated_ref[:, cols] = (gated * mixer_gain_ref[:, cols]).astype(BF16)
        added = jnp.dot(tail_moved.T.astype(BF16), b_ref[...], preferred_element_type=F32)
        ends = jnp.exp2(cum_t[one : two + 1, rows - 1 : rows])
        keep = jnp.where(first_rows, ends[0:1, :], ends[1:2, :])
        last_ref[cols, :] = keep * state + added
    square_ref[...] = jnp.sum(squares.T, axis=0, keepdims=True)
    give_back = pltpu.make_async_copy(last_ref, last_hbm, sems.at[8])
    give_back.start()

    def rope(vectors):
        return vectors * cos_ref[...] + pltpu.roll(vectors, HEAD_SIZE // 2, 1) * sin_ref[...]

    copies[5].wait()
    for tile in range(wq.shape[1] // 256):
        two_heads = jnp.dot(
            normed[...], wq[:, tile * 256 : tile * 256 + 256], preferred_element_type=F32
        )
        for side in range(2):
            head = 2 * tile + side
            q_ref[head * rows : (head + 1) * rows, :] = rope(
                two_heads[:, side * HEAD_SIZE : (side + 1) * HEAD_SIZE]
            ).astype(BF16)
    copies[6].wait()
    copies[7].wait()
    key_value = jnp.dot(normed[...], wkv[...], preferred_element_type=F32)
    k_ref[...] = rope(key_value[:, :HEAD_SIZE]).astype(BF16)
    v_ref[...] = key_value[:, HEAD_SIZE:].astype(BF16)
    give_back.wait()


def front(
    core, mine, other, gain, cosine, sine,
    histx, histbc, convx, convbc, bias, rate, skip, mixer_gain,
    wdt, wbc, wx, wz, wq, wk, wv, state,
):
    rows, half = mine.shape
    width = 2 * half

    def out(shape, dtype=BF16):
        return jax.ShapeDtypeStruct(shape, dtype)

    return pl.pallas_call(
        front_kernel,
        out_shape=(
            out((wq.shape[1] // HEAD_SIZE * rows, HEAD_SIZE)),
            out((rows, wk.shape[1])),
            out((rows, wv.shape[1])),
            out((rows, wx.shape[1])),
            out((1, rows), F32),
            out(state.shape, F32),
        ),
        in_specs=[SMEM] + [VMEM] * 13 + [HBM] * 8,
        out_specs=(VMEM,) * 5 + (HBM,),
        scratch_shapes=[
            pltpu.VMEM((rows, width), BF16),
            pltpu.VMEM(wdt.shape, BF16),
            pltpu.VMEM(wbc.shape, BF16),
            pltpu.VMEM(wx.shape, BF16),
            pltpu.VMEM(wz.shape, BF16),
            pltpu.VMEM(wq.shape, BF16),
            pltpu.VMEM((width, 2 * HEAD_SIZE), BF16),
            pltpu.VMEM(state.shape, F32),
            pltpu.VMEM(state.shape, F32),
            pltpu.SemaphoreType.DMA((9,)),
            pltpu.VMEM((rows, wx.shape[1]), BF16),
            pltpu.VMEM((rows, wz.shape[1]), BF16),
            pltpu.VMEM((rows, wbc.shape[1]), BF16),
            pltpu.VMEM((rows + 8, 2 * MP), F32),
            pltpu.VMEM((rows, rows), F32),
            pltpu.VMEM((rows, 128), F32),
            pltpu.VMEM((128, rows), F32),
            pltpu.VMEM((rows, 128), F32),
            pltpu.VMEM((rows, MN), BF16),
            pltpu.VMEM((rows, MN), BF16),
        ],
        compiler_params=params(32),
        cost_estimate=pl.CostEstimate(
            flops=16 * 10**9, bytes_accessed=17 * 2**20, transcendentals=4 * 10**6
        ),
        name="front",
    )(
        core, mine, other, gain, cosine, sine,
        histx, histbc, convx, convbc, bias, rate, skip, mixer_gain,
        wdt, wbc, wx, wz, wq, wk, wv, state,
    )


CONTRACT_LAST = (((1,), (1,)), ((), ()))
CHUNK = 512


def across(column, width):
    return jnp.concatenate([column] * (width // HEAD_SIZE), axis=1)


def softmax_step(scores, values, state):
    count = scores.shape[1]
    top = jnp.broadcast_to(jnp.max(scores, axis=-1, keepdims=True), (scores.shape[0], HEAD_SIZE))
    if state is not None:
        top = jnp.maximum(state[2], top)
    weights = jnp.exp2((scores - across(top, count)) * SCORE_SCALE).astype(BF16)
    values = jnp.concatenate([values, jnp.ones((count, HEAD_SIZE), BF16)], axis=1)
    added = jnp.dot(weights, values, preferred_element_type=F32)
    summed, total = added[:, :HEAD_SIZE], added[:, HEAD_SIZE:]
    if state is not None:
        fade = jnp.exp2((state[2] - top) * SCORE_SCALE)
        summed, total = state[0] * fade + summed, state[1] * fade + total
    return summed, total, top


def page_step(query, keys, values, seen, state):
    pages, tokens, width = keys.shape
    scores = lax.dot_general(
        query, keys.reshape(pages * tokens, width), CONTRACT_LAST, preferred_element_type=F32
    )
    token = lax.broadcasted_iota(jnp.int32, (1, tokens), 1)
    hide = jnp.concatenate(
        [jnp.where(token >= seen[page], NEG_FILL, 0.0) for page in range(pages)], axis=1
    )
    return softmax_step(scores + hide, values.reshape(pages * tokens, width), state)


def attend_new_kernel(q_ref, k_ref, v_ref, sum_ref, total_ref, top_ref):
    rows = k_ref.shape[0]
    row = lax.broadcasted_iota(jnp.int32, (rows, rows), 0)
    column = lax.broadcasted_iota(jnp.int32, (rows, rows), 1)
    for start in range(0, q_ref.shape[0], rows):
        here = slice(start, start + rows)
        scores = lax.dot_general(
            q_ref[here, :], k_ref[...], CONTRACT_LAST, preferred_element_type=F32
        )
        scores = jnp.where(column <= row, scores, NEG_FILL)
        sum_ref[here, :], total_ref[here, :], top_ref[here, :] = softmax_step(
            scores, v_ref[...], None
        )


def attend_new(queries, keys, values):
    count = queries.shape[0]
    rows = keys.shape[0]
    return pl.pallas_call(
        attend_new_kernel,
        out_shape=(jax.ShapeDtypeStruct((count, HEAD_SIZE), F32),) * 3,
        in_specs=[VMEM] * 3,
        out_specs=(VMEM,) * 3,
        compiler_params=params(16),
        cost_estimate=pl.CostEstimate(
            flops=8 * count * rows * HEAD_SIZE,
            bytes_accessed=4 * 2**20,
            transcendentals=count * rows,
        ),
        name="attend_new",
    )(queries, keys, values)


def attend_pages_kernel(seen_ref, q_ref, sum_ref, total_ref, top_ref, kv_hbm, out_ref, kv_ref, sems):
    pages, _, tokens, _ = kv_ref.shape
    rows = out_ref.shape[0]
    per_chunk = CHUNK // tokens
    spans = [slice(start, start + per_chunk) for start in range(0, pages, per_chunk)]
    copies = [
        pltpu.make_async_copy(kv_hbm.at[span], kv_ref.at[span], sems.at[i])
        for i, span in enumerate(spans)
    ]
    for copy in copies:
        copy.start()
    for head in range(q_ref.shape[0] // rows):
        here = slice(head * rows, (head + 1) * rows)
        query = q_ref[here, :]
        state = (sum_ref[here, :], total_ref[here, :], top_ref[here, :])
        for span, copy in zip(spans, copies):
            if head == 0:
                copy.wait()
            seen = [seen_ref[page] for page in range(span.start, span.stop)]
            state = page_step(query, kv_ref[span, 0], kv_ref[span, 1], seen, state)
        out_ref[:, head * HEAD_SIZE : (head + 1) * HEAD_SIZE] = (state[0] / state[1]).astype(BF16)


def attend_pages(seen, queries, state, kv, rows):
    pages, _, tokens, _ = kv.shape
    count = queries.shape[0]
    return pl.pallas_call(
        attend_pages_kernel,
        out_shape=jax.ShapeDtypeStruct((rows, count // rows * HEAD_SIZE), BF16),
        in_specs=[SMEM] + [VMEM] * 4 + [HBM],
        out_specs=VMEM,
        scratch_shapes=[
            pltpu.VMEM(kv.shape, kv.dtype),
            pltpu.SemaphoreType.DMA((pages * tokens // CHUNK,)),
        ],
        compiler_params=params(16),
        cost_estimate=pl.CostEstimate(
            flops=8 * count * pages * tokens * HEAD_SIZE,
            bytes_accessed=4 * 2**20,
            transcendentals=count * pages * tokens,
        ),
        name="attend_pages",
    )(seen, queries, *state, kv)


def mixer_out_kernel(gated_ref, scale_ref, weight_ref, out_ref):
    for start in range(0, out_ref.shape[1], 256):
        tile = slice(start, start + 256)
        out_ref[:, tile] = (
            jnp.dot(gated_ref[...], weight_ref[:, tile], preferred_element_type=F32)
            * scale_ref[...]
        )


def mixer_out(gated, scale, weight):
    rows, depth = gated.shape
    width = weight.shape[1]
    return pl.pallas_call(
        mixer_out_kernel,
        out_shape=jax.ShapeDtypeStruct((rows, width), F32),
        in_specs=[VMEM] * 3,
        out_specs=VMEM,
        compiler_params=params(16),
        cost_estimate=pl.CostEstimate(
            flops=2 * rows * depth * width, bytes_accessed=8 * 2**20, transcendentals=0
        ),
        name="mixer_out",
    )(gated, scale, weight)


def attn_out_kernel(core_ref, context_ref, weight_ref, part_ref, out_ref):
    half = out_ref.shape[1]
    for start in range(0, half, 256):
        here = pl.ds(pl.multiple_of(core_ref[0] * half + start, 256), 256)
        out_ref[:, start : start + 256] = (
            jnp.dot(context_ref[...], weight_ref[:, here], preferred_element_type=F32)
            + part_ref[:, here]
        ).astype(out_ref.dtype)


def attn_out(core, context, weight, part, dtype):
    rows, depth = context.shape
    half = weight.shape[1] // 2
    return pl.pallas_call(
        attn_out_kernel,
        out_shape=jax.ShapeDtypeStruct((rows, half), dtype),
        in_specs=[SMEM] + [VMEM] * 3,
        out_specs=VMEM,
        compiler_params=params(16),
        cost_estimate=pl.CostEstimate(
            flops=2 * rows * depth * half, bytes_accessed=4 * 2**20, transcendentals=0
        ),
        name="attn_out",
    )(core, context, weight, part)


def shards(
    tokens,
    attn_gain,
    w_query,
    key_weight,
    value_weight,
    w_attn_out,
    kv_pages,
    page_table,
    cached_len,
    w_gate_z,
    w_ssm_in,
    w_bc,
    w_dt,
    conv_w_x,
    conv_w_bc,
    conv_x_state,
    conv_bc_state,
    dt_bias,
    decay_rate,
    skip_gain,
    mixer_gain,
    w_mixer_out,
    ssm_state,
):
    swap = [(0, 1), (1, 0)]
    core = lax.axis_index("tp").astype(jnp.int32).reshape(1)
    row_count = tokens.shape[0]
    devices = lax.axis_size("req")
    pages_dev = kv_pages.shape[0]
    capacity = pages_dev // devices
    page_size = kv_pages.shape[3]
    length = cached_len[0]

    want, seen = wanted(page_table, cached_len, devices, pages_dev, page_size)
    cosine, sine = rope_tables(length + jnp.arange(row_count, dtype=jnp.int32))
    other = lax.ppermute(tokens, "tp", swap)
    lists = share_wants(want, "req", devices)
    me = lax.axis_index("req").astype(jnp.int32).reshape(1)
    cuts = ((0, page_size),)
    fetched = gather_pages(
        me, lists, kv_pages.reshape((pages_dev, 2, page_size, HEAD_SIZE)), capacity, cuts
    )

    arrived = lax.all_to_all(
        fetched[0].reshape((devices, capacity) + fetched[0].shape[1:]),
        "req",
        split_axis=0,
        concat_axis=0,
        tiled=True,
    ).reshape(fetched[0].shape)

    heads = w_dt.shape[1]
    queries, fresh_keys, fresh_values, gated, squares, last_state = front(
        core, tokens, other, attn_gain[None, :], cosine, sine,
        conv_x_state, conv_bc_state, conv_w_x, conv_w_bc,
        dt_bias[None, :], decay_rate[None, :], jnp.repeat(skip_gain, MP)[None, :],
        mixer_gain[None, :],
        w_dt.T, w_bc, w_ssm_in, w_gate_z, w_query, key_weight, value_weight,
        ssm_state.reshape((heads * MP, MN)),
    )
    total = squares + lax.ppermute(squares, "tp", swap)
    scale = lax.rsqrt(total.reshape((row_count, 1)) / DSSM + EPSILON)
    part = mixer_out(gated, scale, w_mixer_out)
    state = attend_new(queries, fresh_keys, fresh_values)
    context = attend_pages(seen, queries, state, arrived, row_count)
    theirs = attn_out(1 - core, context, w_attn_out, part, BF16)
    ours = attn_out(core, context, w_attn_out, part, F32)
    received = lax.ppermute(theirs, "tp", swap)
    mixed = (ours + received.astype(F32)).astype(BF16)
    return (mixed, last_state.reshape(ssm_state.shape))


def solution(mesh):
    return jax.shard_map(
        shards,
        mesh=mesh,
        in_specs=(
            P("req", "tp"),
            P(),
            P(None, "tp"),
            P(None, "tp"),
            P(None, "tp"),
            P("tp", None),
            P("req", None, "tp", None, None),
            P("req", None),
            P("req"),
            P(None, "tp"),
            P(None, "tp"),
            P(),
            P(None, "tp"),
            P(None, "tp"),
            P(),
            P("req", None, "tp"),
            P("req", None, None),
            P("tp"),
            P("tp"),
            P("tp"),
            P("tp"),
            P("tp", None),
            P("req", "tp", None, None),
        ),
        out_specs=(P("req", "tp"), P("req", "tp", None, None)),
        check_vma=False,
    )
```

time: 168 us -> 99.6 us (0.59)
  Pallas kernels: 126 us -> 45.8 us
  local copies, waits for them, and re-layouts: 6.53 us -> 19.6 us
  blocking collectives: 10.6 us -> 0 us
  starting transfers between devices: 9.68 us -> 18.7 us
  other arithmetic: 7.99 us -> 3.24 us
  waiting for transfers between devices: 5.53 us -> 9.96 us
    pallas_call x6 -> x7, Pallas kernels: 118 us -> 44 us  [the longest x1 19.4 us: front(): pl.pallas_call(front_kernel, out_shape=(out((wq.shape[1] // HEAD_SIZE * r...]
    unnamed x11 -> x74, local copies, waits for them, and re-layouts: 2.39 us -> 19.3 us
    all_to_all x1 -> x0, blocking collectives: 10.6 us -> none  [shards(): lax.all_to_all(want_slot, 'req', split_axis=0, concat_axis=0, tiled=True)]
    pallas_call x1, Pallas kernels: 8.11 us -> 1.82 us  [mixer_out(): pl.pallas_call(mixer_out_kernel, out_shape=jax.ShapeDtypeStruct((rows, wi...]
    ppermute x0 -> x6, starting transfers between devices: none -> 6.27 us  [swapped(): return lax.ppermute(rows, axis, [(i, i ^ mask) for i in range(devices)])]
    ppermute x0 -> x6, waiting for transfers between devices: none -> 3.59 us  [swapped(): return lax.ppermute(rows, axis, [(i, i ^ mask) for i in range(devices)])]
    ppermute x1, starting transfers between devices: 2.45 us -> 4.41 us  [shards(): other = lax.ppermute(tokens, 'tp', swap)]
  transfers between devices with their start and end apart: 4 -> 10, of which waited for: 2 -> 8; matrix products, arithmetic and copies ran while one was open for 4% -> 2% of each run, Pallas kernels for 22% -> 24%
where the time goes in v2:
time: 99.6 us; the launch traced here: 98.9 us
  Pallas kernels  45.8 us (46%)
  local copies, waits for them, and re-layouts  19.6 us (20%)
  starting transfers between devices  18.7 us (19%)
  waiting for transfers between devices  9.96 us (10%)
  other arithmetic  3.24 us (3%)
  between operations  1.63 us (2%)
    pallas_call x1, Pallas kernels, front(): pl.pallas_call(front_kernel, out_shape=(out((wq.shape[1] // HEAD_SIZE * r...  19.4 us
    unnamed x74, local copies, waits for them, and re-layouts  19.3 us
    pallas_call x1, Pallas kernels, attend_pages(): pl.pallas_call(attend_pages_kernel, out_shape=jax.ShapeDtypeStruct((rows,...  15.3 us
    ppermute x6, starting transfers between devices, swapped(): return lax.ppermute(rows, axis, [(i, i ^ mask) for i in range(devices)])  6.27 us
    all_to_all x1, starting transfers between devices, shards(): lax.all_to_all(fetched[0].reshape((devices, capacity) + fetched[0].shape[...  6.01 us
    pallas_call x1, Pallas kernels, gather_pages(): pl.pallas_call(functools.partial(gather_kernel, capacity, cuts, low), out...  4.55 us
    ppermute x1, starting transfers between devices, shards(): other = lax.ppermute(tokens, 'tp', swap)  4.41 us
    ppermute x6, waiting for transfers between devices, swapped(): return lax.ppermute(rows, axis, [(i, i ^ mask) for i in range(devices)])  3.59 us
  transfers between devices with their start and end apart: 10, of which 8 were waited for; matrix products, arithmetic and copies ran while one was open for 2% of the time, Pallas kernels for 24%

profile of v2, /device:TPU:13, one launch (start us, length us, event | category | flops | bytes accessed | tf_op | source)
XLA Modules:
  0.0 98.9 jit_solution(15616469542337037180)
XLA Ops:
  1.3 1.5 %wanted.1 = (s32[1,32]{1,0:T(1,128)}, s32[32]{0:T(128)}) custom-call(s32[1,32]{1,0:T(1,128)} %table_ref.1, s32[1]{0:T(128)} %copy.26.length_ref), custom_call_target="tpu_custom_call" | custom-call | tf_op jit(solution)/shard_map/wanted/pallas_call | solution.py:61
  2.8 1.4 %collective-permute-start.3 = (s32[1,32]{1,0:T(1,128)}, s32[1,32]{1,0:T(1,128)S(1)}, u32[]{:S(2)}, u32[]{:S(2)}) collective-permute-start(s32[1,32]{1,0:T(1,128)} %get-tuple-element.20), channel_id=1, source_target_pairs={{0,24},{2,26},{4,28},{6,30},{8,16},{10,18},{12,20},{14,22},{16,8},... | collective-permute-start | bytes 392 | tf_op jit(solution)/shard_map/ppermute | solution.py:78
  6.4 1.2 %collective-permute-done.2 = s32[1,32]{1,0:T(1,128)S(1)} collective-permute-done((s32[1,32]{1,0:T(1,128)}, s32[1,32]{1,0:T(1,128)S(1)}, u32[]{:S(2)}, u32[]{:S(2)}) %collective-permute-start.2) | collective-permute-done | bytes 160 | tf_op jit(solution)/shard_map/ppermute | solution.py:78
  9.7 1.2 %collective-permute-start.5 = (s32[4,32]{1,0:T(4,128)S(1)}, s32[4,32]{1,0:T(4,128)S(1)}, u32[]{:S(2)}, u32[]{:S(2)}) collective-permute-start(s32[4,32]{1,0:T(4,128)S(1)} %pad_add_fusion.refs_0_), channel_id=1, source_target_pairs={{0,4},{2,6},{4,0},{6,2},{8,12},{10,14},{12,8},{14,10},{16,20},{18,... | collective-permute-start | bytes 1544 | tf_op jit(solution)/shard_map/ppermute | solution.py:78
  12.1 1.2 %collective-permute-done.4.refs_1_ = s32[4,32]{1,0:T(4,128)S(1)} collective-permute-done((s32[4,32]{1,0:T(4,128)S(1)}, s32[4,32]{1,0:T(4,128)S(1)}, u32[]{:S(2)}, u32[]{:S(2)}) %collective-permute-start.4) | collective-permute-done | bytes 544 | tf_op jit(solution)/shard_map/ppermute | solution.py:78
  13.9 4.5 %gather_pages.1 = bf16[32,2,128,128]{3,2,1,0:T(8,128)(2,1)} custom-call(s32[1]{0:T(128)} %bitcast.7.me_ref, s32[4,32]{1,0:T(4,128)} %copy-done.31, s32[4,32]{1,0:T(4,128)} %copy-done.35, s32[4,32]{1,0:T(4,128)} %copy-done.34, s32[4,32]{1,0:T(4,128)} %copy-done.33, bf16[32,2,128,128]{3,2,1,0:T(8,128)(2,1)} %bitcast.21), custom_call_target="tpu_custom_call" | custom-call | bytes 8388608 | tf_op jit(solution)/shard_map/gather_pages/pallas_call | solution.py:118
  18.5 6.0 %all-to-all-start = ((bf16[16,2,2,128,128]{4,3,2,1,0:T(8,128)(2,1)}), bf16[16,2,2,128,128]{4,3,2,1,0:T(8,128)(2,1)}, u32[]{:S(2)}, u32[]{:S(2)}) async-start(bf16[16,2,2,128,128]{4,3,2,1,0:T(8,128)(2,1)} %bitcast.20), calls=%async_computation | async-start | bytes 4194304 | tf_op jit(solution)/shard_map/all_to_all | solution.py:577
  24.6 4.4 %collective-permute-start = (bf16[512,1024]{1,0:T(8,128)(2,1)}, bf16[512,1024]{1,0:T(8,128)(2,1)}, u32[]{:S(2)}, u32[]{:S(2)}) collective-permute-start(bf16[512,1024]{1,0:T(8,128)(2,1)} %mine_ref.1), channel_id=1, source_target_pairs={{0,1},{1,0},{2,3},{3,2},{4,5},{5,4},{6,7},{7,6},{8,9},{9,8},{10,11... | collective-permute-start | bytes 3145736 | tf_op jit(solution)/shard_map/ppermute | solution.py:569
  30.4 1.2 %collective-permute-done.other_ref = bf16[512,1024]{1,0:T(8,128)(2,1)} collective-permute-done((bf16[512,1024]{1,0:T(8,128)(2,1)}, bf16[512,1024]{1,0:T(8,128)(2,1)}, u32[]{:S(2)}, u32[]{:S(2)}) %collective-permute-start) | collective-permute-done | bytes 1048608 | tf_op jit(solution)/shard_map/ppermute | solution.py:569
  31.7 1.9 %copy-done.7 = bf16[2048,768]{1,0:T(8,128)(2,1)S(1)} copy-done((bf16[2048,768]{1,0:T(8,128)(2,1)S(1)}, bf16[2048,768]{1,0:T(8,128)(2,1)}, u32[]{:S(2)}) %copy-start.7) | copy-done | bytes 3145752
  33.6 1.6 %copy-done.9 = bf16[2048,512]{1,0:T(8,128)(2,1)S(1)} copy-done((bf16[2048,512]{1,0:T(8,128)(2,1)S(1)}, bf16[2048,512]{1,0:T(8,128)(2,1)}, u32[]{:S(2)}) %copy-start.9) | copy-done | bytes 2097176
  35.2 1.2 %copy-done.10 = bf16[512,1024]{1,0:T(8,128)(2,1)S(1)} copy-done((bf16[512,1024]{1,0:T(8,128)(2,1)S(1)}, bf16[512,1024]{1,0:T(8,128)(2,1)}, u32[]{:S(2)}) %copy-start.10) | copy-done | bytes 1048600
  39.7 19.4 %front.1 = (bf16[2048,128]{1,0:T(8,128)(2,1)S(1)}, bf16[512,128]{1,0:T(8,128)(2,1)S(1)}, bf16[512,128]{1,0:T(8,128)(2,1)S(1)}, bf16[512,768]{1,0:T(8,128)(2,1)S(...) custom-call(s32[1]{0:T(128)} %bitcast.core_ref, bf16[512,1024]{1,0:T(8,128)(2,1)S(1)} %copy-done.10, ...), custom_call_target="tpu_custom_call" | custom-call | flops 16000000000 | bytes 17825792 | tf_op jit(solution)/shard_map/front/pallas_call | solution.py:323
  59.5 1.8 %attend_new.1 = (f32[2048,128]{1,0:T(8,128)S(1)}, f32[2048,128]{1,0:T(8,128)S(1)}, f32[2048,128]{1,0:T(8,128)S(1)}) custom-call(bf16[2048,128]{1,0:T(8,128)(2,1)S(1)} %get-tuple-element.14.q_ref, bf16[512,128]{1,0:T(8,128)(2,1)S(1)} %get-tuple-element.15.k_ref, bf16[512,128]{1,0:T(8,128)(2,1)S(1)} %get-tuple-element.16.v_ref), custom_call_target="tpu_custom_call" | custom-call | flops 1073741824 | bytes 4194304 | tf_op jit(solution)/shard_map/attend_new/pallas_call | solution.py:422
  65.6 1.8 %mixer_out.1.part_ref = f32[512,2048]{1,0:T(8,128)S(1)} custom-call(bf16[512,768]{1,0:T(8,128)(2,1)S(1)} %copy-done.5, f32[512,1]{1,0:T(8,128)S(1)} %copy.25.scale_ref, bf16[768,2048]{1,0:T(8,128)(2,1)S(1)} %copy-done.3), custom_call_target="tpu_custom_call" | custom-call | flops 1610612736 | bytes 8388608 | tf_op jit(solution)/shard_map/mixer_out/pallas_call | solution.py:494
  67.4 2.0 %copy-done = f32[512,2048]{1,0:T(8,128)} copy-done((f32[512,2048]{1,0:T(8,128)}, f32[512,2048]{1,0:T(8,128)S(1)}, u32[]{:S(2)}) %copy-start) | copy-done | bytes 4194328
  69.4 3.6 %all-to-all-done = bf16[16,2,2,128,128]{4,3,2,1,0:T(8,128)(2,1)} async-done(((bf16[16,2,2,128,128]{4,3,2,1,0:T(8,128)(2,1)}), bf16[16,2,2,128,128]{4,3,2,1,0:T(8,128)(2,1)}, u32[]{:S(2)}, u32[]{:S(2)}) %all-to-all-start) | async-done | bytes 2097184 | tf_op jit(solution)/shard_map/all_to_all | solution.py:577
  72.9 1.2 %copy-done.24 = f32[2048,128]{1,0:T(8,128)S(1)} copy-done((f32[2048,128]{1,0:T(8,128)S(1)}, f32[2048,128]{1,0:T(8,128)}, u32[]{:S(2)}) %copy-start.24) | copy-done | bytes 1048600
  74.2 1.2 %copy-done.26 = f32[2048,128]{1,0:T(8,128)S(1)} copy-done((f32[2048,128]{1,0:T(8,128)S(1)}, f32[2048,128]{1,0:T(8,128)}, u32[]{:S(2)}) %copy-start.26) | copy-done | bytes 1048600
  75.4 1.2 %copy-done.28 = f32[2048,128]{1,0:T(8,128)S(1)} copy-done((f32[2048,128]{1,0:T(8,128)S(1)}, f32[2048,128]{1,0:T(8,128)}, u32[]{:S(2)}) %copy-start.28) | copy-done | bytes 1048600
  77.7 15.3 %attend_pages.1.context_ref = bf16[512,512]{1,0:T(8,128)(2,1)S(1)} custom-call(s32[32]{0:T(128)S(1)} %copy-done.22, bf16[2048,128]{1,0:T(8,128)(2,1)S(1)} %copy-done.30, f32[2048,128]{1,0:T(8,128)S(1)} %copy-done.24, f32[2048,128]{1,0:T(8,128)S(1)} %copy-done.26, f32[2048,128]{1,0:T(8,128)S(1)} %copy-done.28, bf16[32,2,128,128]{3,2,1,0:T(8,128)(2,1)} %bitcast.10.kv_hbm), custom_call_target="tpu_custom_call" | custom-call | flops 8589934592 | bytes 4194304 | tf_op jit(solution)/shard_map/attend_pages/pallas_call | solution.py:463
  93.7 1.6 %collective-permute-start.8 = (bf16[512,1024]{1,0:T(8,128)(2,1)S(1)}, bf16[512,1024]{1,0:T(8,128)(2,1)S(1)}, u32[]{:S(2)}, u32[]{:S(2)}) collective-permute-start(bf16[512,1024]{1,0:T(8,128)(2,1)S(1)} %attn_out.3), channel_id=1, source_target_pairs={{0,1},{1,0},{2,3},{3,2},{4,5},{5,4},{6,7},{7,6},{8,9},{9,8},{10,11... | collective-permute-start | bytes 3145736 | tf_op jit(solution)/shard_map/ppermute | solution.py:601
  96.0 1.6 %collective-permute-done.8 = bf16[512,1024]{1,0:T(8,128)(2,1)S(1)} collective-permute-done((bf16[512,1024]{1,0:T(8,128)(2,1)S(1)}, bf16[512,1024]{1,0:T(8,128)(2,1)S(1)}, u32[]{:S(2)}, u32[]{:S(2)}) %collective-permute-start.8) | collective-permute-done | bytes 1048608 | tf_op jit(solution)/shard_map/ppermute | solution.py:601
  97.5 1.4 %add_convert_fusion = bf16[512,1024]{1,0:T(8,128)(2,1)} fusion(f32[512,1024]{1,0:T(8,128)S(1)} %attn_out.2, bf16[512,1024]{1,0:T(8,128)(2,1)S(1)} %collective-permute-done.8), kind=kLoop, calls=%fused_computation | loop fusion | flops 1572864 | bytes 4194304 | tf_op jit(solution)/shard_map/convert_element_type | solution.py:602
  (89 shorter events, 17.9 us)
Async XLA Ops:
  2.8 3.6 %collective-permute-start.3 = (s32[1,32]{1,0:T(1,128)}, s32[1,32]{1,0:T(1,128)S(1)}, u32[]{:S(2)}, u32[]{:S(2)}) collective-permute-start(s32[1,32]{1,0:T(1,128)} %get-tuple-element.20), channel_id=1, source_target_pairs={{0,24},{2,26},{4,28},{6,30},{8,16},{10,18},{12,20},{14,22},{16,8},... | collective-permute-start | bytes 392 | tf_op jit(solution)/shard_map/ppermute | solution.py:78
  4.2 3.4 %collective-permute-start.2 = (s32[1,32]{1,0:T(1,128)}, s32[1,32]{1,0:T(1,128)S(1)}, u32[]{:S(2)}, u32[]{:S(2)}) collective-permute-start(s32[1,32]{1,0:T(1,128)} %get-tuple-element.20), channel_id=1, source_target_pairs={{0,16},{2,18},{4,20},{6,22},{8,24},{10,26},{12,28},{14,30},{16,0},... | collective-permute-start | bytes 392 | tf_op jit(solution)/shard_map/ppermute | solution.py:78
  5.2 2.5 %collective-permute-start.1 = (s32[1,32]{1,0:T(1,128)}, s32[1,32]{1,0:T(1,128)S(1)}, u32[]{:S(2)}, u32[]{:S(2)}) collective-permute-start(s32[1,32]{1,0:T(1,128)} %get-tuple-element.20), channel_id=1, source_target_pairs={{0,8},{2,10},{4,12},{6,14},{8,0},{10,2},{12,4},{14,6},{16,24},{18,... | collective-permute-start | bytes 392 | tf_op jit(solution)/shard_map/ppermute | solution.py:78
  8.4 3.4 %collective-permute-start.6 = (s32[4,32]{1,0:T(4,128)S(1)}, s32[4,32]{1,0:T(4,128)S(1)}, u32[]{:S(2)}, u32[]{:S(2)}) collective-permute-start(s32[4,32]{1,0:T(4,128)S(1)} %pad_add_fusion.refs_0_), channel_id=1, source_target_pairs={{0,6},{2,4},{4,2},{6,0},{8,14},{10,12},{12,10},{14,8},{16,22},{18,... | collective-permute-start | bytes 1544 | tf_op jit(solution)/shard_map/ppermute | solution.py:78
  9.7 2.4 %collective-permute-start.5 = (s32[4,32]{1,0:T(4,128)S(1)}, s32[4,32]{1,0:T(4,128)S(1)}, u32[]{:S(2)}, u32[]{:S(2)}) collective-permute-start(s32[4,32]{1,0:T(4,128)S(1)} %pad_add_fusion.refs_0_), channel_id=1, source_target_pairs={{0,4},{2,6},{4,0},{6,2},{8,12},{10,14},{12,8},{14,10},{16,20},{18,... | collective-permute-start | bytes 1544 | tf_op jit(solution)/shard_map/ppermute | solution.py:78
  10.9 2.4 %collective-permute-start.4 = (s32[4,32]{1,0:T(4,128)S(1)}, s32[4,32]{1,0:T(4,128)S(1)}, u32[]{:S(2)}, u32[]{:S(2)}) collective-permute-start(s32[4,32]{1,0:T(4,128)S(1)} %pad_add_fusion.refs_0_), channel_id=1, source_target_pairs={{0,2},{2,0},{4,6},{6,4},{8,10},{10,8},{12,14},{14,12},{16,18},{18,... | collective-permute-start | bytes 1544 | tf_op jit(solution)/shard_map/ppermute | solution.py:78
  18.5 10.6 %copy-start.32 = (f32[768]{0:T(1024)S(1)}, f32[768]{0:T(1024)}, u32[]{:S(2)}) copy-start(f32[768]{0:T(1024)} %param.43) | copy-start | bytes 9220
  18.5 10.6 %copy-start.36 = (f32[12]{0:T(128)S(1)}, f32[12]{0:T(128)}, u32[]{:S(2)}) copy-start(f32[12]{0:T(128)} %param.42) | copy-start | bytes 148
  18.5 13.2 %copy-start.6 = (bf16[2048,768]{1,0:T(8,128)(2,1)S(1)}, bf16[2048,768]{1,0:T(8,128)(2,1)}, u32[]{:S(2)}) copy-start(bf16[2048,768]{1,0:T(8,128)(2,1)} %wx_hbm.1) | copy-start | bytes 9437188
  18.5 13.2 %copy-start.14 = (bf16[2048,12]{0,1:T(8,128)(2,1)S(1)}, bf16[2048,12]{0,1:T(8,128)(2,1)}, u32[]{:S(2)}) copy-start(bf16[2048,12]{0,1:T(8,128)(2,1)} %param.35) | copy-start | bytes 147460
  18.5 54.4 %all-to-all-start = ((bf16[16,2,2,128,128]{4,3,2,1,0:T(8,128)(2,1)}), bf16[16,2,2,128,128]{4,3,2,1,0:T(8,128)(2,1)}, u32[]{:S(2)}, u32[]{:S(2)}) async-start(bf16[16,2,2,128,128]{4,3,2,1,0:T(8,128)(2,1)} %bitcast.20), calls=%async_computation | async-start | bytes 4194304 | tf_op jit(solution)/shard_map/all_to_all | solution.py:577
  24.5 7.1 %copy-start.15 = (f32[4,768]{1,0:T(4,128)S(1)}, f32[4,768]{1,0:T(4,128)}, u32[]{:S(2)}) copy-start(f32[4,768]{1,0:T(4,128)} %convx_ref.1) | copy-start | bytes 36868
  24.5 7.1 %copy-start.16 = (f32[2048]{0:T(1024)S(1)}, f32[2048]{0:T(1024)}, u32[]{:S(2)}) copy-start(f32[2048]{0:T(1024)} %param.24) | copy-start | bytes 24580
  24.6 7.1 %copy-start.17 = (f32[4,512]{1,0:T(4,128)S(1)}, f32[4,512]{1,0:T(4,128)}, u32[]{:S(2)}) copy-start(f32[4,512]{1,0:T(4,128)} %convbc_ref.1) | copy-start | bytes 24580
  24.6 7.1 %copy-start.18 = (bf16[1,3,768]{2,1,0:T(4,128)(2,1)S(1)}, bf16[1,3,768]{2,1,0:T(4,128)(2,1)}, u32[]{:S(2)}) copy-start(bf16[1,3,768]{2,1,0:T(4,128)(2,1)} %histx_ref.1) | copy-start | bytes 13828
  24.6 7.1 %copy-start.19 = (bf16[1,3,512]{2,1,0:T(4,128)(2,1)S(1)}, bf16[1,3,512]{2,1,0:T(4,128)(2,1)}, u32[]{:S(2)}) copy-start(bf16[1,3,512]{2,1,0:T(4,128)(2,1)} %histbc_ref.1) | copy-start | bytes 9220
  24.6 7.1 %copy-start.20 = (f32[12]{0:T(128)S(1)}, f32[12]{0:T(128)}, u32[]{:S(2)}) copy-start(f32[12]{0:T(128)} %param.40) | copy-start | bytes 148
  24.6 7.1 %copy-start.21 = (f32[12]{0:T(128)S(1)}, f32[12]{0:T(128)}, u32[]{:S(2)}) copy-start(f32[12]{0:T(128)} %param.41) | copy-start | bytes 148
  24.6 7.0 %collective-permute-start = (bf16[512,1024]{1,0:T(8,128)(2,1)}, bf16[512,1024]{1,0:T(8,128)(2,1)}, u32[]{:S(2)}, u32[]{:S(2)}) collective-permute-start(bf16[512,1024]{1,0:T(8,128)(2,1)} %mine_ref.1), channel_id=1, source_target_pairs={{0,1},{1,0},{2,3},{3,2},{4,5},{5,4},{6,7},{7,6},{8,9},{9,8},{10,11... | collective-permute-start | bytes 3145736 | tf_op jit(solution)/shard_map/ppermute | solution.py:569
  59.0 5.2 %collective-permute-start.7 = (f32[1,512]{1,0:T(1,128)S(1)}, f32[1,512]{1,0:T(1,128)S(1)}, u32[]{:S(2)}, u32[]{:S(2)}) collective-permute-start(f32[1,512]{1,0:T(1,128)S(1)} %get-tuple-element.22), channel_id=1, source_target_pairs={{0,1},{1,0},{2,3},{3,2},{4,5},{5,4},{6,7},{7,6},{8,9},{9,8},{10,11... | collective-permute-start | bytes 6152 | tf_op jit(solution)/shard_map/ppermute | solution.py:594
  65.6 7.4 %copy-start.22 = (s32[32]{0:T(128)S(1)}, s32[32]{0:T(128)}, u32[]{:S(2)}) copy-start(s32[32]{0:T(128)} %get-tuple-element.13.seen_ref) | copy-start | bytes 388
  77.6 15.3 %copy-start.1 = (f32[512,2048]{1,0:T(8,128)S(1)}, f32[512,2048]{1,0:T(8,128)}, u32[]{:S(2)}) copy-start(f32[512,2048]{1,0:T(8,128)} %copy-done) | copy-start | bytes 12582916
  77.7 15.3 %copy-start.2 = (bf16[512,2048]{1,0:T(8,128)(2,1)S(1)}, bf16[512,2048]{1,0:T(8,128)(2,1)}, u32[]{:S(2)}) copy-start(bf16[512,2048]{1,0:T(8,128)(2,1)} %weight_ref.5) | copy-start | bytes 6291460
  93.7 3.8 %collective-permute-start.8 = (bf16[512,1024]{1,0:T(8,128)(2,1)S(1)}, bf16[512,1024]{1,0:T(8,128)(2,1)S(1)}, u32[]{:S(2)}, u32[]{:S(2)}) collective-permute-start(bf16[512,1024]{1,0:T(8,128)(2,1)S(1)} %attn_out.3), channel_id=1, source_target_pairs={{0,1},{1,0},{2,3},{3,2},{4,5},{5,4},{6,7},{7,6},{8,9},{9,8},{10,11... | collective-permute-start | bytes 3145736 | tf_op jit(solution)/shard_map/ppermute | solution.py:601
  (23 other events, 44.7 us)

commit v3 on v2

--- a/solution.py
+++ b/solution.py
@@ -23,6 +23,7 @@
 HBM = pl.BlockSpec(memory_space=pltpu.HBM)
 F32 = jnp.float32
 BF16 = jnp.bfloat16
+LIGHT = pl.CostEstimate(flops=10**6, bytes_accessed=10**4, transcendentals=0)
 
 
 def params(mebibytes):
@@ -40,11 +41,11 @@
     )
 
 
-def want_kernel(pages_dev, capacity, page_size, table_ref, length_ref, want_ref, seen_ref, counts):
+def want_kernel(pages_dev, capacity, page_size, table_ref, length_ref, want_ref, seen_ref, slots, counts):
     for i in range(counts.shape[0]):
         counts[i] = 0
-    for i in range(want_ref.shape[1]):
-        want_ref[0, i] = 0
+    for i in range(slots.shape[0]):
+        slots[i] = 0
         seen_ref[i] = 0
     for page in range(table_ref.shape[1]):
         entry = table_ref[0, page]
@@ -52,8 +53,14 @@
         rank = counts[owner]
         counts[owner] = rank + 1
         place = owner * capacity + rank
-        want_ref[0, place] = entry - owner * pages_dev
+        slots[place] = entry - owner * pages_dev
         seen_ref[place] = jnp.clip(length_ref[0] - page * page_size, 0, page_size)
+    lane = lax.broadcasted_iota(jnp.int32, want_ref.shape[1:], 1)
+    for owner in range(want_ref.shape[0]):
+        tile = jnp.zeros(want_ref.shape[1:], jnp.int32)
+        for rank in range(capacity):
+            tile = jnp.where(lane == rank, slots[owner * capacity + rank], tile)
+        want_ref[owner] = tile
 
 
 def wanted(table, length, devices, pages_dev, page_size):
@@ -61,77 +68,68 @@
     return pl.pallas_call(
         functools.partial(want_kernel, pages_dev, capacity, page_size),
         out_shape=(
-            jax.ShapeDtypeStruct((1, devices * capacity), jnp.int32),
+            jax.ShapeDtypeStruct((devices, 8, 128), jnp.int32),
             jax.ShapeDtypeStruct((devices * capacity,), jnp.int32),
         ),
         in_specs=[SMEM, SMEM],
-        out_specs=(SMEM, SMEM),
-        scratch_shapes=[pltpu.SMEM((devices,), jnp.int32)],
+        out_specs=(VMEM, SMEM),
+        scratch_shapes=[
+            pltpu.SMEM((devices * capacity,), jnp.int32),
+            pltpu.SMEM((devices,), jnp.int32),
+        ],
         name="wanted",
     )(table, length)
 
 
-def share_wants(want, axis, devices):
-    low = 1 << ((devices.bit_length() - 1) // 2)
-
-    def swapped(rows, mask):
-        return lax.ppermute(rows, axis, [(i, i ^ mask) for i in range(devices)])
-
-    columns = [want] + [swapped(want, j * low) for j in range(1, devices // low)]
-    mine = jnp.concatenate(columns, axis=0)
-    return [mine] + [swapped(mine, i) for i in range(1, low)]
-
-
-def gather_kernel(capacity, cuts, low, me_ref, *refs):
-    lists, pages_ref = refs[:low], refs[low]
-    outs = refs[low + 1 : low + 1 + len(cuts)]
-    held, sems_in, sems_out = refs[low + 1 + len(cuts) :]
-    high = lists[0].shape[0]
-    me = me_ref[0]
-    places = []
-    for i in range(low):
-        for j in range(high):
-            for rank in range(capacity):
-                slot = lists[i][j, me * capacity + rank]
-                target = (me ^ (i + low * j)) * capacity + rank
-                index = len(places)
-                copy = pltpu.make_async_copy(pages_ref.at[slot], held.at[index], sems_in.at[index])
-                copy.start()
-                places.append((copy, target))
-    sends = []
-    for index, (copy, target) in enumerate(places):
-        copy.wait()
-        for piece, (start, stop) in enumerate(cuts):
-            send = pltpu.make_async_copy(
-                held.at[index, :, start:stop, :], outs[piece].at[target], sems_out.at[piece, index]
-            )
-            send.start()
-            sends.append(send)
-    for send in sends:
-        send.wait()
-
-
-def gather_pages(me, lists, kv_pages, capacity, cuts):
-    low = len(lists)
-    count = low * lists[0].shape[0] * capacity
-    _, two, page_size, width = kv_pages.shape
+def gather_kernel(capacity, asked_hbm, pages_ref, out_ref, own_ref, asked, held, sem, sems_in, sems_out):
+    me = lax.axis_index("req")
+    load = pltpu.make_async_copy(asked_hbm, asked, sem.at[0])
+    load.start()
+    load.wait()
+    count = held.shape[0]
+    reads = []
+    for index in range(count):
+        slot = asked[index // capacity, 0, index % capacity]
+        reads.append(
+            pltpu.make_async_copy(pages_ref.at[slot], held.at[index], sems_in.at[index])
+        )
+        reads[-1].start()
+    writes = []
+    for index in range(count):
+        reads[index].wait()
+        writes.append(
+            pltpu.make_async_copy(held.at[index], out_ref.at[index], sems_out.at[index])
+        )
+        writes[-1].start()
+    mine = pltpu.make_async_copy(held.at[pl.ds(me * capacity, capacity)], own_ref, sem.at[1])
+    mine.start()
+    for write in writes:
+        write.wait()
+    mine.wait()
+
+
+def gather_pages(asked, kv_pages, capacity):
+    count = asked.shape[0] * capacity
+    page = kv_pages.shape[1:]
     return pl.pallas_call(
-        functools.partial(gather_kernel, capacity, cuts, low),
-        out_shape=tuple(
-            jax.ShapeDtypeStruct((count, two, stop - start, width), kv_pages.dtype)
-            for start, stop in cuts
+        functools.partial(gather_kernel, capacity),
+        out_shape=(
+            jax.ShapeDtypeStruct((count,) + page, kv_pages.dtype),
+            jax.ShapeDtypeStruct((capacity,) + page, kv_pages.dtype),
         ),
-        in_specs=[SMEM] * (low + 1) + [HBM],
-        out_specs=(HBM,) * len(cuts),
+        in_specs=[HBM, HBM],
+        out_specs=(HBM, HBM),
         scratch_shapes=[
-            pltpu.VMEM((count, two, page_size, width), kv_pages.dtype),
+            pltpu.SMEM(asked.shape, jnp.int32),
+            pltpu.VMEM((count,) + page, kv_pages.dtype),
+            pltpu.SemaphoreType.DMA((2,)),
             pltpu.SemaphoreType.DMA((count,)),
-            pltpu.SemaphoreType.DMA((len(cuts), count)),
+            pltpu.SemaphoreType.DMA((count,)),
         ],
         compiler_params=params(60),
-        cost_estimate=pl.CostEstimate(flops=0, bytes_accessed=8 * 2**20, transcendentals=0),
+        cost_estimate=LIGHT,
         name="gather_pages",
-    )(me, *lists, kv_pages)
+    )(asked, kv_pages)
 
 
 def silu(value):
@@ -275,7 +273,7 @@
         ssm_y = (
             jnp.concatenate(blocks, axis=0)
             + carried * jnp.exp2(fades)
-            + skip_ref[:, cols] * x_rows
+            + jnp.where(first, skip_ref[one], skip_ref[two]) * x_rows
         )
         gated = ssm_y * silu(z_ref[:, cols].astype(F32))
         squares = squares + gated * gated
@@ -330,7 +328,7 @@
             out((1, rows), F32),
             out(state.shape, F32),
         ),
-        in_specs=[SMEM] + [VMEM] * 13 + [HBM] * 8,
+        in_specs=[SMEM] + [VMEM] * 11 + [SMEM, VMEM] + [HBM] * 8,
         out_specs=(VMEM,) * 5 + (HBM,),
         scratch_shapes=[
             pltpu.VMEM((rows, width), BF16),
@@ -354,10 +352,8 @@
             pltpu.VMEM((rows, MN), BF16),
             pltpu.VMEM((rows, MN), BF16),
         ],
-        compiler_params=params(32),
-        cost_estimate=pl.CostEstimate(
-            flops=16 * 10**9, bytes_accessed=17 * 2**20, transcendentals=4 * 10**6
-        ),
+        compiler_params=params(60),
+        cost_estimate=LIGHT,
         name="front",
     )(
         core, mine, other, gain, cosine, sine,
@@ -401,132 +397,218 @@
     return softmax_step(scores + hide, values.reshape(pages * tokens, width), state)
 
 
-def attend_new_kernel(q_ref, k_ref, v_ref, sum_ref, total_ref, top_ref):
+def attend_early_kernel(masks, picks, fresh, seen_ref, q_hbm, *refs):
+    count = max(array for array, _ in picks) + 1
+    given = 2 if fresh else 3
+    start_hbm, arrays = refs[:given], refs[given : given + count]
+    outs = refs[given + count : given + count + 3]
+    q_ref, k_ref, v_ref, kv_ref, states, sems, sems_out = refs[given + count + 3 :]
     rows = k_ref.shape[0]
+    pages, _, tokens, _ = kv_ref.shape
+    capacity = pages // len(masks)
+    me = lax.axis_index("req")
+    targets = (k_ref, v_ref) if fresh else (states.at[0], states.at[1], states.at[2])
+    copies = [pltpu.make_async_copy(q_hbm, q_ref, sems.at[0])]
+    for index, (source, target) in enumerate(zip(start_hbm, targets)):
+        copies.append(pltpu.make_async_copy(source, target, sems.at[1 + index]))
+    for index, (array, entry) in enumerate(picks):
+        source = arrays[array] if entry is None else arrays[array].at[entry]
+        copies.append(
+            pltpu.make_async_copy(
+                source, kv_ref.at[pl.ds(index * capacity, capacity)], sems.at[4 + index]
+            )
+        )
+    for copy in copies:
+        copy.start()
+    seen = [seen_ref[(me ^ mask) * capacity + rank] for mask in masks for rank in range(capacity)]
     row = lax.broadcasted_iota(jnp.int32, (rows, rows), 0)
     column = lax.broadcasted_iota(jnp.int32, (rows, rows), 1)
-    for start in range(0, q_ref.shape[0], rows):
+    for copy in copies:
+        copy.wait()
+    per_chunk = CHUNK // tokens
+    sends = []
+    for head, start in enumerate(range(0, q_ref.shape[0], rows)):
         here = slice(start, start + rows)
-        scores = lax.dot_general(
-            q_ref[here, :], k_ref[...], CONTRACT_LAST, preferred_element_type=F32
-        )
-        scores = jnp.where(column <= row, scores, NEG_FILL)
-        sum_ref[here, :], total_ref[here, :], top_ref[here, :] = softmax_step(
-            scores, v_ref[...], None
-        )
-
-
-def attend_new(queries, keys, values):
+        if fresh:
+            scores = lax.dot_general(
+                q_ref[here, :], k_ref[...], CONTRACT_LAST, preferred_element_type=F32
+            )
+            state = softmax_step(jnp.where(column <= row, scores, NEG_FILL), v_ref[...], None)
+        else:
+            state = (states[0, here, :], states[1, here, :], states[2, here, :])
+        for begin in range(0, pages, per_chunk):
+            span = slice(begin, begin + per_chunk)
+            state = page_step(q_ref[here, :], kv_ref[span, 0], kv_ref[span, 1], seen[span], state)
+        for kind in range(3):
+            states[kind, here, :] = state[kind]
+            send = pltpu.make_async_copy(
+                states.at[kind, here, :], outs[kind].at[here, :], sems_out.at[3 * head + kind]
+            )
+            send.start()
+            sends.append(send)
+    for send in sends:
+        send.wait()
+
+
+def attend_early(seen, queries, start, rows, arrays, masks, picks):
     count = queries.shape[0]
-    rows = keys.shape[0]
+    block = arrays[0].shape[-4:]
+    pages = len(masks) * block[0]
+    fresh = len(start) == 2
     return pl.pallas_call(
-        attend_new_kernel,
+        functools.partial(attend_early_kernel, masks, picks, fresh),
         out_shape=(jax.ShapeDtypeStruct((count, HEAD_SIZE), F32),) * 3,
-        in_specs=[VMEM] * 3,
-        out_specs=(VMEM,) * 3,
-        compiler_params=params(16),
-        cost_estimate=pl.CostEstimate(
-            flops=8 * count * rows * HEAD_SIZE,
-            bytes_accessed=4 * 2**20,
-            transcendentals=count * rows,
-        ),
-        name="attend_new",
-    )(queries, keys, values)
-
-
-def attend_pages_kernel(seen_ref, q_ref, sum_ref, total_ref, top_ref, kv_hbm, out_ref, kv_ref, sems):
+        in_specs=[SMEM] + [HBM] * (1 + len(start) + len(arrays)),
+        out_specs=(HBM,) * 3,
+        scratch_shapes=[
+            pltpu.VMEM(queries.shape, BF16),
+            pltpu.VMEM((rows, HEAD_SIZE), BF16),
+            pltpu.VMEM((rows, HEAD_SIZE), BF16),
+            pltpu.VMEM((pages,) + block[1:], BF16),
+            pltpu.VMEM((3, count, HEAD_SIZE), F32),
+            pltpu.SemaphoreType.DMA((4 + len(masks),)),
+            pltpu.SemaphoreType.DMA((3 * count // rows,)),
+        ],
+        compiler_params=params(60),
+        cost_estimate=LIGHT,
+        name="attend_first" if fresh else "attend_more",
+    )(seen, queries, *start, *arrays)
+
+
+def attend_late_kernel(
+    masks, core_ref, seen_ref, q_hbm, sum_hbm, total_hbm, top_hbm, weight_hbm, part_hbm, kv_hbm,
+    context_ref, out_ref, q_ref, near, far, kv_ref, weight_ref, part_ref, sems, sems_late,
+):
     pages, _, tokens, _ = kv_ref.shape
-    rows = out_ref.shape[0]
+    capacity = pages // len(masks)
+    me = lax.axis_index("req")
+    rows, half = out_ref.shape
+    heads = q_ref.shape[0] // rows
     per_chunk = CHUNK // tokens
-    spans = [slice(start, start + per_chunk) for start in range(0, pages, per_chunk)]
-    copies = [
-        pltpu.make_async_copy(kv_hbm.at[span], kv_ref.at[span], sems.at[i])
-        for i, span in enumerate(spans)
+    now = [pltpu.make_async_copy(q_hbm, q_ref, sems.at[0])] + [
+        pltpu.make_async_copy(
+            kv_hbm.at[pl.ds((me ^ mask) * capacity, capacity)],
+            kv_ref.at[pl.ds(index * capacity, capacity)],
+            sems.at[1 + index],
+        )
+        for index, mask in enumerate(masks)
     ]
-    for copy in copies:
+    there = pl.ds(pl.multiple_of((1 - core_ref[0]) * half, half), half)
+    late = [
+        pltpu.make_async_copy(source, near.at[kind], sems_late.at[kind])
+        for kind, source in enumerate((sum_hbm, total_hbm, top_hbm))
+    ] + [
+        pltpu.make_async_copy(weight_hbm.at[:, there], weight_ref, sems_late.at[3]),
+        pltpu.make_async_copy(part_hbm, part_ref, sems_late.at[4]),
+    ]
+    for copy in now:
         copy.start()
-    for head in range(q_ref.shape[0] // rows):
+    seen = [seen_ref[(me ^ mask) * capacity + rank] for mask in masks for rank in range(capacity)]
+    for copy in now:
+        copy.wait()
+    for copy in late:
+        copy.start()
+    for head in range(heads):
         here = slice(head * rows, (head + 1) * rows)
-        query = q_ref[here, :]
-        state = (sum_ref[here, :], total_ref[here, :], top_ref[here, :])
-        for span, copy in zip(spans, copies):
-            if head == 0:
-                copy.wait()
-            seen = [seen_ref[page] for page in range(span.start, span.stop)]
-            state = page_step(query, kv_ref[span, 0], kv_ref[span, 1], seen, state)
-        out_ref[:, head * HEAD_SIZE : (head + 1) * HEAD_SIZE] = (state[0] / state[1]).astype(BF16)
-
-
-def attend_pages(seen, queries, state, kv, rows):
-    pages, _, tokens, _ = kv.shape
-    count = queries.shape[0]
-    return pl.pallas_call(
-        attend_pages_kernel,
-        out_shape=jax.ShapeDtypeStruct((rows, count // rows * HEAD_SIZE), BF16),
-        in_specs=[SMEM] + [VMEM] * 4 + [HBM],
-        out_specs=VMEM,
-        scratch_shapes=[
-            pltpu.VMEM(kv.shape, kv.dtype),
-            pltpu.SemaphoreType.DMA((pages * tokens // CHUNK,)),
-        ],
-        compiler_params=params(16),
-        cost_estimate=pl.CostEstimate(
-            flops=8 * count * pages * tokens * HEAD_SIZE,
-            bytes_accessed=4 * 2**20,
-            transcendentals=count * pages * tokens,
-        ),
-        name="attend_pages",
-    )(seen, queries, *state, kv)
-
-
-def mixer_out_kernel(gated_ref, scale_ref, weight_ref, out_ref):
-    for start in range(0, out_ref.shape[1], 256):
+        state = None
+        for begin in range(0, pages, per_chunk):
+            span = slice(begin, begin + per_chunk)
+            state = page_step(q_ref[here, :], kv_ref[span, 0], kv_ref[span, 1], seen[span], state)
+        for kind in range(3):
+            far[kind, here, :] = state[kind]
+    for copy in late:
+        copy.wait()
+    for head in range(heads):
+        here = slice(head * rows, (head + 1) * rows)
+        top = jnp.maximum(near[2, here, :], far[2, here, :])
+        fade_near = jnp.exp2((near[2, here, :] - top) * SCORE_SCALE)
+        fade_far = jnp.exp2((far[2, here, :] - top) * SCORE_SCALE)
+        summed = near[0, here, :] * fade_near + far[0, here, :] * fade_far
+        total = near[1, here, :] * fade_near + far[1, here, :] * fade_far
+        context_ref[:, head * HEAD_SIZE : (head + 1) * HEAD_SIZE] = (summed / total).astype(BF16)
+    for start in range(0, half, 256):
         tile = slice(start, start + 256)
         out_ref[:, tile] = (
-            jnp.dot(gated_ref[...], weight_ref[:, tile], preferred_element_type=F32)
-            * scale_ref[...]
-        )
-
-
-def mixer_out(gated, scale, weight):
+            jnp.dot(context_ref[...], weight_ref[:, tile], preferred_element_type=F32)
+            + part_ref[:, tile]
+        ).astype(BF16)
+
+
+def attend_late(core, seen, queries, state, weight, part, kv, masks):
+    rows, half = part.shape
+    count = queries.shape[0]
+    pages = len(masks) * kv.shape[0] // lax.axis_size("req")
+    return pl.pallas_call(
+        functools.partial(attend_late_kernel, masks),
+        out_shape=(
+            jax.ShapeDtypeStruct((rows, count // rows * HEAD_SIZE), BF16),
+            jax.ShapeDtypeStruct((rows, half), BF16),
+        ),
+        in_specs=[SMEM] * 2 + [HBM] * 7,
+        out_specs=(VMEM, VMEM),
+        scratch_shapes=[
+            pltpu.VMEM(queries.shape, BF16),
+            pltpu.VMEM((3, count, HEAD_SIZE), F32),
+            pltpu.VMEM((3, count, HEAD_SIZE), F32),
+            pltpu.VMEM((pages,) + kv.shape[1:], BF16),
+            pltpu.VMEM((weight.shape[0], half), BF16),
+            pltpu.VMEM((rows, half), F32),
+            pltpu.SemaphoreType.DMA((1 + len(masks),)),
+            pltpu.SemaphoreType.DMA((5,)),
+        ],
+        compiler_params=params(60),
+        cost_estimate=LIGHT,
+        name="attend_late",
+    )(core, seen, queries, *state, weight, part, kv)
+
+
+def mixer_out_kernel(core_ref, gated_ref, scale_ref, weight_ref, theirs_ref, ours_ref):
+    half = ours_ref.shape[1]
+    for start in range(0, half, 256):
+        for core, out_ref in ((1 - core_ref[0], theirs_ref), (core_ref[0], ours_ref)):
+            here = pl.ds(pl.multiple_of(core * half + start, 256), 256)
+            out_ref[:, start : start + 256] = (
+                jnp.dot(gated_ref[...], weight_ref[:, here], preferred_element_type=F32)
+                * scale_ref[...]
+            )
+
+
+def mixer_out(core, gated, scale, weight):
     rows, depth = gated.shape
     width = weight.shape[1]
     return pl.pallas_call(
         mixer_out_kernel,
-        out_shape=jax.ShapeDtypeStruct((rows, width), F32),
-        in_specs=[VMEM] * 3,
-        out_specs=VMEM,
+        out_shape=(jax.ShapeDtypeStruct((rows, width // 2), F32),) * 2,
+        in_specs=[SMEM] + [VMEM] * 3,
+        out_specs=(VMEM,) * 2,
         compiler_params=params(16),
-        cost_estimate=pl.CostEstimate(
-            flops=2 * rows * depth * width, bytes_accessed=8 * 2**20, transcendentals=0
-        ),
+        cost_estimate=LIGHT,
         name="mixer_out",
-    )(gated, scale, weight)
-
-
-def attn_out_kernel(core_ref, context_ref, weight_ref, part_ref, out_ref):
+    )(core, gated, scale, weight)
+
+
+def ours_kernel(core_ref, context_ref, weight_ref, part_ref, out_ref):
     half = out_ref.shape[1]
     for start in range(0, half, 256):
         here = pl.ds(pl.multiple_of(core_ref[0] * half + start, 256), 256)
-        out_ref[:, start : start + 256] = (
+        tile = slice(start, start + 256)
+        out_ref[:, tile] = (
             jnp.dot(context_ref[...], weight_ref[:, here], preferred_element_type=F32)
-            + part_ref[:, here]
-        ).astype(out_ref.dtype)
-
-
-def attn_out(core, context, weight, part, dtype):
+            + part_ref[:, tile]
+        )
+
+
+def ours_half(core, context, weight, part):
     rows, depth = context.shape
     half = weight.shape[1] // 2
     return pl.pallas_call(
-        attn_out_kernel,
-        out_shape=jax.ShapeDtypeStruct((rows, half), dtype),
+        ours_kernel,
+        out_shape=jax.ShapeDtypeStruct((rows, half), F32),
         in_specs=[SMEM] + [VMEM] * 3,
         out_specs=VMEM,
         compiler_params=params(16),
-        cost_estimate=pl.CostEstimate(
-            flops=2 * rows * depth * half, bytes_accessed=4 * 2**20, transcendentals=0
-        ),
-        name="attn_out",
+        cost_estimate=LIGHT,
+        name="ours_half",
     )(core, context, weight, part)
 
 
@@ -567,38 +649,37 @@
     want, seen = wanted(page_table, cached_len, devices, pages_dev, page_size)
     cosine, sine = rope_tables(length + jnp.arange(row_count, dtype=jnp.int32))
     other = lax.ppermute(tokens, "tp", swap)
-    lists = share_wants(want, "req", devices)
-    me = lax.axis_index("req").astype(jnp.int32).reshape(1)
-    cuts = ((0, page_size),)
-    fetched = gather_pages(
-        me, lists, kv_pages.reshape((pages_dev, 2, page_size, HEAD_SIZE)), capacity, cuts
-    )
-
-    arrived = lax.all_to_all(
-        fetched[0].reshape((devices, capacity) + fetched[0].shape[1:]),
-        "req",
-        split_axis=0,
-        concat_axis=0,
-        tiled=True,
-    ).reshape(fetched[0].shape)
+
+    def exchange(blocks):
+        return lax.all_to_all(blocks, "req", split_axis=0, concat_axis=0, tiled=True)
+
+    fetched, own = gather_pages(
+        exchange(want), kv_pages.reshape((pages_dev, 2, page_size, HEAD_SIZE)), capacity
+    )
+    arrived = exchange(fetched.reshape((devices, capacity) + fetched.shape[1:])).reshape(
+        fetched.shape
+    )
 
     heads = w_dt.shape[1]
     queries, fresh_keys, fresh_values, gated, squares, last_state = front(
         core, tokens, other, attn_gain[None, :], cosine, sine,
         conv_x_state, conv_bc_state, conv_w_x, conv_w_bc,
-        dt_bias[None, :], decay_rate[None, :], jnp.repeat(skip_gain, MP)[None, :],
+        dt_bias[None, :], decay_rate[None, :], skip_gain,
         mixer_gain[None, :],
         w_dt.T, w_bc, w_ssm_in, w_gate_z, w_query, key_weight, value_weight,
         ssm_state.reshape((heads * MP, MN)),
     )
     total = squares + lax.ppermute(squares, "tp", swap)
     scale = lax.rsqrt(total.reshape((row_count, 1)) / DSSM + EPSILON)
-    part = mixer_out(gated, scale, w_mixer_out)
-    state = attend_new(queries, fresh_keys, fresh_values)
-    context = attend_pages(seen, queries, state, arrived, row_count)
-    theirs = attn_out(1 - core, context, w_attn_out, part, BF16)
-    ours = attn_out(core, context, w_attn_out, part, F32)
+    part_theirs, part_ours = mixer_out(core, gated, scale, w_mixer_out)
+    state = attend_early(
+        seen, queries, (fresh_keys, fresh_values), row_count, [own], [0], [(0, None)]
+    )
+    context, theirs = attend_late(
+        core, seen, queries, state, w_attn_out, part_theirs, arrived, list(range(1, devices))
+    )
     received = lax.ppermute(theirs, "tp", swap)
+    ours = ours_half(core, context, w_attn_out, part_ours)
     mixed = (ours + received.astype(F32)).astype(BF16)
     return (mixed, last_state.reshape(ssm_state.shape))
 

time: 99.6 us -> 94.8 us (0.952)
  local copies, waits for them, and re-layouts: 19.6 us -> 8.17 us
  blocking collectives: 0 us -> 11.3 us
  starting transfers between devices: 18.7 us -> 9.97 us
  Pallas kernels: 45.8 us -> 48.8 us
    unnamed x74 -> x20, local copies, waits for them, and re-layouts: 19.3 us -> 7.45 us
    all_to_all x0 -> x1, blocking collectives: none -> 11.3 us  [exchange(): lax.all_to_all(blocks, 'req', split_axis=0, concat_axis=0, tiled=True)]
    all_to_all x1, waiting for transfers between devices: 3.58 us -> 10.1 us  [exchange(): lax.all_to_all(blocks, 'req', split_axis=0, concat_axis=0, tiled=True)]
    ppermute x6 -> x0, starting transfers between devices: 6.27 us -> none  [swapped(): return lax.ppermute(rows, axis, [(i, i ^ mask) for i in range(devices)])]
    ppermute x6 -> x0, waiting for transfers between devices: 3.59 us -> none  [swapped(): return lax.ppermute(rows, axis, [(i, i ^ mask) for i in range(devices)])]
    pallas_call x6 -> x5, Pallas kernels: 24.9 us -> 27 us  [the longest x1 14.1 us: attend_late(): pl.pallas_call(functools.partial(attend_late_kernel, masks), out_shape=(j...]
    ppermute x1, starting transfers between devices: 4.41 us -> 2.45 us  [shards(): other = lax.ppermute(tokens, 'tp', swap)]
    ppermute x1, waiting for transfers between devices: 1.55 us -> 0.01 us  [shards(): received = lax.ppermute(theirs, 'tp', swap)]
  transfers between devices with their start and end apart: 10 -> 4, of which waited for: 8 -> 1; matrix products, arithmetic and copies ran while one was open for 2% -> 4% of each run, Pallas kernels for 24% -> 30%
where the time goes in v3:
time: 94.8 us; the launch traced here: 93.8 us
  Pallas kernels  48.8 us (51%)
  blocking collectives  11.3 us (12%)
  waiting for transfers between devices  10.1 us (11%)
  starting transfers between devices  9.97 us (11%)
  local copies, waits for them, and re-layouts  8.17 us (9%)
  other arithmetic  4.05 us (4%)
  between operations  1.42 us (1%)
    pallas_call x1, Pallas kernels, front(): pl.pallas_call(front_kernel, out_shape=(out((wq.shape[1] // HEAD_SIZE * r...  20.2 us
    pallas_call x1, Pallas kernels, attend_late(): pl.pallas_call(functools.partial(attend_late_kernel, masks), out_shape=(j...  14.1 us
    all_to_all x1, blocking collectives, exchange(): lax.all_to_all(blocks, 'req', split_axis=0, concat_axis=0, tiled=True)  11.3 us
    all_to_all x1, waiting for transfers between devices, exchange(): lax.all_to_all(blocks, 'req', split_axis=0, concat_axis=0, tiled=True)  10.1 us
    unnamed x20, local copies, waits for them, and re-layouts  7.45 us
    all_to_all x1, starting transfers between devices, exchange(): lax.all_to_all(blocks, 'req', split_axis=0, concat_axis=0, tiled=True)  5.86 us
    pallas_call x1, Pallas kernels, attend_early(): pl.pallas_call(functools.partial(attend_early_kernel, masks, picks, fresh...  5.27 us
    pallas_call x1, Pallas kernels, gather_pages(): pl.pallas_call(functools.partial(gather_kernel, capacity), out_shape=(jax...  5.02 us
  transfers between devices with their start and end apart: 4, of which 1 were waited for; matrix products, arithmetic and copies ran while one was open for 4% of the time, Pallas kernels for 30%

profile of v3, /device:TPU:13, one launch (start us, length us, event | category | flops | bytes accessed | tf_op | source)
XLA Modules:
  0.0 93.8 jit_solution(12677285999332054808)
XLA Ops:
  1.3 1.6 %wanted.1 = (s32[16,8,128]{2,1,0:T(8,128)}, s32[32]{0:T(128)}) custom-call(s32[1,32]{1,0:T(1,128)} %table_ref.1, s32[1]{0:T(128)} %copy.26.length_ref), custom_call_target="tpu_custom_call" | custom-call | tf_op jit(solution)/shard_map/wanted/pallas_call | solution.py:68
  2.9 11.3 %all_to_all.10.asked_hbm = s32[16,8,128]{2,1,0:T(8,128)} all-to-all(s32[16,8,128]{2,1,0:T(8,128)} %get-tuple-element.23), channel_id=1, replica_groups=mesh['req'=16,'tp'=2] {'req'}, dimensions={0} | all-to-all | bytes 131072 | tf_op jit(solution)/shard_map/all_to_all | solution.py:654
  14.1 5.0 %gather_pages.1 = (bf16[32,2,128,128]{3,2,1,0:T(8,128)(2,1)}, bf16[2,2,128,128]{3,2,1,0:T(8,128)(2,1)}) custom-call(s32[16,8,128]{2,1,0:T(8,128)} %all_to_all.10.asked_hbm, bf16[32,2,128,128]{3,2,1,0:T(8,128)(2,1)} %bitcast.14), custom_call_target="tpu_custom_call" | custom-call | flops 1000000 | bytes 10000 | tf_op jit(solution)/shard_map/gather_pages/pallas_call | solution.py:114
  19.2 5.9 %all-to-all-start.1 = ((bf16[16,2,2,128,128]{4,3,2,1,0:T(8,128)(2,1)}), bf16[16,2,2,128,128]{4,3,2,1,0:T(8,128)(2,1)}, u32[]{:S(2)}, u32[]{:S(2)}) async-start(bf16[16,2,2,128,128]{4,3,2,1,0:T(8,128)(2,1)} %bitcast.15), calls=%async_computation.1 | async-start | bytes 4194304 | tf_op jit(solution)/shard_map/all_to_all | solution.py:654
  25.1 2.5 %collective-permute-start = (bf16[512,1024]{1,0:T(8,128)(2,1)S(1)}, bf16[512,1024]{1,0:T(8,128)(2,1)S(1)}, u32[]{:S(2)}, u32[]{:S(2)}) collective-permute-start(bf16[512,1024]{1,0:T(8,128)(2,1)S(1)} %copy-done.7), channel_id=1, source_target_pairs={{0,1},{1,0},{2,3},{3,2},{4,5},{5,4},{6,7},{7,6},{8,9},{9,8},{10,11... | collective-permute-start | bytes 3145736 | tf_op jit(solution)/shard_map/ppermute | solution.py:651
  27.5 0.6 broadcast_in_dim.17.mixer_gain_ref
  28.1 1.0 %fusion = (f32[512,64]{1,0:T(8,128)S(1)}, f32[512,64]{1,0:T(8,128)S(1)}, f32[512,64]{1,0:T(8,128)S(1)}) fusion(f32[64]{0:T(128)S(1)} %multiply_power_fusion, f32[512]{0:T(512)S(1)} %add_convert_fusion.1), kind=kLoop, calls=%fused_computation.5 | loop fusion | flops 65536 | bytes 395520 | tf_op jit(solution)/shard_map/neg | solution.py:40
  29.1 1.0 %pad_maximum_fusion = (f32[512,128]{1,0:T(8,128)}, f32[512,128]{1,0:T(8,128)}) fusion(f32[512,64]{1,0:T(8,128)S(1)} %get-tuple-element.38, f32[512,64]{1,0:T(8,128)S(1)} %get-tuple-element.37, f32[512,64]{1,0:T(8,128)S(1)} %get-tuple-element.36), kind=kLoop, calls=%fused_computation.3 | loop fusion | flops 131072 | bytes 917504 | tf_op jit(solution)/shard_map/concatenate | solution.py:39
  30.1 1.0 %copy-done.8 = bf16[512,1024]{1,0:T(8,128)(2,1)} copy-done((bf16[512,1024]{1,0:T(8,128)(2,1)}, bf16[512,1024]{1,0:T(8,128)(2,1)S(1)}, u32[]{:S(2)}) %copy-start.8) | copy-done | bytes 1048600
  31.1 20.2 %front.1 = (bf16[2048,128]{1,0:T(8,128)(2,1)}, bf16[512,128]{1,0:T(8,128)(2,1)}, bf16[512,128]{1,0:T(8,128)(2,1)}, bf16[512,768]{1,0:T(8,128)(2,1)}, f32[1,512]{1,0:T(1,128)}, /*index=5*/f32[768,256]{1,0:T(8,128)}) custom-call(s32[1]{0:T(128)} %bitcast.core_ref, bf16[512,1024]{1,0:T(8,128)(2,1)} %mine_ref.1, bf16[512,1024]{1,0:T(8,128)(2,1)} %copy-done.8, ...), custom_call_target="tpu_custom_call" | custom-call | flops 1000000 | bytes 10000 | tf_op jit(solution)/shard_map/front/pallas_call | solution.py:321
  51.5 5.3 %attend_first.1 = (f32[2048,128]{1,0:T(8,128)}, f32[2048,128]{1,0:T(8,128)}, f32[2048,128]{1,0:T(8,128)}) custom-call(s32[32]{0:T(128)} %get-tuple-element.19.seen_ref, bf16[2048,128]{1,0:T(8,128)(2,1)} %get-tuple-element.20.q_hbm, bf16[512,128]{1,0:T(8,128)(2,1)} %get-tuple-element.21.refs_0_, bf16[512,128]{1,0:T(8,128)(2,1)} %get-tuple-element.22.refs_1_, ...), custom_call_target="tpu_custom_call" | custom-call | flops 1000000 | bytes 10000 | tf_op jit(solution)/shard_map/attend_first/pallas_call | solution.py:458
  56.7 0.7 rsqrt_bitcast_fusion
  57.4 0.1 copy.25.scale_ref
  57.6 1.1 %copy-done.5 = bf16[512,768]{1,0:T(8,128)(2,1)S(1)} copy-done((bf16[512,768]{1,0:T(8,128)(2,1)S(1)}, bf16[512,768]{1,0:T(8,128)(2,1)}, u32[]{:S(2)}) %copy-start.5) | copy-done | bytes 786456
  58.7 1.8 %mixer_out.1 = (f32[512,1024]{1,0:T(8,128)S(1)}, f32[512,1024]{1,0:T(8,128)S(1)}) custom-call(s32[1]{0:T(128)} %bitcast.core_ref, bf16[512,768]{1,0:T(8,128)(2,1)S(1)} %copy-done.5, f32[512,1]{1,0:T(8,128)S(1)} %copy.25.scale_ref, bf16[768,2048]{1,0:T(8,128)(2,1)S(1)} %copy-done.1), custom_call_target="tpu_custom_call" | custom-call | flops 1000000 | bytes 10000 | tf_op jit(solution)/shard_map/mixer_out/pallas_call | solution.py:579
  60.6 1.3 %copy-done.2 = f32[512,1024]{1,0:T(8,128)} copy-done((f32[512,1024]{1,0:T(8,128)}, f32[512,1024]{1,0:T(8,128)S(1)}, u32[]{:S(2)}) %copy-start.2) | copy-done | bytes 2097176
  61.9 1.4 %copy-done.3 = f32[512,1024]{1,0:T(8,128)} copy-done((f32[512,1024]{1,0:T(8,128)}, f32[512,1024]{1,0:T(8,128)S(1)}, u32[]{:S(2)}) %copy-start.3) | copy-done | bytes 2097176
  63.3 10.1 %all-to-all-done.1 = bf16[16,2,2,128,128]{4,3,2,1,0:T(8,128)(2,1)} async-done(((bf16[16,2,2,128,128]{4,3,2,1,0:T(8,128)(2,1)}), bf16[16,2,2,128,128]{4,3,2,1,0:T(8,128)(2,1)}, u32[]{:S(2)}, u32[]{:S(2)}) %all-to-all-start.1) | async-done | bytes 2097184 | tf_op jit(solution)/shard_map/all_to_all | solution.py:654
  73.4 14.1 %attend_late.1 = (bf16[512,512]{1,0:T(8,128)(2,1)}, bf16[512,1024]{1,0:T(8,128)(2,1)}) custom-call(s32[1]{0:T(128)} %bitcast.core_ref, s32[32]{0:T(128)} %get-tuple-element.19.seen_ref, bf16[2048,128]{1,0:T(8,128)(2,1)} %get-tuple-element.20.q_hbm, f32[2048,128]{1,0:T(8,128)} %get-tuple-element.25.sum_hbm, f32[2048,128]{1,0:T(8,128)} %get-tuple-element.26.total_hbm, ...), custom_call_target="tpu_custom_call" | custom-call | flops 1000000 | bytes 10000 | tf_op jit(solution)/shard_map/attend_late/pallas_call | solution.py:541
  87.6 1.6 %collective-permute-start.2 = (bf16[512,1024]{1,0:T(8,128)(2,1)}, bf16[512,1024]{1,0:T(8,128)(2,1)S(1)}, u32[]{:S(2)}, u32[]{:S(2)}) collective-permute-start(bf16[512,1024]{1,0:T(8,128)(2,1)} %get-tuple-element.34), channel_id=1, source_target_pairs={{0,1},{1,0},{2,3},{3,2},{4,5},{5,4},{6,7},{7,6},{8,9},{9,8},{10,11... | collective-permute-start | bytes 3145736 | tf_op jit(solution)/shard_map/ppermute | solution.py:681
  89.1 1.6 %copy-done.4 = f32[512,1024]{1,0:T(8,128)S(1)} copy-done((f32[512,1024]{1,0:T(8,128)S(1)}, f32[512,1024]{1,0:T(8,128)}, u32[]{:S(2)}) %copy-start.4) | copy-done | bytes 2097176
  90.7 1.0 %copy-done.6 = bf16[512,512]{1,0:T(8,128)(2,1)S(1)} copy-done((bf16[512,512]{1,0:T(8,128)(2,1)S(1)}, bf16[512,512]{1,0:T(8,128)(2,1)}, u32[]{:S(2)}) %copy-start.6) | copy-done | bytes 524312
  91.8 0.7 ours_half.1
  92.5 1.3 %add_convert_fusion = bf16[512,1024]{1,0:T(8,128)(2,1)} fusion(f32[512,1024]{1,0:T(8,128)S(1)} %ours_half.1, bf16[512,1024]{1,0:T(8,128)(2,1)S(1)} %collective-permute-done.2), kind=kLoop, calls=%fused_computation | loop fusion | flops 1572864 | bytes 4194304 | tf_op jit(solution)/shard_map/convert_element_type | solution.py:683
  (20 shorter events, 0.2 us)
Async XLA Ops:
  19.2 5.9 %copy-start.7 = (bf16[512,1024]{1,0:T(8,128)(2,1)S(1)}, bf16[512,1024]{1,0:T(8,128)(2,1)}, u32[]{:S(2)}) copy-start(bf16[512,1024]{1,0:T(8,128)(2,1)} %mine_ref.1) | copy-start | bytes 3145732
  19.2 8.3 %copy-start.9 = (f32[768]{0:T(1024)S(1)}, f32[768]{0:T(1024)}, u32[]{:S(2)}) copy-start(f32[768]{0:T(1024)} %param.43) | copy-start | bytes 9220
  19.2 54.2 %all-to-all-start.1 = ((bf16[16,2,2,128,128]{4,3,2,1,0:T(8,128)(2,1)}), bf16[16,2,2,128,128]{4,3,2,1,0:T(8,128)(2,1)}, u32[]{:S(2)}, u32[]{:S(2)}) async-start(bf16[16,2,2,128,128]{4,3,2,1,0:T(8,128)(2,1)} %bitcast.15), calls=%async_computation.1 | async-start | bytes 4194304 | tf_op jit(solution)/shard_map/all_to_all | solution.py:654
  25.1 5.1 %collective-permute-start = (bf16[512,1024]{1,0:T(8,128)(2,1)S(1)}, bf16[512,1024]{1,0:T(8,128)(2,1)S(1)}, u32[]{:S(2)}, u32[]{:S(2)}) collective-permute-start(bf16[512,1024]{1,0:T(8,128)(2,1)S(1)} %copy-done.7), channel_id=1, source_target_pairs={{0,1},{1,0},{2,3},{3,2},{4,5},{5,4},{6,7},{7,6},{8,9},{9,8},{10,11... | collective-permute-start | bytes 3145736 | tf_op jit(solution)/shard_map/ppermute | solution.py:651
  30.1 1.0 %copy-start.8 = (bf16[512,1024]{1,0:T(8,128)(2,1)}, bf16[512,1024]{1,0:T(8,128)(2,1)S(1)}, u32[]{:S(2)}) copy-start(bf16[512,1024]{1,0:T(8,128)(2,1)S(1)} %collective-permute-done.other_ref) | copy-start | bytes 3145732
  31.1 26.5 %copy-start.1 = (bf16[768,2048]{1,0:T(8,128)(2,1)S(1)}, bf16[768,2048]{1,0:T(8,128)(2,1)}, u32[]{:S(2)}) copy-start(bf16[768,2048]{1,0:T(8,128)(2,1)} %weight_ref.2) | copy-start | bytes 9437188
  51.3 5.4 %collective-permute-start.1 = (f32[1,512]{1,0:T(1,128)}, f32[1,512]{1,0:T(1,128)S(1)}, u32[]{:S(2)}, u32[]{:S(2)}) collective-permute-start(f32[1,512]{1,0:T(1,128)} %get-tuple-element.29), channel_id=1, source_target_pairs={{0,1},{1,0},{2,3},{3,2},{4,5},{5,4},{6,7},{7,6},{8,9},{9,8},{10,11... | collective-permute-start | bytes 6152 | tf_op jit(solution)/shard_map/ppermute | solution.py:672
  57.6 1.1 %copy-start.5 = (bf16[512,768]{1,0:T(8,128)(2,1)S(1)}, bf16[512,768]{1,0:T(8,128)(2,1)}, u32[]{:S(2)}) copy-start(bf16[512,768]{1,0:T(8,128)(2,1)} %get-tuple-element.28.gated_ref) | copy-start | bytes 2359300
  60.6 1.3 %copy-start.2 = (f32[512,1024]{1,0:T(8,128)}, f32[512,1024]{1,0:T(8,128)S(1)}, u32[]{:S(2)}) copy-start(f32[512,1024]{1,0:T(8,128)S(1)} %get-tuple-element.30.part_hbm) | copy-start | bytes 6291460
  61.9 1.4 %copy-start.3 = (f32[512,1024]{1,0:T(8,128)}, f32[512,1024]{1,0:T(8,128)S(1)}, u32[]{:S(2)}) copy-start(f32[512,1024]{1,0:T(8,128)S(1)} %get-tuple-element.33.part_ref) | copy-start | bytes 6291460
  73.4 15.7 %copy-start = (bf16[512,2048]{1,0:T(8,128)(2,1)S(1)}, bf16[512,2048]{1,0:T(8,128)(2,1)}, u32[]{:S(2)}) copy-start(bf16[512,2048]{1,0:T(8,128)(2,1)} %weight_ref.3) | copy-start | bytes 6291460
  87.6 4.9 %collective-permute-start.2 = (bf16[512,1024]{1,0:T(8,128)(2,1)}, bf16[512,1024]{1,0:T(8,128)(2,1)S(1)}, u32[]{:S(2)}, u32[]{:S(2)}) collective-permute-start(bf16[512,1024]{1,0:T(8,128)(2,1)} %get-tuple-element.34), channel_id=1, source_target_pairs={{0,1},{1,0},{2,3},{3,2},{4,5},{5,4},{6,7},{7,6},{8,9},{9,8},{10,11... | collective-permute-start | bytes 3145736 | tf_op jit(solution)/shard_map/ppermute | solution.py:681
  89.1 1.6 %copy-start.4 = (f32[512,1024]{1,0:T(8,128)S(1)}, f32[512,1024]{1,0:T(8,128)}, u32[]{:S(2)}) copy-start(f32[512,1024]{1,0:T(8,128)} %copy-done.3) | copy-start | bytes 6291460
  90.7 1.0 %copy-start.6 = (bf16[512,512]{1,0:T(8,128)(2,1)S(1)}, bf16[512,512]{1,0:T(8,128)(2,1)}, u32[]{:S(2)}) copy-start(bf16[512,512]{1,0:T(8,128)(2,1)} %get-tuple-element.32.context_ref) | copy-start | bytes 1572868

commit v4 on v3

--- a/solution.py
+++ b/solution.py
@@ -83,7 +83,7 @@
 
 def gather_kernel(capacity, asked_hbm, pages_ref, out_ref, own_ref, asked, held, sem, sems_in, sems_out):
     me = lax.axis_index("req")
-    load = pltpu.make_async_copy(asked_hbm, asked, sem.at[0])
+    load = pltpu.make_async_copy(asked_hbm.at[:, 0:1, :], asked, sem.at[0])
     load.start()
     load.wait()
     count = held.shape[0]
@@ -120,7 +120,7 @@
         in_specs=[HBM, HBM],
         out_specs=(HBM, HBM),
         scratch_shapes=[
-            pltpu.SMEM(asked.shape, jnp.int32),
+            pltpu.SMEM((asked.shape[0], 1, asked.shape[2]), jnp.int32),
             pltpu.VMEM((count,) + page, kv_pages.dtype),
             pltpu.SemaphoreType.DMA((2,)),
             pltpu.SemaphoreType.DMA((count,)),
@@ -485,7 +485,7 @@
     rows, half = out_ref.shape
     heads = q_ref.shape[0] // rows
     per_chunk = CHUNK // tokens
-    now = [pltpu.make_async_copy(q_hbm, q_ref, sems.at[0])] + [
+    pages_in = [
         pltpu.make_async_copy(
             kv_hbm.at[pl.ds((me ^ mask) * capacity, capacity)],
             kv_ref.at[pl.ds(index * capacity, capacity)],
@@ -493,6 +493,7 @@
         )
         for index, mask in enumerate(masks)
     ]
+    queries_in = pltpu.make_async_copy(q_hbm, q_ref, sems.at[0])
     there = pl.ds(pl.multiple_of((1 - core_ref[0]) * half, half), half)
     late = [
         pltpu.make_async_copy(source, near.at[kind], sems_late.at[kind])
@@ -501,21 +502,31 @@
         pltpu.make_async_copy(weight_hbm.at[:, there], weight_ref, sems_late.at[3]),
         pltpu.make_async_copy(part_hbm, part_ref, sems_late.at[4]),
     ]
-    for copy in now:
+    seen = [seen_ref[(me ^ mask) * capacity + rank] for mask in masks for rank in range(capacity)]
+    ahead = max(2 * per_chunk // capacity, 1)
+    split = ahead * capacity
+    queries_in.start()
+    for copy in pages_in:
         copy.start()
-    seen = [seen_ref[(me ^ mask) * capacity + rank] for mask in masks for rank in range(capacity)]
-    for copy in now:
+    queries_in.wait()
+    for copy in pages_in[:ahead]:
         copy.wait()
-    for copy in late:
-        copy.start()
-    for head in range(heads):
-        here = slice(head * rows, (head + 1) * rows)
-        state = None
-        for begin in range(0, pages, per_chunk):
-            span = slice(begin, begin + per_chunk)
-            state = page_step(q_ref[here, :], kv_ref[span, 0], kv_ref[span, 1], seen[span], state)
-        for kind in range(3):
-            far[kind, here, :] = state[kind]
+    for first in (True, False):
+        if not first:
+            for copy in pages_in[ahead:]:
+                copy.wait()
+            for copy in late:
+                copy.start()
+        for head in range(heads):
+            here = slice(head * rows, (head + 1) * rows)
+            state = None if first else (far[0, here, :], far[1, here, :], far[2, here, :])
+            for begin in range(*((0, split) if first else (split, pages)), per_chunk):
+                span = slice(begin, min(begin + per_chunk, split if first else pages))
+                state = page_step(
+                    q_ref[here, :], kv_ref[span, 0], kv_ref[span, 1], seen[span], state
+                )
+            for kind in range(3):
+                far[kind, here, :] = state[kind]
     for copy in late:
         copy.wait()
     for head in range(heads):
@@ -562,8 +573,13 @@
     )(core, seen, queries, *state, weight, part, kv)
 
 
-def mixer_out_kernel(core_ref, gated_ref, scale_ref, weight_ref, theirs_ref, ours_ref):
+def mixer_out_kernel(
+    core_ref, gated_ref, scale_ref, weight_ref, attn_hbm, theirs_ref, ours_ref, attn_ref, sem
+):
     half = ours_ref.shape[1]
+    mine = pl.ds(pl.multiple_of(core_ref[0] * half, half), half)
+    cut = pltpu.make_async_copy(attn_hbm.at[:, mine], attn_ref, sem.at[0])
+    cut.start()
     for start in range(0, half, 256):
         for core, out_ref in ((1 - core_ref[0], theirs_ref), (core_ref[0], ours_ref)):
             here = pl.ds(pl.multiple_of(core * half + start, 256), 256)
@@ -571,45 +587,44 @@
                 jnp.dot(gated_ref[...], weight_ref[:, here], preferred_element_type=F32)
                 * scale_ref[...]
             )
-
-
-def mixer_out(core, gated, scale, weight):
+    cut.wait()
+
+
+def mixer_out(core, gated, scale, weight, attn_weight):
     rows, depth = gated.shape
     width = weight.shape[1]
     return pl.pallas_call(
         mixer_out_kernel,
-        out_shape=(jax.ShapeDtypeStruct((rows, width // 2), F32),) * 2,
-        in_specs=[SMEM] + [VMEM] * 3,
-        out_specs=(VMEM,) * 2,
+        out_shape=(jax.ShapeDtypeStruct((rows, width // 2), F32),) * 2
+        + (jax.ShapeDtypeStruct((attn_weight.shape[0], width // 2), BF16),),
+        in_specs=[SMEM] + [VMEM] * 3 + [HBM],
+        out_specs=(VMEM,) * 3,
+        scratch_shapes=[pltpu.SemaphoreType.DMA((1,))],
         compiler_params=params(16),
         cost_estimate=LIGHT,
         name="mixer_out",
-    )(core, gated, scale, weight)
-
-
-def ours_kernel(core_ref, context_ref, weight_ref, part_ref, out_ref):
-    half = out_ref.shape[1]
-    for start in range(0, half, 256):
-        here = pl.ds(pl.multiple_of(core_ref[0] * half + start, 256), 256)
+    )(core, gated, scale, weight, attn_weight)
+
+
+def ours_kernel(context_ref, weight_ref, part_ref, out_ref):
+    for start in range(0, out_ref.shape[1], 256):
         tile = slice(start, start + 256)
         out_ref[:, tile] = (
-            jnp.dot(context_ref[...], weight_ref[:, here], preferred_element_type=F32)
+            jnp.dot(context_ref[...], weight_ref[:, tile], preferred_element_type=F32)
             + part_ref[:, tile]
-        )
-
-
-def ours_half(core, context, weight, part):
-    rows, depth = context.shape
-    half = weight.shape[1] // 2
+        ).astype(BF16)
+
+
+def ours_half(context, weight, part):
     return pl.pallas_call(
         ours_kernel,
-        out_shape=jax.ShapeDtypeStruct((rows, half), F32),
-        in_specs=[SMEM] + [VMEM] * 3,
+        out_shape=jax.ShapeDtypeStruct(part.shape, BF16),
+        in_specs=[VMEM] * 3,
         out_specs=VMEM,
         compiler_params=params(16),
         cost_estimate=LIGHT,
         name="ours_half",
-    )(core, context, weight, part)
+    )(context, weight, part)
 
 
 def shards(
@@ -671,7 +686,7 @@
     )
     total = squares + lax.ppermute(squares, "tp", swap)
     scale = lax.rsqrt(total.reshape((row_count, 1)) / DSSM + EPSILON)
-    part_theirs, part_ours = mixer_out(core, gated, scale, w_mixer_out)
+    part_theirs, part_ours, weight_ours = mixer_out(core, gated, scale, w_mixer_out, w_attn_out)
     state = attend_early(
         seen, queries, (fresh_keys, fresh_values), row_count, [own], [0], [(0, None)]
     )
@@ -679,8 +694,8 @@
         core, seen, queries, state, w_attn_out, part_theirs, arrived, list(range(1, devices))
     )
     received = lax.ppermute(theirs, "tp", swap)
-    ours = ours_half(core, context, w_attn_out, part_ours)
-    mixed = (ours + received.astype(F32)).astype(BF16)
+    ours = ours_half(context, weight_ours, part_ours)
+    mixed = (ours.astype(F32) + received.astype(F32)).astype(BF16)
     return (mixed, last_state.reshape(ssm_state.shape))
 
 

time: 94.8 us -> 93.3 us (0.984)
  waiting for transfers between devices: 10.1 us -> 8.78 us
  Pallas kernels: 48.8 us -> 47.7 us
    all_to_all x1, waiting for transfers between devices: 10.1 us -> 8.05 us  [exchange(): lax.all_to_all(blocks, 'req', split_axis=0, concat_axis=0, tiled=True)]
    pallas_call x1, Pallas kernels: 5.02 us -> 3.69 us  [gather_pages(): pl.pallas_call(functools.partial(gather_kernel, capacity), out_shape=(jax...]
    all_to_all x1, starting transfers between devices: 5.86 us -> 6.84 us  [exchange(): lax.all_to_all(blocks, 'req', split_axis=0, concat_axis=0, tiled=True)]
  transfers between devices with their start and end apart: 4 -> 4, of which waited for: 1 -> 2; matrix products, arithmetic and copies ran while one was open for 4% -> 4% of each run, Pallas kernels for 30% -> 30%
where the time goes in v4:
time: 93.3 us; the launch traced here: 92.7 us
  Pallas kernels  47.7 us (51%)
  blocking collectives  11.3 us (12%)
  starting transfers between devices  10.9 us (12%)
  waiting for transfers between devices  8.78 us (9%)
  local copies, waits for them, and re-layouts  8.47 us (9%)
  other arithmetic  4.09 us (4%)
  between operations  1.41 us (2%)
    pallas_call x1, Pallas kernels, front(): pl.pallas_call(front_kernel, out_shape=(out((wq.shape[1] // HEAD_SIZE * r...  20.2 us
    pallas_call x1, Pallas kernels, attend_late(): pl.pallas_call(functools.partial(attend_late_kernel, masks), out_shape=(j...  14.2 us
    all_to_all x1, blocking collectives, exchange(): lax.all_to_all(blocks, 'req', split_axis=0, concat_axis=0, tiled=True)  11.3 us
    all_to_all x1, waiting for transfers between devices, exchange(): lax.all_to_all(blocks, 'req', split_axis=0, concat_axis=0, tiled=True)  8.05 us
    unnamed x20, local copies, waits for them, and re-layouts  7.75 us
    all_to_all x1, starting transfers between devices, exchange(): lax.all_to_all(blocks, 'req', split_axis=0, concat_axis=0, tiled=True)  6.84 us
    pallas_call x1, Pallas kernels, attend_early(): pl.pallas_call(functools.partial(attend_early_kernel, masks, picks, fresh...  5.04 us
    pallas_call x1, Pallas kernels, gather_pages(): pl.pallas_call(functools.partial(gather_kernel, capacity), out_shape=(jax...  3.69 us
  transfers between devices with their start and end apart: 4, of which 2 were waited for; matrix products, arithmetic and copies ran while one was open for 4% of the time, Pallas kernels for 30%

profile of v4, /device:TPU:13, one launch (start us, length us, event | category | flops | bytes accessed | tf_op | source)
XLA Modules:
  0.0 92.7 jit_solution(11832641578262467453)
XLA Ops:
  1.3 1.6 %wanted.1 = (s32[16,8,128]{2,1,0:T(8,128)}, s32[32]{0:T(128)}) custom-call(s32[1,32]{1,0:T(1,128)} %table_ref.1, s32[1]{0:T(128)} %copy.26.length_ref), custom_call_target="tpu_custom_call" | custom-call | tf_op jit(solution)/shard_map/wanted/pallas_call | solution.py:68
  2.9 11.3 %all_to_all.10.asked_hbm = s32[16,8,128]{2,1,0:T(8,128)} all-to-all(s32[16,8,128]{2,1,0:T(8,128)} %get-tuple-element.24), channel_id=1, replica_groups=mesh['req'=16,'tp'=2] {'req'}, dimensions={0} | all-to-all | bytes 131072 | tf_op jit(solution)/shard_map/all_to_all | solution.py:669
  14.1 3.7 %gather_pages.1 = (bf16[32,2,128,128]{3,2,1,0:T(8,128)(2,1)}, bf16[2,2,128,128]{3,2,1,0:T(8,128)(2,1)}) custom-call(s32[16,8,128]{2,1,0:T(8,128)} %all_to_all.10.asked_hbm, bf16[32,2,128,128]{3,2,1,0:T(8,128)(2,1)} %bitcast.14), custom_call_target="tpu_custom_call" | custom-call | flops 1000000 | bytes 10000 | tf_op jit(solution)/shard_map/gather_pages/pallas_call | solution.py:114
  17.9 6.8 %all-to-all-start.1 = ((bf16[16,2,2,128,128]{4,3,2,1,0:T(8,128)(2,1)}), bf16[16,2,2,128,128]{4,3,2,1,0:T(8,128)(2,1)}, u32[]{:S(2)}, u32[]{:S(2)}) async-start(bf16[16,2,2,128,128]{4,3,2,1,0:T(8,128)(2,1)} %bitcast.15), calls=%async_computation.1 | async-start | bytes 4194304 | tf_op jit(solution)/shard_map/all_to_all | solution.py:669
  24.7 2.5 %collective-permute-start = (bf16[512,1024]{1,0:T(8,128)(2,1)S(1)}, bf16[512,1024]{1,0:T(8,128)(2,1)S(1)}, u32[]{:S(2)}, u32[]{:S(2)}) collective-permute-start(bf16[512,1024]{1,0:T(8,128)(2,1)S(1)} %copy-done.7), channel_id=1, source_target_pairs={{0,1},{1,0},{2,3},{3,2},{4,5},{5,4},{6,7},{7,6},{8,9},{9,8},{10,11... | collective-permute-start | bytes 3145736 | tf_op jit(solution)/shard_map/ppermute | solution.py:666
  27.2 0.6 broadcast_in_dim.17.mixer_gain_ref
  27.8 1.0 %fusion = (f32[512,64]{1,0:T(8,128)S(1)}, f32[512,64]{1,0:T(8,128)S(1)}, f32[512,64]{1,0:T(8,128)S(1)}) fusion(f32[64]{0:T(128)S(1)} %multiply_power_fusion, f32[512]{0:T(512)S(1)} %add_convert_fusion.1), kind=kLoop, calls=%fused_computation.5 | loop fusion | flops 65536 | bytes 395520 | tf_op jit(solution)/shard_map/neg | solution.py:40
  28.8 1.0 %pad_maximum_fusion = (f32[512,128]{1,0:T(8,128)}, f32[512,128]{1,0:T(8,128)}) fusion(f32[512,64]{1,0:T(8,128)S(1)} %get-tuple-element.40, f32[512,64]{1,0:T(8,128)S(1)} %get-tuple-element.39, f32[512,64]{1,0:T(8,128)S(1)} %get-tuple-element.38), kind=kLoop, calls=%fused_computation.3 | loop fusion | flops 131072 | bytes 917504 | tf_op jit(solution)/shard_map/concatenate | solution.py:39
  29.8 1.0 %copy-done.8 = bf16[512,1024]{1,0:T(8,128)(2,1)} copy-done((bf16[512,1024]{1,0:T(8,128)(2,1)}, bf16[512,1024]{1,0:T(8,128)(2,1)S(1)}, u32[]{:S(2)}) %copy-start.8) | copy-done | bytes 1048600
  30.8 20.2 %front.1 = (bf16[2048,128]{1,0:T(8,128)(2,1)}, bf16[512,128]{1,0:T(8,128)(2,1)}, bf16[512,128]{1,0:T(8,128)(2,1)}, bf16[512,768]{1,0:T(8,128)(2,1)}, f32[1,512]{1,0:T(1,128)}, /*index=5*/f32[768,256]{1,0:T(8,128)}) custom-call(s32[1]{0:T(128)} %bitcast.core_ref, bf16[512,1024]{1,0:T(8,128)(2,1)} %mine_ref.1, bf16[512,1024]{1,0:T(8,128)(2,1)} %copy-done.8, ...), custom_call_target="tpu_custom_call" | custom-call | flops 1000000 | bytes 10000 | tf_op jit(solution)/shard_map/front/pallas_call | solution.py:321
  51.1 5.0 %attend_first.1 = (f32[2048,128]{1,0:T(8,128)}, f32[2048,128]{1,0:T(8,128)}, f32[2048,128]{1,0:T(8,128)}) custom-call(s32[32]{0:T(128)} %get-tuple-element.20.seen_ref, bf16[2048,128]{1,0:T(8,128)(2,1)} %get-tuple-element.21.q_hbm, bf16[512,128]{1,0:T(8,128)(2,1)} %get-tuple-element.22.refs_0_, bf16[512,128]{1,0:T(8,128)(2,1)} %get-tuple-element.23.refs_1_, ...), custom_call_target="tpu_custom_call" | custom-call | flops 1000000 | bytes 10000 | tf_op jit(solution)/shard_map/attend_first/pallas_call | solution.py:458
  56.2 0.7 rsqrt_bitcast_fusion
  57.0 1.9 %copy-done.1 = bf16[768,2048]{1,0:T(8,128)(2,1)S(1)} copy-done((bf16[768,2048]{1,0:T(8,128)(2,1)S(1)}, bf16[768,2048]{1,0:T(8,128)(2,1)}, u32[]{:S(2)}) %copy-start.1) | copy-done | bytes 3145752
  58.9 1.1 %copy-done.5 = bf16[512,768]{1,0:T(8,128)(2,1)S(1)} copy-done((bf16[512,768]{1,0:T(8,128)(2,1)S(1)}, bf16[512,768]{1,0:T(8,128)(2,1)}, u32[]{:S(2)}) %copy-start.5) | copy-done | bytes 786456
  60.0 2.3 %mixer_out.1 = (f32[512,1024]{1,0:T(8,128)S(1)}, f32[512,1024]{1,0:T(8,128)S(1)}, bf16[512,1024]{1,0:T(8,128)(2,1)S(1)}) custom-call(s32[1]{0:T(128)} %bitcast.core_ref, bf16[512,768]{1,0:T(8,128)(2,1)S(1)} %copy-done.5, f32[512,1]{1,0:T(8,128)S(1)} %copy.25.scale_ref, bf16[768,2048]{1,0:T(8,128)(2,1)S(1)} %copy-done.1, bf16[512,2048]{1,0:T(8,128)(2,1)S(1)} %copy-done), custom_call_target="tpu_custom_call" | custom-call | flops 1000000 | bytes 10000 | tf_op jit(solution)/shard_map/mixer_out/pallas_call | solution.py:596
  62.3 1.3 %copy-done.2 = f32[512,1024]{1,0:T(8,128)} copy-done((f32[512,1024]{1,0:T(8,128)}, f32[512,1024]{1,0:T(8,128)S(1)}, u32[]{:S(2)}) %copy-start.2) | copy-done | bytes 2097176
  63.7 1.4 %copy-done.3 = f32[512,1024]{1,0:T(8,128)} copy-done((f32[512,1024]{1,0:T(8,128)}, f32[512,1024]{1,0:T(8,128)S(1)}, u32[]{:S(2)}) %copy-start.3) | copy-done | bytes 2097176
  65.0 8.0 %all-to-all-done.1 = bf16[16,2,2,128,128]{4,3,2,1,0:T(8,128)(2,1)} async-done(((bf16[16,2,2,128,128]{4,3,2,1,0:T(8,128)(2,1)}), bf16[16,2,2,128,128]{4,3,2,1,0:T(8,128)(2,1)}, u32[]{:S(2)}, u32[]{:S(2)}) %all-to-all-start.1) | async-done | bytes 2097184 | tf_op jit(solution)/shard_map/all_to_all | solution.py:669
  73.1 14.2 %attend_late.1 = (bf16[512,512]{1,0:T(8,128)(2,1)}, bf16[512,1024]{1,0:T(8,128)(2,1)}) custom-call(s32[1]{0:T(128)} %bitcast.core_ref, s32[32]{0:T(128)} %get-tuple-element.20.seen_ref, bf16[2048,128]{1,0:T(8,128)(2,1)} %get-tuple-element.21.q_hbm, f32[2048,128]{1,0:T(8,128)} %get-tuple-element.26.sum_hbm, f32[2048,128]{1,0:T(8,128)} %get-tuple-element.27.total_hbm, ...), custom_call_target="tpu_custom_call" | custom-call | flops 1000000 | bytes 10000 | tf_op jit(solution)/shard_map/attend_late/pallas_call | solution.py:552
  87.3 1.5 %collective-permute-start.2 = (bf16[512,1024]{1,0:T(8,128)(2,1)}, bf16[512,1024]{1,0:T(8,128)(2,1)S(1)}, u32[]{:S(2)}, u32[]{:S(2)}) collective-permute-start(bf16[512,1024]{1,0:T(8,128)(2,1)} %get-tuple-element.36), channel_id=1, source_target_pairs={{0,1},{1,0},{2,3},{3,2},{4,5},{5,4},{6,7},{7,6},{8,9},{9,8},{10,11... | collective-permute-start | bytes 3145736 | tf_op jit(solution)/shard_map/ppermute | solution.py:696
  88.8 1.0 %copy-done.6 = bf16[512,512]{1,0:T(8,128)(2,1)S(1)} copy-done((bf16[512,512]{1,0:T(8,128)(2,1)S(1)}, bf16[512,512]{1,0:T(8,128)(2,1)}, u32[]{:S(2)}) %copy-start.6) | copy-done | bytes 524312
  89.9 0.7 ours_half.1
  90.6 0.7 collective-permute-done.2
  91.3 1.4 %add_convert_fusion = bf16[512,1024]{1,0:T(8,128)(2,1)} fusion(bf16[512,1024]{1,0:T(8,128)(2,1)S(1)} %collective-permute-done.2, bf16[512,1024]{1,0:T(8,128)(2,1)S(1)} %ours_half.1), kind=kLoop, calls=%fused_computation | loop fusion | flops 2097152 | bytes 3145728 | tf_op jit(solution)/shard_map/convert_element_type | solution.py:698
  (20 shorter events, 0.3 us)
Async XLA Ops:
  17.8 6.9 %copy-start.7 = (bf16[512,1024]{1,0:T(8,128)(2,1)S(1)}, bf16[512,1024]{1,0:T(8,128)(2,1)}, u32[]{:S(2)}) copy-start(bf16[512,1024]{1,0:T(8,128)(2,1)} %mine_ref.1) | copy-start | bytes 3145732
  17.9 9.3 %copy-start.9 = (f32[768]{0:T(1024)S(1)}, f32[768]{0:T(1024)}, u32[]{:S(2)}) copy-start(f32[768]{0:T(1024)} %param.43) | copy-start | bytes 9220
  17.9 55.2 %all-to-all-start.1 = ((bf16[16,2,2,128,128]{4,3,2,1,0:T(8,128)(2,1)}), bf16[16,2,2,128,128]{4,3,2,1,0:T(8,128)(2,1)}, u32[]{:S(2)}, u32[]{:S(2)}) async-start(bf16[16,2,2,128,128]{4,3,2,1,0:T(8,128)(2,1)} %bitcast.15), calls=%async_computation.1 | async-start | bytes 4194304 | tf_op jit(solution)/shard_map/all_to_all | solution.py:669
  24.7 5.1 %collective-permute-start = (bf16[512,1024]{1,0:T(8,128)(2,1)S(1)}, bf16[512,1024]{1,0:T(8,128)(2,1)S(1)}, u32[]{:S(2)}, u32[]{:S(2)}) collective-permute-start(bf16[512,1024]{1,0:T(8,128)(2,1)S(1)} %copy-done.7), channel_id=1, source_target_pairs={{0,1},{1,0},{2,3},{3,2},{4,5},{5,4},{6,7},{7,6},{8,9},{9,8},{10,11... | collective-permute-start | bytes 3145736 | tf_op jit(solution)/shard_map/ppermute | solution.py:666
  29.8 1.0 %copy-start.8 = (bf16[512,1024]{1,0:T(8,128)(2,1)}, bf16[512,1024]{1,0:T(8,128)(2,1)S(1)}, u32[]{:S(2)}) copy-start(bf16[512,1024]{1,0:T(8,128)(2,1)S(1)} %collective-permute-done.other_ref) | copy-start | bytes 3145732
  30.8 26.3 %copy-start = (bf16[512,2048]{1,0:T(8,128)(2,1)S(1)}, bf16[512,2048]{1,0:T(8,128)(2,1)}, u32[]{:S(2)}) copy-start(bf16[512,2048]{1,0:T(8,128)(2,1)} %weight_hbm.1) | copy-start | bytes 6291460
  51.0 5.2 %collective-permute-start.1 = (f32[1,512]{1,0:T(1,128)}, f32[1,512]{1,0:T(1,128)S(1)}, u32[]{:S(2)}, u32[]{:S(2)}) collective-permute-start(f32[1,512]{1,0:T(1,128)} %get-tuple-element.30), channel_id=1, source_target_pairs={{0,1},{1,0},{2,3},{3,2},{4,5},{5,4},{6,7},{7,6},{8,9},{9,8},{10,11... | collective-permute-start | bytes 6152 | tf_op jit(solution)/shard_map/ppermute | solution.py:687
  57.0 1.9 %copy-start.1 = (bf16[768,2048]{1,0:T(8,128)(2,1)S(1)}, bf16[768,2048]{1,0:T(8,128)(2,1)}, u32[]{:S(2)}) copy-start(bf16[768,2048]{1,0:T(8,128)(2,1)} %weight_ref.1) | copy-start | bytes 9437188
  58.9 1.1 %copy-start.5 = (bf16[512,768]{1,0:T(8,128)(2,1)S(1)}, bf16[512,768]{1,0:T(8,128)(2,1)}, u32[]{:S(2)}) copy-start(bf16[512,768]{1,0:T(8,128)(2,1)} %get-tuple-element.29.gated_ref) | copy-start | bytes 2359300
  62.3 1.3 %copy-start.2 = (f32[512,1024]{1,0:T(8,128)}, f32[512,1024]{1,0:T(8,128)S(1)}, u32[]{:S(2)}) copy-start(f32[512,1024]{1,0:T(8,128)S(1)} %get-tuple-element.31.part_hbm) | copy-start | bytes 6291460
  63.7 1.4 %copy-start.3 = (f32[512,1024]{1,0:T(8,128)}, f32[512,1024]{1,0:T(8,128)S(1)}, u32[]{:S(2)}) copy-start(f32[512,1024]{1,0:T(8,128)S(1)} %get-tuple-element.35.part_ref) | copy-start | bytes 6291460
  73.1 15.7 %copy-start.4 = (f32[512,1024]{1,0:T(8,128)S(1)}, f32[512,1024]{1,0:T(8,128)}, u32[]{:S(2)}) copy-start(f32[512,1024]{1,0:T(8,128)} %copy-done.3) | copy-start | bytes 6291460
  87.3 4.0 %collective-permute-start.2 = (bf16[512,1024]{1,0:T(8,128)(2,1)}, bf16[512,1024]{1,0:T(8,128)(2,1)S(1)}, u32[]{:S(2)}, u32[]{:S(2)}) collective-permute-start(bf16[512,1024]{1,0:T(8,128)(2,1)} %get-tuple-element.36), channel_id=1, source_target_pairs={{0,1},{1,0},{2,3},{3,2},{4,5},{5,4},{6,7},{7,6},{8,9},{9,8},{10,11... | collective-permute-start | bytes 3145736 | tf_op jit(solution)/shard_map/ppermute | solution.py:696
  88.8 1.0 %copy-start.6 = (bf16[512,512]{1,0:T(8,128)(2,1)S(1)}, bf16[512,512]{1,0:T(8,128)(2,1)}, u32[]{:S(2)}) copy-start(bf16[512,512]{1,0:T(8,128)(2,1)} %get-tuple-element.33.context_ref) | copy-start | bytes 1572868

commit v5 on v4

--- a/solution.py
+++ b/solution.py
@@ -68,7 +68,7 @@
     return pl.pallas_call(
         functools.partial(want_kernel, pages_dev, capacity, page_size),
         out_shape=(
-            jax.ShapeDtypeStruct((devices, 8, 128), jnp.int32),
+            jax.ShapeDtypeStruct((devices, 1, 128), jnp.int32),
             jax.ShapeDtypeStruct((devices * capacity,), jnp.int32),
         ),
         in_specs=[SMEM, SMEM],
@@ -83,7 +83,7 @@
 
 def gather_kernel(capacity, asked_hbm, pages_ref, out_ref, own_ref, asked, held, sem, sems_in, sems_out):
     me = lax.axis_index("req")
-    load = pltpu.make_async_copy(asked_hbm.at[:, 0:1, :], asked, sem.at[0])
+    load = pltpu.make_async_copy(asked_hbm, asked, sem.at[0])
     load.start()
     load.wait()
     count = held.shape[0]
@@ -95,10 +95,12 @@
         )
         reads[-1].start()
     writes = []
-    for index in range(count):
-        reads[index].wait()
+    for request in range(count // capacity):
+        block = pl.ds(request * capacity, capacity)
+        for read in reads[request * capacity : (request + 1) * capacity]:
+            read.wait()
         writes.append(
-            pltpu.make_async_copy(held.at[index], out_ref.at[index], sems_out.at[index])
+            pltpu.make_async_copy(held.at[block], out_ref.at[block], sems_out.at[request])
         )
         writes[-1].start()
     mine = pltpu.make_async_copy(held.at[pl.ds(me * capacity, capacity)], own_ref, sem.at[1])
@@ -120,11 +122,11 @@
         in_specs=[HBM, HBM],
         out_specs=(HBM, HBM),
         scratch_shapes=[
-            pltpu.SMEM((asked.shape[0], 1, asked.shape[2]), jnp.int32),
+            pltpu.SMEM(asked.shape, jnp.int32),
             pltpu.VMEM((count,) + page, kv_pages.dtype),
             pltpu.SemaphoreType.DMA((2,)),
             pltpu.SemaphoreType.DMA((count,)),
-            pltpu.SemaphoreType.DMA((count,)),
+            pltpu.SemaphoreType.DMA((asked.shape[0],)),
         ],
         compiler_params=params(60),
         cost_estimate=LIGHT,
@@ -476,7 +478,7 @@
 
 
 def attend_late_kernel(
-    masks, core_ref, seen_ref, q_hbm, sum_hbm, total_hbm, top_hbm, weight_hbm, part_hbm, kv_hbm,
+    masks, seen_ref, q_hbm, sum_hbm, total_hbm, top_hbm, weight_hbm, part_hbm, kv_hbm,
     context_ref, out_ref, q_ref, near, far, kv_ref, weight_ref, part_ref, sems, sems_late,
 ):
     pages, _, tokens, _ = kv_ref.shape
@@ -494,7 +496,7 @@
         for index, mask in enumerate(masks)
     ]
     queries_in = pltpu.make_async_copy(q_hbm, q_ref, sems.at[0])
-    there = pl.ds(pl.multiple_of((1 - core_ref[0]) * half, half), half)
+    there = pl.ds(pl.multiple_of((1 - lax.axis_index("tp")) * half, half), half)
     late = [
         pltpu.make_async_copy(source, near.at[kind], sems_late.at[kind])
         for kind, source in enumerate((sum_hbm, total_hbm, top_hbm))
@@ -505,37 +507,34 @@
     seen = [seen_ref[(me ^ mask) * capacity + rank] for mask in masks for rank in range(capacity)]
     ahead = max(2 * per_chunk // capacity, 1)
     split = ahead * capacity
-    queries_in.start()
-    for copy in pages_in:
+    for copy in [queries_in] + pages_in:
         copy.start()
-    queries_in.wait()
-    for copy in pages_in[:ahead]:
+    for copy in [queries_in] + pages_in[:ahead]:
         copy.wait()
-    for first in (True, False):
-        if not first:
-            for copy in pages_in[ahead:]:
-                copy.wait()
-            for copy in late:
-                copy.start()
-        for head in range(heads):
-            here = slice(head * rows, (head + 1) * rows)
-            state = None if first else (far[0, here, :], far[1, here, :], far[2, here, :])
-            for begin in range(*((0, split) if first else (split, pages)), per_chunk):
-                span = slice(begin, min(begin + per_chunk, split if first else pages))
-                state = page_step(
-                    q_ref[here, :], kv_ref[span, 0], kv_ref[span, 1], seen[span], state
-                )
-            for kind in range(3):
-                far[kind, here, :] = state[kind]
     for copy in late:
+        copy.start()
+
+    def steps(head, begin, end, state):
+        query = q_ref[head * rows : (head + 1) * rows, :]
+        for start in range(begin, end, per_chunk):
+            span = slice(start, min(start + per_chunk, end))
+            state = page_step(query, kv_ref[span, 0], kv_ref[span, 1], seen[span], state)
+        return state
+
+    for head in range(heads):
+        state = steps(head, 0, split, None)
+        for kind in range(3):
+            far[kind, head * rows : (head + 1) * rows, :] = state[kind]
+    for copy in pages_in[ahead:] + late:
         copy.wait()
     for head in range(heads):
         here = slice(head * rows, (head + 1) * rows)
-        top = jnp.maximum(near[2, here, :], far[2, here, :])
+        state = steps(head, split, pages, (far[0, here, :], far[1, here, :], far[2, here, :]))
+        top = jnp.maximum(near[2, here, :], state[2])
         fade_near = jnp.exp2((near[2, here, :] - top) * SCORE_SCALE)
-        fade_far = jnp.exp2((far[2, here, :] - top) * SCORE_SCALE)
-        summed = near[0, here, :] * fade_near + far[0, here, :] * fade_far
-        total = near[1, here, :] * fade_near + far[1, here, :] * fade_far
+        fade_far = jnp.exp2((state[2] - top) * SCORE_SCALE)
+        summed = near[0, here, :] * fade_near + state[0] * fade_far
+        total = near[1, here, :] * fade_near + state[1] * fade_far
         context_ref[:, head * HEAD_SIZE : (head + 1) * HEAD_SIZE] = (summed / total).astype(BF16)
     for start in range(0, half, 256):
         tile = slice(start, start + 256)
@@ -545,7 +544,7 @@
         ).astype(BF16)
 
 
-def attend_late(core, seen, queries, state, weight, part, kv, masks):
+def attend_late(seen, queries, state, weight, part, kv, masks):
     rows, half = part.shape
     count = queries.shape[0]
     pages = len(masks) * kv.shape[0] // lax.axis_size("req")
@@ -555,7 +554,7 @@
             jax.ShapeDtypeStruct((rows, count // rows * HEAD_SIZE), BF16),
             jax.ShapeDtypeStruct((rows, half), BF16),
         ),
-        in_specs=[SMEM] * 2 + [HBM] * 7,
+        in_specs=[SMEM] + [HBM] * 7,
         out_specs=(VMEM, VMEM),
         scratch_shapes=[
             pltpu.VMEM(queries.shape, BF16),
@@ -570,7 +569,7 @@
         compiler_params=params(60),
         cost_estimate=LIGHT,
         name="attend_late",
-    )(core, seen, queries, *state, weight, part, kv)
+    )(seen, queries, *state, weight, part, kv)
 
 
 def mixer_out_kernel(
@@ -691,7 +690,7 @@
         seen, queries, (fresh_keys, fresh_values), row_count, [own], [0], [(0, None)]
     )
     context, theirs = attend_late(
-        core, seen, queries, state, w_attn_out, part_theirs, arrived, list(range(1, devices))
+        seen, queries, state, w_attn_out, part_theirs, arrived, list(range(1, devices))
     )
     received = lax.ppermute(theirs, "tp", swap)
     ours = ours_half(context, weight_ours, part_ours)

time: 93.3 us -> 92.3 us (0.989)
  transfers between devices with their start and end apart: 4 -> 4, of which waited for: 2 -> 2; matrix products, arithmetic and copies ran while one was open for 4% -> 4% of each run, Pallas kernels for 30% -> 31%
where the time goes in v5:
time: 92.3 us; the launch traced here: 91.9 us
  Pallas kernels  48 us (52%)
  blocking collectives  10.8 us (12%)
  starting transfers between devices  10.5 us (11%)
  waiting for transfers between devices  8.61 us (9%)
  local copies, waits for them, and re-layouts  8.47 us (9%)
  other arithmetic  4.09 us (4%)
  between operations  1.41 us (2%)
    pallas_call x1, Pallas kernels, front(): pl.pallas_call(front_kernel, out_shape=(out((wq.shape[1] // HEAD_SIZE * r...  20.2 us
    pallas_call x1, Pallas kernels, attend_late(): pl.pallas_call(functools.partial(attend_late_kernel, masks), out_shape=(j...  14.2 us
    all_to_all x1, blocking collectives, exchange(): lax.all_to_all(blocks, 'req', split_axis=0, concat_axis=0, tiled=True)  10.8 us
    all_to_all x1, waiting for transfers between devices, exchange(): lax.all_to_all(blocks, 'req', split_axis=0, concat_axis=0, tiled=True)  7.87 us
    unnamed x20, local copies, waits for them, and re-layouts  7.75 us
    all_to_all x1, starting transfers between devices, exchange(): lax.all_to_all(blocks, 'req', split_axis=0, concat_axis=0, tiled=True)  6.2 us
    pallas_call x1, Pallas kernels, attend_early(): pl.pallas_call(functools.partial(attend_early_kernel, masks, picks, fresh...  5.05 us
    pallas_call x1, Pallas kernels, gather_pages(): pl.pallas_call(functools.partial(gather_kernel, capacity), out_shape=(jax...  4.05 us
  transfers between devices with their start and end apart: 4, of which 2 were waited for; matrix products, arithmetic and copies ran while one was open for 4% of the time, Pallas kernels for 31%

profile of v5, /device:TPU:13, one launch (start us, length us, event | category | flops | bytes accessed | tf_op | source)
XLA Modules:
  0.0 91.9 jit_solution(506904044649807625)
XLA Ops:
  1.3 1.5 %wanted.1 = (s32[16,1,128]{2,1,0:T(1,128)}, s32[32]{0:T(128)}) custom-call(s32[1,32]{1,0:T(1,128)} %table_ref.1, s32[1]{0:T(128)} %copy.26.length_ref), custom_call_target="tpu_custom_call" | custom-call | tf_op jit(solution)/shard_map/wanted/pallas_call | solution.py:68
  2.8 10.8 %all_to_all.10.asked_hbm = s32[16,1,128]{2,1,0:T(1,128)} all-to-all(s32[16,1,128]{2,1,0:T(1,128)} %get-tuple-element.24), channel_id=1, replica_groups=mesh['req'=16,'tp'=2] {'req'}, dimensions={0} | all-to-all | bytes 16384 | tf_op jit(solution)/shard_map/all_to_all | solution.py:668
  13.6 4.0 %gather_pages.1 = (bf16[32,2,128,128]{3,2,1,0:T(8,128)(2,1)}, bf16[2,2,128,128]{3,2,1,0:T(8,128)(2,1)}) custom-call(s32[16,1,128]{2,1,0:T(1,128)} %all_to_all.10.asked_hbm, bf16[32,2,128,128]{3,2,1,0:T(8,128)(2,1)} %bitcast.14), custom_call_target="tpu_custom_call" | custom-call | flops 1000000 | bytes 10000 | tf_op jit(solution)/shard_map/gather_pages/pallas_call | solution.py:116
  17.7 6.2 %all-to-all-start.1 = ((bf16[16,2,2,128,128]{4,3,2,1,0:T(8,128)(2,1)}), bf16[16,2,2,128,128]{4,3,2,1,0:T(8,128)(2,1)}, u32[]{:S(2)}, u32[]{:S(2)}) async-start(bf16[16,2,2,128,128]{4,3,2,1,0:T(8,128)(2,1)} %bitcast.15), calls=%async_computation.1 | async-start | bytes 4194304 | tf_op jit(solution)/shard_map/all_to_all | solution.py:668
  23.9 2.6 %collective-permute-start = (bf16[512,1024]{1,0:T(8,128)(2,1)S(1)}, bf16[512,1024]{1,0:T(8,128)(2,1)S(1)}, u32[]{:S(2)}, u32[]{:S(2)}) collective-permute-start(bf16[512,1024]{1,0:T(8,128)(2,1)S(1)} %copy-done.7), channel_id=1, source_target_pairs={{0,1},{1,0},{2,3},{3,2},{4,5},{5,4},{6,7},{7,6},{8,9},{9,8},{10,11... | collective-permute-start | bytes 3145736 | tf_op jit(solution)/shard_map/ppermute | solution.py:665
  26.5 0.6 broadcast_in_dim.17.mixer_gain_ref
  27.1 1.0 %fusion = (f32[512,64]{1,0:T(8,128)S(1)}, f32[512,64]{1,0:T(8,128)S(1)}, f32[512,64]{1,0:T(8,128)S(1)}) fusion(f32[64]{0:T(128)S(1)} %multiply_power_fusion, f32[512]{0:T(512)S(1)} %add_convert_fusion.1), kind=kLoop, calls=%fused_computation.5 | loop fusion | flops 65536 | bytes 395520 | tf_op jit(solution)/shard_map/neg | solution.py:40
  28.1 1.0 %pad_maximum_fusion = (f32[512,128]{1,0:T(8,128)}, f32[512,128]{1,0:T(8,128)}) fusion(f32[512,64]{1,0:T(8,128)S(1)} %get-tuple-element.40, f32[512,64]{1,0:T(8,128)S(1)} %get-tuple-element.39, f32[512,64]{1,0:T(8,128)S(1)} %get-tuple-element.38), kind=kLoop, calls=%fused_computation.3 | loop fusion | flops 131072 | bytes 917504 | tf_op jit(solution)/shard_map/concatenate | solution.py:39
  29.1 1.0 %copy-done.8 = bf16[512,1024]{1,0:T(8,128)(2,1)} copy-done((bf16[512,1024]{1,0:T(8,128)(2,1)}, bf16[512,1024]{1,0:T(8,128)(2,1)S(1)}, u32[]{:S(2)}) %copy-start.8) | copy-done | bytes 1048600
  30.1 20.2 %front.1 = (bf16[2048,128]{1,0:T(8,128)(2,1)}, bf16[512,128]{1,0:T(8,128)(2,1)}, bf16[512,128]{1,0:T(8,128)(2,1)}, bf16[512,768]{1,0:T(8,128)(2,1)}, f32[1,512]{1,0:T(1,128)}, /*index=5*/f32[768,256]{1,0:T(8,128)}) custom-call(s32[1]{0:T(128)} %bitcast.core_ref, bf16[512,1024]{1,0:T(8,128)(2,1)} %mine_ref.1, bf16[512,1024]{1,0:T(8,128)(2,1)} %copy-done.8, ...), custom_call_target="tpu_custom_call" | custom-call | flops 1000000 | bytes 10000 | tf_op jit(solution)/shard_map/front/pallas_call | solution.py:323
  50.5 5.0 %attend_first.1 = (f32[2048,128]{1,0:T(8,128)}, f32[2048,128]{1,0:T(8,128)}, f32[2048,128]{1,0:T(8,128)}) custom-call(s32[32]{0:T(128)} %get-tuple-element.20.seen_ref, bf16[2048,128]{1,0:T(8,128)(2,1)} %get-tuple-element.21.q_hbm, bf16[512,128]{1,0:T(8,128)(2,1)} %get-tuple-element.22.refs_0_, bf16[512,128]{1,0:T(8,128)(2,1)} %get-tuple-element.23.refs_1_, ...), custom_call_target="tpu_custom_call" | custom-call | flops 1000000 | bytes 10000 | tf_op jit(solution)/shard_map/attend_first/pallas_call | solution.py:460
  55.5 0.7 rsqrt_bitcast_fusion
  56.4 1.9 %copy-done.1 = bf16[768,2048]{1,0:T(8,128)(2,1)S(1)} copy-done((bf16[768,2048]{1,0:T(8,128)(2,1)S(1)}, bf16[768,2048]{1,0:T(8,128)(2,1)}, u32[]{:S(2)}) %copy-start.1) | copy-done | bytes 3145752
  58.3 1.1 %copy-done.5 = bf16[512,768]{1,0:T(8,128)(2,1)S(1)} copy-done((bf16[512,768]{1,0:T(8,128)(2,1)S(1)}, bf16[512,768]{1,0:T(8,128)(2,1)}, u32[]{:S(2)}) %copy-start.5) | copy-done | bytes 786456
  59.4 2.3 %mixer_out.1 = (f32[512,1024]{1,0:T(8,128)S(1)}, f32[512,1024]{1,0:T(8,128)S(1)}, bf16[512,1024]{1,0:T(8,128)(2,1)S(1)}) custom-call(s32[1]{0:T(128)} %bitcast.core_ref, bf16[512,768]{1,0:T(8,128)(2,1)S(1)} %copy-done.5, f32[512,1]{1,0:T(8,128)S(1)} %copy.25.scale_ref, bf16[768,2048]{1,0:T(8,128)(2,1)S(1)} %copy-done.1, bf16[512,2048]{1,0:T(8,128)(2,1)S(1)} %copy-done), custom_call_target="tpu_custom_call" | custom-call | flops 1000000 | bytes 10000 | tf_op jit(solution)/shard_map/mixer_out/pallas_call | solution.py:595
  61.7 1.3 %copy-done.2 = f32[512,1024]{1,0:T(8,128)} copy-done((f32[512,1024]{1,0:T(8,128)}, f32[512,1024]{1,0:T(8,128)S(1)}, u32[]{:S(2)}) %copy-start.2) | copy-done | bytes 2097176
  63.0 1.4 %copy-done.3 = f32[512,1024]{1,0:T(8,128)} copy-done((f32[512,1024]{1,0:T(8,128)}, f32[512,1024]{1,0:T(8,128)S(1)}, u32[]{:S(2)}) %copy-start.3) | copy-done | bytes 2097176
  64.4 7.9 %all-to-all-done.1 = bf16[16,2,2,128,128]{4,3,2,1,0:T(8,128)(2,1)} async-done(((bf16[16,2,2,128,128]{4,3,2,1,0:T(8,128)(2,1)}), bf16[16,2,2,128,128]{4,3,2,1,0:T(8,128)(2,1)}, u32[]{:S(2)}, u32[]{:S(2)}) %all-to-all-start.1) | async-done | bytes 2097184 | tf_op jit(solution)/shard_map/all_to_all | solution.py:668
  72.2 14.2 %attend_late.1 = (bf16[512,512]{1,0:T(8,128)(2,1)}, bf16[512,1024]{1,0:T(8,128)(2,1)}) custom-call(s32[32]{0:T(128)} %get-tuple-element.20.seen_ref, bf16[2048,128]{1,0:T(8,128)(2,1)} %get-tuple-element.21.q_hbm, f32[2048,128]{1,0:T(8,128)} %get-tuple-element.26.sum_hbm, f32[2048,128]{1,0:T(8,128)} %get-tuple-element.27.total_hbm, ...), custom_call_target="tpu_custom_call" | custom-call | flops 1000000 | bytes 10000 | tf_op jit(solution)/shard_map/attend_late/pallas_call | solution.py:551
  86.5 1.5 %collective-permute-start.2 = (bf16[512,1024]{1,0:T(8,128)(2,1)}, bf16[512,1024]{1,0:T(8,128)(2,1)S(1)}, u32[]{:S(2)}, u32[]{:S(2)}) collective-permute-start(bf16[512,1024]{1,0:T(8,128)(2,1)} %get-tuple-element.36), channel_id=1, source_target_pairs={{0,1},{1,0},{2,3},{3,2},{4,5},{5,4},{6,7},{7,6},{8,9},{9,8},{10,11... | collective-permute-start | bytes 3145736 | tf_op jit(solution)/shard_map/ppermute | solution.py:695
  88.0 1.0 %copy-done.6 = bf16[512,512]{1,0:T(8,128)(2,1)S(1)} copy-done((bf16[512,512]{1,0:T(8,128)(2,1)S(1)}, bf16[512,512]{1,0:T(8,128)(2,1)}, u32[]{:S(2)}) %copy-start.6) | copy-done | bytes 524312
  89.1 0.7 ours_half.1
  89.8 0.7 collective-permute-done.2
  90.5 1.4 %add_convert_fusion = bf16[512,1024]{1,0:T(8,128)(2,1)} fusion(bf16[512,1024]{1,0:T(8,128)(2,1)S(1)} %collective-permute-done.2, bf16[512,1024]{1,0:T(8,128)(2,1)S(1)} %ours_half.1), kind=kLoop, calls=%fused_computation | loop fusion | flops 2097152 | bytes 3145728 | tf_op jit(solution)/shard_map/convert_element_type | solution.py:697
  (20 shorter events, 0.3 us)
Async XLA Ops:
  17.7 6.2 %copy-start.7 = (bf16[512,1024]{1,0:T(8,128)(2,1)S(1)}, bf16[512,1024]{1,0:T(8,128)(2,1)}, u32[]{:S(2)}) copy-start(bf16[512,1024]{1,0:T(8,128)(2,1)} %mine_ref.1) | copy-start | bytes 3145732
  17.7 8.8 %copy-start.9 = (f32[768]{0:T(1024)S(1)}, f32[768]{0:T(1024)}, u32[]{:S(2)}) copy-start(f32[768]{0:T(1024)} %param.43) | copy-start | bytes 9220
  17.7 54.5 %all-to-all-start.1 = ((bf16[16,2,2,128,128]{4,3,2,1,0:T(8,128)(2,1)}), bf16[16,2,2,128,128]{4,3,2,1,0:T(8,128)(2,1)}, u32[]{:S(2)}, u32[]{:S(2)}) async-start(bf16[16,2,2,128,128]{4,3,2,1,0:T(8,128)(2,1)} %bitcast.15), calls=%async_computation.1 | async-start | bytes 4194304 | tf_op jit(solution)/shard_map/all_to_all | solution.py:668
  23.9 5.2 %collective-permute-start = (bf16[512,1024]{1,0:T(8,128)(2,1)S(1)}, bf16[512,1024]{1,0:T(8,128)(2,1)S(1)}, u32[]{:S(2)}, u32[]{:S(2)}) collective-permute-start(bf16[512,1024]{1,0:T(8,128)(2,1)S(1)} %copy-done.7), channel_id=1, source_target_pairs={{0,1},{1,0},{2,3},{3,2},{4,5},{5,4},{6,7},{7,6},{8,9},{9,8},{10,11... | collective-permute-start | bytes 3145736 | tf_op jit(solution)/shard_map/ppermute | solution.py:665
  29.1 1.0 %copy-start.8 = (bf16[512,1024]{1,0:T(8,128)(2,1)}, bf16[512,1024]{1,0:T(8,128)(2,1)S(1)}, u32[]{:S(2)}) copy-start(bf16[512,1024]{1,0:T(8,128)(2,1)S(1)} %collective-permute-done.other_ref) | copy-start | bytes 3145732
  30.1 26.3 %copy-start = (bf16[512,2048]{1,0:T(8,128)(2,1)S(1)}, bf16[512,2048]{1,0:T(8,128)(2,1)}, u32[]{:S(2)}) copy-start(bf16[512,2048]{1,0:T(8,128)(2,1)} %weight_hbm.1) | copy-start | bytes 6291460
  50.3 5.2 %collective-permute-start.1 = (f32[1,512]{1,0:T(1,128)}, f32[1,512]{1,0:T(1,128)S(1)}, u32[]{:S(2)}, u32[]{:S(2)}) collective-permute-start(f32[1,512]{1,0:T(1,128)} %get-tuple-element.30), channel_id=1, source_target_pairs={{0,1},{1,0},{2,3},{3,2},{4,5},{5,4},{6,7},{7,6},{8,9},{9,8},{10,11... | collective-permute-start | bytes 6152 | tf_op jit(solution)/shard_map/ppermute | solution.py:686
  56.4 1.9 %copy-start.1 = (bf16[768,2048]{1,0:T(8,128)(2,1)S(1)}, bf16[768,2048]{1,0:T(8,128)(2,1)}, u32[]{:S(2)}) copy-start(bf16[768,2048]{1,0:T(8,128)(2,1)} %weight_ref.1) | copy-start | bytes 9437188
  58.3 1.1 %copy-start.5 = (bf16[512,768]{1,0:T(8,128)(2,1)S(1)}, bf16[512,768]{1,0:T(8,128)(2,1)}, u32[]{:S(2)}) copy-start(bf16[512,768]{1,0:T(8,128)(2,1)} %get-tuple-element.29.gated_ref) | copy-start | bytes 2359300
  61.7 1.3 %copy-start.2 = (f32[512,1024]{1,0:T(8,128)}, f32[512,1024]{1,0:T(8,128)S(1)}, u32[]{:S(2)}) copy-start(f32[512,1024]{1,0:T(8,128)S(1)} %get-tuple-element.31.part_hbm) | copy-start | bytes 6291460
  63.0 1.4 %copy-start.3 = (f32[512,1024]{1,0:T(8,128)}, f32[512,1024]{1,0:T(8,128)S(1)}, u32[]{:S(2)}) copy-start(f32[512,1024]{1,0:T(8,128)S(1)} %get-tuple-element.35.part_ref) | copy-start | bytes 6291460
  72.2 15.8 %copy-start.4 = (f32[512,1024]{1,0:T(8,128)S(1)}, f32[512,1024]{1,0:T(8,128)}, u32[]{:S(2)}) copy-start(f32[512,1024]{1,0:T(8,128)} %copy-done.3) | copy-start | bytes 6291460
  86.5 4.0 %collective-permute-start.2 = (bf16[512,1024]{1,0:T(8,128)(2,1)}, bf16[512,1024]{1,0:T(8,128)(2,1)S(1)}, u32[]{:S(2)}, u32[]{:S(2)}) collective-permute-start(bf16[512,1024]{1,0:T(8,128)(2,1)} %get-tuple-element.36), channel_id=1, source_target_pairs={{0,1},{1,0},{2,3},{3,2},{4,5},{5,4},{6,7},{7,6},{8,9},{9,8},{10,11... | collective-permute-start | bytes 3145736 | tf_op jit(solution)/shard_map/ppermute | solution.py:695
  88.0 1.0 %copy-start.6 = (bf16[512,512]{1,0:T(8,128)(2,1)S(1)}, bf16[512,512]{1,0:T(8,128)(2,1)}, u32[]{:S(2)}) copy-start(bf16[512,512]{1,0:T(8,128)(2,1)} %get-tuple-element.33.context_ref) | copy-start | bytes 1572868

commit v6 on v5

--- a/solution.py
+++ b/solution.py
@@ -85,29 +85,38 @@
     me = lax.axis_index("req")
     load = pltpu.make_async_copy(asked_hbm, asked, sem.at[0])
     load.start()
+    parts = sems_in.shape[0]
+    size = held.shape[0] // parts
+    reads = [
+        pltpu.make_async_copy(
+            pages_ref.at[pl.ds(part * size, size)],
+            held.at[pl.ds(part * size, size)],
+            sems_in.at[part],
+        )
+        for part in range(parts)
+    ]
+    for read in reads:
+        read.start()
     load.wait()
-    count = held.shape[0]
-    reads = []
-    for index in range(count):
+    for read in reads:
+        read.wait()
+    writes = []
+    for index in range(out_ref.shape[0]):
         slot = asked[index // capacity, 0, index % capacity]
-        reads.append(
-            pltpu.make_async_copy(pages_ref.at[slot], held.at[index], sems_in.at[index])
-        )
-        reads[-1].start()
-    writes = []
-    for request in range(count // capacity):
-        block = pl.ds(request * capacity, capacity)
-        for read in reads[request * capacity : (request + 1) * capacity]:
-            read.wait()
         writes.append(
-            pltpu.make_async_copy(held.at[block], out_ref.at[block], sems_out.at[request])
-        )
-        writes[-1].start()
-    mine = pltpu.make_async_copy(held.at[pl.ds(me * capacity, capacity)], own_ref, sem.at[1])
-    mine.start()
+            pltpu.make_async_copy(held.at[slot], out_ref.at[index], sems_out.at[index])
+        )
+    for rank in range(capacity):
+        slot = asked[me, 0, rank]
+        writes.append(
+            pltpu.make_async_copy(
+                held.at[slot], own_ref.at[rank], sems_out.at[out_ref.shape[0] + rank]
+            )
+        )
+    for write in writes:
+        write.start()
     for write in writes:
         write.wait()
-    mine.wait()
 
 
 def gather_pages(asked, kv_pages, capacity):
@@ -123,10 +132,10 @@
         out_specs=(HBM, HBM),
         scratch_shapes=[
             pltpu.SMEM(asked.shape, jnp.int32),
-            pltpu.VMEM((count,) + page, kv_pages.dtype),
-            pltpu.SemaphoreType.DMA((2,)),
-            pltpu.SemaphoreType.DMA((count,)),
-            pltpu.SemaphoreType.DMA((asked.shape[0],)),
+            pltpu.VMEM(kv_pages.shape, kv_pages.dtype),
+            pltpu.SemaphoreType.DMA((1,)),
+            pltpu.SemaphoreType.DMA((4,)),
+            pltpu.SemaphoreType.DMA((count + capacity,)),
         ],
         compiler_params=params(60),
         cost_estimate=LIGHT,

time: 92.3 us -> 91.6 us (level)
  no operation moved by 1% of the time
where the time goes in v6:
time: 91.6 us; the launch traced here: 91.1 us
  Pallas kernels  47.2 us (52%)
  blocking collectives  10.8 us (12%)
  starting transfers between devices  10.5 us (11%)
  waiting for transfers between devices  8.61 us (9%)
  local copies, waits for them, and re-layouts  8.47 us (9%)
  other arithmetic  4.09 us (4%)
  between operations  1.41 us (2%)
    pallas_call x1, Pallas kernels, front(): pl.pallas_call(front_kernel, out_shape=(out((wq.shape[1] // HEAD_SIZE * r...  20.2 us
    pallas_call x1, Pallas kernels, attend_late(): pl.pallas_call(functools.partial(attend_late_kernel, masks), out_shape=(j...  14.2 us
    all_to_all x1, blocking collectives, exchange(): lax.all_to_all(blocks, 'req', split_axis=0, concat_axis=0, tiled=True)  10.8 us
    all_to_all x1, waiting for transfers between devices, exchange(): lax.all_to_all(blocks, 'req', split_axis=0, concat_axis=0, tiled=True)  7.87 us
    unnamed x20, local copies, waits for them, and re-layouts  7.75 us
    all_to_all x1, starting transfers between devices, exchange(): lax.all_to_all(blocks, 'req', split_axis=0, concat_axis=0, tiled=True)  6.25 us
    pallas_call x1, Pallas kernels, attend_early(): pl.pallas_call(functools.partial(attend_early_kernel, masks, picks, fresh...  5.04 us
    pallas_call x1, Pallas kernels, gather_pages(): pl.pallas_call(functools.partial(gather_kernel, capacity), out_shape=(jax...  3.23 us
  transfers between devices with their start and end apart: 4, of which 2 were waited for; matrix products, arithmetic and copies ran while one was open for 4% of the time, Pallas kernels for 31%

profile of v6, /device:TPU:13, one launch (start us, length us, event | category | flops | bytes accessed | tf_op | source)
XLA Modules:
  0.0 91.1 jit_solution(7552360224841537231)
XLA Ops:
  1.3 1.5 %wanted.1 = (s32[16,1,128]{2,1,0:T(1,128)}, s32[32]{0:T(128)}) custom-call(s32[1,32]{1,0:T(1,128)} %table_ref.1, s32[1]{0:T(128)} %copy.26.length_ref), custom_call_target="tpu_custom_call" | custom-call | tf_op jit(solution)/shard_map/wanted/pallas_call | solution.py:68
  2.8 10.8 %all_to_all.10.asked_hbm = s32[16,1,128]{2,1,0:T(1,128)} all-to-all(s32[16,1,128]{2,1,0:T(1,128)} %get-tuple-element.24), channel_id=1, replica_groups=mesh['req'=16,'tp'=2] {'req'}, dimensions={0} | all-to-all | bytes 16384 | tf_op jit(solution)/shard_map/all_to_all | solution.py:677
  13.6 3.2 %gather_pages.1 = (bf16[32,2,128,128]{3,2,1,0:T(8,128)(2,1)}, bf16[2,2,128,128]{3,2,1,0:T(8,128)(2,1)}) custom-call(s32[16,1,128]{2,1,0:T(1,128)} %all_to_all.10.asked_hbm, bf16[32,2,128,128]{3,2,1,0:T(8,128)(2,1)} %bitcast.14), custom_call_target="tpu_custom_call" | custom-call | flops 1000000 | bytes 10000 | tf_op jit(solution)/shard_map/gather_pages/pallas_call | solution.py:125
  16.9 6.2 %all-to-all-start.1 = ((bf16[16,2,2,128,128]{4,3,2,1,0:T(8,128)(2,1)}), bf16[16,2,2,128,128]{4,3,2,1,0:T(8,128)(2,1)}, u32[]{:S(2)}, u32[]{:S(2)}) async-start(bf16[16,2,2,128,128]{4,3,2,1,0:T(8,128)(2,1)} %bitcast.15), calls=%async_computation.1 | async-start | bytes 4194304 | tf_op jit(solution)/shard_map/all_to_all | solution.py:677
  23.1 2.6 %collective-permute-start = (bf16[512,1024]{1,0:T(8,128)(2,1)S(1)}, bf16[512,1024]{1,0:T(8,128)(2,1)S(1)}, u32[]{:S(2)}, u32[]{:S(2)}) collective-permute-start(bf16[512,1024]{1,0:T(8,128)(2,1)S(1)} %copy-done.7), channel_id=1, source_target_pairs={{0,1},{1,0},{2,3},{3,2},{4,5},{5,4},{6,7},{7,6},{8,9},{9,8},{10,11... | collective-permute-start | bytes 3145736 | tf_op jit(solution)/shard_map/ppermute | solution.py:674
  25.8 0.6 broadcast_in_dim.17.mixer_gain_ref
  26.3 1.0 %fusion = (f32[512,64]{1,0:T(8,128)S(1)}, f32[512,64]{1,0:T(8,128)S(1)}, f32[512,64]{1,0:T(8,128)S(1)}) fusion(f32[64]{0:T(128)S(1)} %multiply_power_fusion, f32[512]{0:T(512)S(1)} %add_convert_fusion.1), kind=kLoop, calls=%fused_computation.5 | loop fusion | flops 65536 | bytes 395520 | tf_op jit(solution)/shard_map/neg | solution.py:40
  27.4 1.0 %pad_maximum_fusion = (f32[512,128]{1,0:T(8,128)}, f32[512,128]{1,0:T(8,128)}) fusion(f32[512,64]{1,0:T(8,128)S(1)} %get-tuple-element.40, f32[512,64]{1,0:T(8,128)S(1)} %get-tuple-element.39, f32[512,64]{1,0:T(8,128)S(1)} %get-tuple-element.38), kind=kLoop, calls=%fused_computation.3 | loop fusion | flops 131072 | bytes 917504 | tf_op jit(solution)/shard_map/concatenate | solution.py:39
  28.4 1.0 %copy-done.8 = bf16[512,1024]{1,0:T(8,128)(2,1)} copy-done((bf16[512,1024]{1,0:T(8,128)(2,1)}, bf16[512,1024]{1,0:T(8,128)(2,1)S(1)}, u32[]{:S(2)}) %copy-start.8) | copy-done | bytes 1048600
  29.3 20.2 %front.1 = (bf16[2048,128]{1,0:T(8,128)(2,1)}, bf16[512,128]{1,0:T(8,128)(2,1)}, bf16[512,128]{1,0:T(8,128)(2,1)}, bf16[512,768]{1,0:T(8,128)(2,1)}, f32[1,512]{1,0:T(1,128)}, /*index=5*/f32[768,256]{1,0:T(8,128)}) custom-call(s32[1]{0:T(128)} %bitcast.core_ref, bf16[512,1024]{1,0:T(8,128)(2,1)} %mine_ref.1, bf16[512,1024]{1,0:T(8,128)(2,1)} %copy-done.8, ...), custom_call_target="tpu_custom_call" | custom-call | flops 1000000 | bytes 10000 | tf_op jit(solution)/shard_map/front/pallas_call | solution.py:332
  49.7 5.0 %attend_first.1 = (f32[2048,128]{1,0:T(8,128)}, f32[2048,128]{1,0:T(8,128)}, f32[2048,128]{1,0:T(8,128)}) custom-call(s32[32]{0:T(128)} %get-tuple-element.20.seen_ref, bf16[2048,128]{1,0:T(8,128)(2,1)} %get-tuple-element.21.q_hbm, bf16[512,128]{1,0:T(8,128)(2,1)} %get-tuple-element.22.refs_0_, bf16[512,128]{1,0:T(8,128)(2,1)} %get-tuple-element.23.refs_1_, ...), custom_call_target="tpu_custom_call" | custom-call | flops 1000000 | bytes 10000 | tf_op jit(solution)/shard_map/attend_first/pallas_call | solution.py:469
  54.8 0.7 rsqrt_bitcast_fusion
  55.6 1.9 %copy-done.1 = bf16[768,2048]{1,0:T(8,128)(2,1)S(1)} copy-done((bf16[768,2048]{1,0:T(8,128)(2,1)S(1)}, bf16[768,2048]{1,0:T(8,128)(2,1)}, u32[]{:S(2)}) %copy-start.1) | copy-done | bytes 3145752
  57.5 1.1 %copy-done.5 = bf16[512,768]{1,0:T(8,128)(2,1)S(1)} copy-done((bf16[512,768]{1,0:T(8,128)(2,1)S(1)}, bf16[512,768]{1,0:T(8,128)(2,1)}, u32[]{:S(2)}) %copy-start.5) | copy-done | bytes 786456
  58.6 2.3 %mixer_out.1 = (f32[512,1024]{1,0:T(8,128)S(1)}, f32[512,1024]{1,0:T(8,128)S(1)}, bf16[512,1024]{1,0:T(8,128)(2,1)S(1)}) custom-call(s32[1]{0:T(128)} %bitcast.core_ref, bf16[512,768]{1,0:T(8,128)(2,1)S(1)} %copy-done.5, f32[512,1]{1,0:T(8,128)S(1)} %copy.25.scale_ref, bf16[768,2048]{1,0:T(8,128)(2,1)S(1)} %copy-done.1, bf16[512,2048]{1,0:T(8,128)(2,1)S(1)} %copy-done), custom_call_target="tpu_custom_call" | custom-call | flops 1000000 | bytes 10000 | tf_op jit(solution)/shard_map/mixer_out/pallas_call | solution.py:604
  60.9 1.3 %copy-done.2 = f32[512,1024]{1,0:T(8,128)} copy-done((f32[512,1024]{1,0:T(8,128)}, f32[512,1024]{1,0:T(8,128)S(1)}, u32[]{:S(2)}) %copy-start.2) | copy-done | bytes 2097176
  62.2 1.4 %copy-done.3 = f32[512,1024]{1,0:T(8,128)} copy-done((f32[512,1024]{1,0:T(8,128)}, f32[512,1024]{1,0:T(8,128)S(1)}, u32[]{:S(2)}) %copy-start.3) | copy-done | bytes 2097176
  63.6 7.9 %all-to-all-done.1 = bf16[16,2,2,128,128]{4,3,2,1,0:T(8,128)(2,1)} async-done(((bf16[16,2,2,128,128]{4,3,2,1,0:T(8,128)(2,1)}), bf16[16,2,2,128,128]{4,3,2,1,0:T(8,128)(2,1)}, u32[]{:S(2)}, u32[]{:S(2)}) %all-to-all-start.1) | async-done | bytes 2097184 | tf_op jit(solution)/shard_map/all_to_all | solution.py:677
  71.5 14.2 %attend_late.1 = (bf16[512,512]{1,0:T(8,128)(2,1)}, bf16[512,1024]{1,0:T(8,128)(2,1)}) custom-call(s32[32]{0:T(128)} %get-tuple-element.20.seen_ref, bf16[2048,128]{1,0:T(8,128)(2,1)} %get-tuple-element.21.q_hbm, f32[2048,128]{1,0:T(8,128)} %get-tuple-element.26.sum_hbm, f32[2048,128]{1,0:T(8,128)} %get-tuple-element.27.total_hbm, ...), custom_call_target="tpu_custom_call" | custom-call | flops 1000000 | bytes 10000 | tf_op jit(solution)/shard_map/attend_late/pallas_call | solution.py:560
  85.7 1.6 %collective-permute-start.2 = (bf16[512,1024]{1,0:T(8,128)(2,1)}, bf16[512,1024]{1,0:T(8,128)(2,1)S(1)}, u32[]{:S(2)}, u32[]{:S(2)}) collective-permute-start(bf16[512,1024]{1,0:T(8,128)(2,1)} %get-tuple-element.36), channel_id=1, source_target_pairs={{0,1},{1,0},{2,3},{3,2},{4,5},{5,4},{6,7},{7,6},{8,9},{9,8},{10,11... | collective-permute-start | bytes 3145736 | tf_op jit(solution)/shard_map/ppermute | solution.py:704
  87.3 1.0 %copy-done.6 = bf16[512,512]{1,0:T(8,128)(2,1)S(1)} copy-done((bf16[512,512]{1,0:T(8,128)(2,1)S(1)}, bf16[512,512]{1,0:T(8,128)(2,1)}, u32[]{:S(2)}) %copy-start.6) | copy-done | bytes 524312
  88.3 0.7 ours_half.1
  89.0 0.7 collective-permute-done.2
  89.8 1.4 %add_convert_fusion = bf16[512,1024]{1,0:T(8,128)(2,1)} fusion(bf16[512,1024]{1,0:T(8,128)(2,1)S(1)} %collective-permute-done.2, bf16[512,1024]{1,0:T(8,128)(2,1)S(1)} %ours_half.1), kind=kLoop, calls=%fused_computation | loop fusion | flops 2097152 | bytes 3145728 | tf_op jit(solution)/shard_map/convert_element_type | solution.py:706
  (20 shorter events, 0.3 us)
Async XLA Ops:
  16.9 6.3 %copy-start.7 = (bf16[512,1024]{1,0:T(8,128)(2,1)S(1)}, bf16[512,1024]{1,0:T(8,128)(2,1)}, u32[]{:S(2)}) copy-start(bf16[512,1024]{1,0:T(8,128)(2,1)} %mine_ref.1) | copy-start | bytes 3145732
  16.9 8.9 %copy-start.9 = (f32[768]{0:T(1024)S(1)}, f32[768]{0:T(1024)}, u32[]{:S(2)}) copy-start(f32[768]{0:T(1024)} %param.43) | copy-start | bytes 9220
  16.9 54.6 %all-to-all-start.1 = ((bf16[16,2,2,128,128]{4,3,2,1,0:T(8,128)(2,1)}), bf16[16,2,2,128,128]{4,3,2,1,0:T(8,128)(2,1)}, u32[]{:S(2)}, u32[]{:S(2)}) async-start(bf16[16,2,2,128,128]{4,3,2,1,0:T(8,128)(2,1)} %bitcast.15), calls=%async_computation.1 | async-start | bytes 4194304 | tf_op jit(solution)/shard_map/all_to_all | solution.py:677
  23.1 5.2 %collective-permute-start = (bf16[512,1024]{1,0:T(8,128)(2,1)S(1)}, bf16[512,1024]{1,0:T(8,128)(2,1)S(1)}, u32[]{:S(2)}, u32[]{:S(2)}) collective-permute-start(bf16[512,1024]{1,0:T(8,128)(2,1)S(1)} %copy-done.7), channel_id=1, source_target_pairs={{0,1},{1,0},{2,3},{3,2},{4,5},{5,4},{6,7},{7,6},{8,9},{9,8},{10,11... | collective-permute-start | bytes 3145736 | tf_op jit(solution)/shard_map/ppermute | solution.py:674
  28.4 1.0 %copy-start.8 = (bf16[512,1024]{1,0:T(8,128)(2,1)}, bf16[512,1024]{1,0:T(8,128)(2,1)S(1)}, u32[]{:S(2)}) copy-start(bf16[512,1024]{1,0:T(8,128)(2,1)S(1)} %collective-permute-done.other_ref) | copy-start | bytes 3145732
  29.3 26.3 %copy-start = (bf16[512,2048]{1,0:T(8,128)(2,1)S(1)}, bf16[512,2048]{1,0:T(8,128)(2,1)}, u32[]{:S(2)}) copy-start(bf16[512,2048]{1,0:T(8,128)(2,1)} %weight_hbm.1) | copy-start | bytes 6291460
  49.6 5.2 %collective-permute-start.1 = (f32[1,512]{1,0:T(1,128)}, f32[1,512]{1,0:T(1,128)S(1)}, u32[]{:S(2)}, u32[]{:S(2)}) collective-permute-start(f32[1,512]{1,0:T(1,128)} %get-tuple-element.30), channel_id=1, source_target_pairs={{0,1},{1,0},{2,3},{3,2},{4,5},{5,4},{6,7},{7,6},{8,9},{9,8},{10,11... | collective-permute-start | bytes 6152 | tf_op jit(solution)/shard_map/ppermute | solution.py:695
  55.6 1.9 %copy-start.1 = (bf16[768,2048]{1,0:T(8,128)(2,1)S(1)}, bf16[768,2048]{1,0:T(8,128)(2,1)}, u32[]{:S(2)}) copy-start(bf16[768,2048]{1,0:T(8,128)(2,1)} %weight_ref.1) | copy-start | bytes 9437188
  57.5 1.1 %copy-start.5 = (bf16[512,768]{1,0:T(8,128)(2,1)S(1)}, bf16[512,768]{1,0:T(8,128)(2,1)}, u32[]{:S(2)}) copy-start(bf16[512,768]{1,0:T(8,128)(2,1)} %get-tuple-element.29.gated_ref) | copy-start | bytes 2359300
  60.9 1.3 %copy-start.2 = (f32[512,1024]{1,0:T(8,128)}, f32[512,1024]{1,0:T(8,128)S(1)}, u32[]{:S(2)}) copy-start(f32[512,1024]{1,0:T(8,128)S(1)} %get-tuple-element.31.part_hbm) | copy-start | bytes 6291460
  62.2 1.4 %copy-start.3 = (f32[512,1024]{1,0:T(8,128)}, f32[512,1024]{1,0:T(8,128)S(1)}, u32[]{:S(2)}) copy-start(f32[512,1024]{1,0:T(8,128)S(1)} %get-tuple-element.35.part_ref) | copy-start | bytes 6291460
  71.5 15.8 %copy-start.4 = (f32[512,1024]{1,0:T(8,128)S(1)}, f32[512,1024]{1,0:T(8,128)}, u32[]{:S(2)}) copy-start(f32[512,1024]{1,0:T(8,128)} %copy-done.3) | copy-start | bytes 6291460
  85.7 4.0 %collective-permute-start.2 = (bf16[512,1024]{1,0:T(8,128)(2,1)}, bf16[512,1024]{1,0:T(8,128)(2,1)S(1)}, u32[]{:S(2)}, u32[]{:S(2)}) collective-permute-start(bf16[512,1024]{1,0:T(8,128)(2,1)} %get-tuple-element.36), channel_id=1, source_target_pairs={{0,1},{1,0},{2,3},{3,2},{4,5},{5,4},{6,7},{7,6},{8,9},{9,8},{10,11... | collective-permute-start | bytes 3145736 | tf_op jit(solution)/shard_map/ppermute | solution.py:704
  87.3 1.0 %copy-start.6 = (bf16[512,512]{1,0:T(8,128)(2,1)S(1)}, bf16[512,512]{1,0:T(8,128)(2,1)}, u32[]{:S(2)}) copy-start(bf16[512,512]{1,0:T(8,128)(2,1)} %get-tuple-element.33.context_ref) | copy-start | bytes 1572868
